TPU v7x, 128 devices: a whole 4x4x4 slice. The times are simulated.
128 devices in a mesh: det: 2 (over z_hi), grp: 2 (over core), tm: 32 (over y, z_lo, x).
Axes of the slice: x: 4, y: 4, z: 4 (z_hi: 2, z_lo: 2; z = z_hi * 2 + z_lo), core: 2. Of those that a mesh axis runs over, the one named last changes fastest.
Arguments:
- strain: float32 [2, 2, 128, 4096], P('det', None, 'tm'), may hold values from -6 to 6
- bank: float32 [16, 2, 128, 4096], P('grp', None, 'tm'), may hold values from -64 to 64
- assignment: int32 [16], replicated, may hold values from 0 to 15, each once
- slides: int32 [4], replicated, may hold values from 0 to 524287
- bounds: int32 [7], replicated, may hold values from 49152 to 475136, as said below
- antenna: float32 [2, 2], replicated, may hold values from 0.2 to 1
Outputs:
- chi_squared: float32 [2, 16, 128, 4096], P('det', 'grp', 'tm')
- network: float32 [16, 4, 128, 4096], P('grp', 'det', 'tm')
Inputs may be any that keep to these rules, and one draw needn't show every extreme that they name: `assignment`: each template index appears once. `bounds`: strictly rising; bound j lies within 16384 of (j + 1) * 65536.
All inputs are finite; a program needn't handle non-finite values.
Results may differ from a plain program's by a relative error of at most 0.0003.
Values sent between devices are 32-bit elements; how exact they have to be, the bound alone decides.
A program may use at most 128 MiB of HBM per device.

v0:
```python
import math

import jax
import jax.numpy as jnp
from jax import lax
from jax.sharding import PartitionSpec as P

DENSE = 512


HIGHEST = lax.Precision.HIGHEST


def from_partner(value, axis, stride):
    mask = 2**stride
    pairs = [(source, source ^ mask) for source in range(lax.axis_size(axis))]
    return lax.ppermute(value, axis, pairs)


def slide_phase(index, shift, total):
    first = shift % total
    second = first * 128 % total
    third = second * 128 % total
    lowest = index % 128
    middle = index // 128 % 128
    upper = index // 16384
    summed = lowest * first % total + middle * second % total + upper * third % total
    return (summed % total).astype(jnp.float32) * (2.0 * math.pi / total)


def unit_table(rows, cols, total, col_start):
    row_index = lax.broadcasted_iota(jnp.int32, (rows, cols), 0)
    col_index = col_start + lax.broadcasted_iota(jnp.int32, (rows, cols), 1)
    angle = (row_index * col_index % total).astype(jnp.float32) * (2.0 * math.pi / total)
    return (jnp.cos(angle), jnp.sin(angle))


def complex_einsum(form, left, right):
    real = jnp.einsum(form, left[0], right[0], precision=HIGHEST) - jnp.einsum(
        form, left[1], right[1], precision=HIGHEST
    )
    imag = jnp.einsum(form, left[0], right[1], precision=HIGHEST) + jnp.einsum(
        form, left[1], right[0], precision=HIGHEST
    )
    return (real, imag)


def complex_times(left, right):
    return (left[0] * right[0] - left[1] * right[1], left[0] * right[1] + left[1] * right[0])


def conj_times(signal, wave):
    return (signal[0] * wave[0] + signal[1] * wave[1], signal[1] * wave[0] - signal[0] * wave[1])


def band_masks(index, bounds, bands):
    widened = bounds.reshape((-1,) + (1,) * index.ndim)
    band_index = jnp.sum((index[None] >= widened).astype(jnp.int32), axis=0)
    levels = jnp.arange(bands, dtype=jnp.int32).reshape((-1,) + (1,) * index.ndim)
    return (band_index[None] == levels).astype(jnp.float32)


def on_device(strain, bank, assignment, slides, bounds, antenna):
    parts = lax.axis_size("tm")
    tm_index = lax.axis_index("tm")
    det_index = lax.axis_index("det")
    per_group = bank.shape[0]
    rows_dev = bank.shape[2]
    cols = bank.shape[3]
    fold = rows_dev * parts
    bins = fold * cols
    width = cols // parts
    radix = min(cols, DENSE)
    split = cols // radix
    bands = bounds.shape[0] + 1
    half_slides = slides.shape[0] // lax.axis_size("det")
    per_item = bands + half_slides
    whole_bank = lax.all_gather(bank, "grp", axis=0, tiled=True)
    mine = lax.dynamic_slice_in_dim(assignment, lax.axis_index("grp") * per_group, per_group)
    chosen = jnp.take(whole_bank, mine, axis=0)
    local_rows = lax.broadcasted_iota(jnp.int32, (rows_dev, cols), 0)
    local_cols = lax.broadcasted_iota(jnp.int32, (rows_dev, cols), 1)
    local_index = local_cols + cols * (tm_index * rows_dev + local_rows)
    local_masks = band_masks(local_index, bounds, bands)
    power = chosen[:, 0] * chosen[:, 0] + chosen[:, 1] * chosen[:, 1]
    partial_power = jnp.sum(power[:, None] * local_masks[None], axis=(2, 3))
    band_power = lax.psum(partial_power, "tm")
    fold_table = unit_table(fold, fold, fold, 0)
    fold_twiddle = unit_table(fold, width, bins, tm_index * width)
    split_table = unit_table(split, split, split, 0)
    radix_twiddle = unit_table(split, radix, cols, 0)
    radix_table = unit_table(radix, radix, radix, 0)
    weight_one = (antenna[0, 0], antenna[0, 1])
    weight_two = (antenna[1, 0], antenna[1, 1])
    response = jnp.sum(antenna * antenna)
    chosen_slides = lax.dynamic_slice_in_dim(slides, det_index * half_slides, half_slides)

    def make_items(own, other, masks, ramp):
        lead = (
            jnp.where(det_index == 0, own[0], other[0]),
            jnp.where(det_index == 0, own[1], other[1]),
        )
        trail = (
            jnp.where(det_index == 0, other[0], own[0]),
            jnp.where(det_index == 0, other[1], own[1]),
        )
        banded_re = own[0][None] * masks
        banded_im = own[1][None] * masks
        joined = complex_times(weight_one, lead)
        shifted = complex_times(complex_times(weight_two, trail), ramp)
        combined_re = joined[0][None] + shifted[0]
        combined_im = joined[1][None] + shifted[1]
        return (
            jnp.concatenate([banded_re, combined_re], axis=0),
            jnp.concatenate([banded_im, combined_im], axis=0),
        )

    def finish(series, powers):
        total = jnp.sum(powers)
        share = powers / total
        scale = 1.0 / jnp.sqrt(total)
        band_re = series[0][:bands] * scale
        band_im = series[1][:bands] * scale
        whole_re = jnp.sum(band_re, axis=0)
        whole_im = jnp.sum(band_im, axis=0)
        weight = share[:, None, None]
        gap_re = band_re - weight * whole_re[None]
        gap_im = band_im - weight * whole_im[None]
        chi = jnp.sum((gap_re * gap_re + gap_im * gap_im) / weight, axis=0) / (2 * bands - 2)
        net_re = series[0][bands:]
        net_im = series[1][bands:]
        net = (net_re * net_re + net_im * net_im) * (scale * scale) / response
        return (chi, net)

    all_items = jax.vmap(make_items, in_axes=(0, 0, None, None))
    angle = slide_phase(
        local_index[None], chosen_slides.reshape((-1,) + (1,) * local_index.ndim), bins
    )
    local_ramp = (jnp.cos(angle), jnp.sin(angle))
    own = conj_times((strain[0, 0][None], strain[0, 1][None]), (chosen[:, 0], chosen[:, 1]))
    other = from_partner(jnp.stack(own), "det", 0)
    items = all_items(own, (other[0], other[1]), local_masks, local_ramp)
    items = tuple((part.reshape((per_group * per_item,) + part.shape[2:]) for part in items))
    mixed = complex_einsum(
        "db,ibc->idc",
        fold_table,
        (
            lax.all_to_all(items[0], "tm", split_axis=2, concat_axis=1, tiled=True),
            lax.all_to_all(items[1], "tm", split_axis=2, concat_axis=1, tiled=True),
        ),
    )
    folded = complex_times(mixed, fold_twiddle)
    pieces = (
        lax.all_to_all(folded[0], "tm", split_axis=1, concat_axis=2, tiled=True),
        lax.all_to_all(folded[1], "tm", split_axis=1, concat_axis=2, tiled=True),
    )
    count = pieces[0].shape[0]
    depth = pieces[0].shape[1]
    shaped = (
        pieces[0].reshape(count, depth, split, radix),
        pieces[1].reshape(count, depth, split, radix),
    )
    first = complex_einsum("vs,idsr->idvr", split_table, shaped)
    turned = complex_times(first, radix_twiddle)
    second = complex_einsum("idvr,ru->idvu", turned, radix_table)
    series = (second[0].reshape(count, depth, cols), second[1].reshape(count, depth, cols))
    series = tuple((part.reshape((per_group, per_item) + part.shape[1:]) for part in series))
    chi_all, net_all = jax.vmap(finish)(series, band_power)
    return (chi_all[None], net_all)


def solution(mesh):
    return jax.shard_map(
        on_device,
        mesh=mesh,
        in_specs=(P("det", None, "tm", None), P("grp", None, "tm", None), P(), P(), P(), P()),
        out_specs=(P("det", "grp", "tm", None), P("grp", "det", "tm", None)),
        check_vma=False,
    )
```

profile of v0, /device:TPU:0, one launch (start us, length us, event | category | flops | bytes accessed | tf_op | source)
XLA Modules:
  0.0 751.9 jit_solution(7583599895560997845)
XLA Ops:
  12.6 12.8 %all-gather.2.cloned.1.call-done = f32[16,2,4,4096]{3,2,1,0:T(4,128)} async-done(((f32[8,2,4,4096]{3,2,1,0:T(4,128)}), f32[16,2,4,4096]{3,2,1,0:T(4,128)}) %all-gather.2.cloned.1.call-update) | async-done | bytes 2097168 | tf_op jit(solution)/shard_map/all_gather | solution.py:78
  34.3 21.8 %collective-permute-done = f32[2,8,4,4096]{3,2,1,0:T(4,128)S(1)} collective-permute-done((f32[2,8,4,4096]{3,2,1,0:T(4,128)S(1)}, f32[2,8,4,4096]{3,2,1,0:T(4,128)S(1)}, u32[]{:S(2)}, u32[]{:S(2)}) %collective-permute-start) | collective-permute-done | bytes 1048608 | tf_op jit(solution)/shard_map/ppermute | solution.py:17
  70.6 10.2 %copy.93 = f32[80,4,4096]{0,1,2:T(4,128)} copy(f32[80,4,4096]{2,1,0:T(4,128)} %bitcast.186) | data formatting | bytes 10485760 | tf_op jit(solution)/shard_map/reshape | solution.py:143
  80.8 8.3 %all-to-all-start.1 = ((f32[80,4,4096]{0,1,2:T(4,128)}), f32[80,4,4096]{0,1,2:T(4,128)}, u32[]{:S(2)}, u32[]{:S(2)}) async-start(f32[80,4,4096]{0,1,2:T(4,128)} %copy.93), calls=%async_computation.1 | async-start | bytes 16777216 | tf_op jit(solution)/shard_map/all_to_all | solution.py:149
  89.1 10.3 %copy.89 = f32[80,4,4096]{0,1,2:T(4,128)} copy(f32[80,4,4096]{2,1,0:T(4,128)} %bitcast.185) | data formatting | bytes 10485760 | tf_op jit(solution)/shard_map/reshape | solution.py:143
  99.4 99.7 %all-to-all-done.1 = f32[80,4,4096]{0,1,2:T(4,128)} async-done(((f32[80,4,4096]{0,1,2:T(4,128)}), f32[80,4,4096]{0,1,2:T(4,128)}, u32[]{:S(2)}, u32[]{:S(2)}) %all-to-all-start.1) | async-done | bytes 5242912 | tf_op jit(solution)/shard_map/all_to_all | solution.py:149
  199.1 16.3 %all-to-all-start = ((f32[80,4,4096]{0,1,2:T(4,128)}), f32[80,4,4096]{0,1,2:T(4,128)}, u32[]{:S(2)}, u32[]{:S(2)}) async-start(f32[80,4,4096]{0,1,2:T(4,128)} %copy.89), calls=%async_computation | async-start | bytes 16777216 | tf_op jit(solution)/shard_map/all_to_all | solution.py:148
  215.9 8.8 %copy.112 = f32[80,4,32,128]{3,0,1,2:T(8,128)} copy(f32[80,4,32,128]{0,1,3,2:T(4,128)} %bitcast.25) | data formatting | bytes 10485760 | tf_op jit(solution)/shard_map/all_to_all | solution.py:149
  231.0 88.7 %all-to-all-done = f32[80,4,4096]{0,1,2:T(4,128)} async-done(((f32[80,4,4096]{0,1,2:T(4,128)}), f32[80,4,4096]{0,1,2:T(4,128)}, u32[]{:S(2)}, u32[]{:S(2)}) %all-to-all-start) | async-done | bytes 5242912 | tf_op jit(solution)/shard_map/all_to_all | solution.py:148
  319.7 9.0 %copy.110 = f32[80,4,32,128]{3,0,1,2:T(8,128)} copy(f32[80,4,32,128]{0,1,3,2:T(4,128)} %bitcast.17) | data formatting | bytes 10485760 | tf_op jit(solution)/shard_map/all_to_all | solution.py:148
  353.0 10.2 %fusion.2 = (f32[80,128,128]{1,2,0:T(8,128)}, f32[80,128,128]{1,2,0:T(8,128)}) fusion(f32[80,128,128]{2,1,0:T(8,128)} %convolution_subtract_fusion.1, f32[128,128]{0,1:T(8,128)S(1)} %copy.100, f32[128,128]{0,1:T(8,128)S(1)} %copy.97, f32[80,128,128]{2,1,0:T(8,128)S(1)} %fusion.57, f32[80,128,128]{1,2,0:T(8,128)S(1)} %bitcast.182), kind=kOutput, calls=%fused_computation.11 | convolution fusion | flops 2022670336 | bytes 26345472 | tf_op jit(solution)/shard_map/db,ibc->idc/dot_general | solution.py:42
  369.6 13.4 %all-to-all-start.2 = ((f32[80,128,128]{2,0,1:T(8,128)}), f32[80,128,128]{2,0,1:T(8,128)}, u32[]{:S(2)}, u32[]{:S(2)}) async-start(f32[80,128,128]{2,0,1:T(8,128)} %copy.101), calls=%async_computation.2 | async-start | bytes 10485760 | tf_op jit(solution)/shard_map/all_to_all | solution.py:154
  389.3 55.5 %all-to-all-done.2 = f32[80,128,128]{2,0,1:T(8,128)} async-done(((f32[80,128,128]{2,0,1:T(8,128)}), f32[80,128,128]{2,0,1:T(8,128)}, u32[]{:S(2)}, u32[]{:S(2)}) %all-to-all-start.2) | async-done | bytes 5242912 | tf_op jit(solution)/shard_map/all_to_all | solution.py:154
  444.8 11.9 %all-to-all-start.3 = ((f32[80,128,128]{2,0,1:T(8,128)}), f32[80,128,128]{2,0,1:T(8,128)}, u32[]{:S(2)}, u32[]{:S(2)}) async-start(f32[80,128,128]{2,0,1:T(8,128)} %copy.103), calls=%async_computation.3 | async-start | bytes 10485760 | tf_op jit(solution)/shard_map/all_to_all | solution.py:155
  457.4 131.9 %psum.7 = f32[8,8]{1,0:T(8,128)S(1)} all-reduce(f32[8,8]{1,0:T(8,128)S(1)} %get-tuple-element.22), channel_id=1, replica_groups=mesh['det'=2,'grp'=2,'tm'=32] {'tm'}, use_global_device_ids=true, to_apply=%region_2.3 | all-reduce | flops 64 | bytes 512 | tf_op jit(solution)/shard_map/psum | solution.py:87
  589.5 7.8 %copy.102 = f32[80,4,32,128]{3,2,1,0:T(8,128)} copy(f32[80,4,32,128]{3,0,1,2:T(8,128)} %bitcast.35) | data formatting | bytes 10485760 | tf_op jit(solution)/shard_map/all_to_all | solution.py:154
  604.5 10.1 %fusion.93 = f32[80,4,512,8]{2,3,1,0:T(8,128)} fusion(f32[80,4,8,512]{3,2,1,0:T(8,128)} %reshape.398), kind=kOutput, calls=%fused_computation.175 | convolution fusion | flops 125830016 | bytes 10485760 | tf_op jit(solution)/shard_map/vs,idsr->idvr/dot_general | solution.py:39
  614.6 7.9 %copy.104 = f32[80,4,32,128]{3,2,1,0:T(8,128)} copy(f32[80,4,32,128]{3,0,1,2:T(8,128)} %bitcast.39) | data formatting | bytes 10485760 | tf_op jit(solution)/shard_map/all_to_all | solution.py:155
  636.7 7.9 %convolution_subtract_fusion = f32[80,4,512,8]{2,3,1,0:T(8,128)S(1)} fusion(f32[80,4,512,8]{2,3,1,0:T(8,128)} %fusion.93, f32[80,4,8,512]{3,2,1,0:T(8,128)S(1)} %copy-done.2), kind=kOutput, calls=%fused_computation.23 | convolution fusion | flops 127140736 | bytes 15728640 | tf_op jit(solution)/shard_map/vs,idsr->idvr/dot_general | solution.py:39
  651.2 13.8 %fusion.9 = f32[80,4,8,512]{3,2,1,0:T(8,128)S(1)} fusion(f32[80,4,512,8]{2,3,1,0:T(8,128)S(1)} %convolution_add_fusion, f32[80,4,512,8]{2,3,1,0:T(8,128)S(1)} %convolution_subtract_fusion, f32[8,512]{1,0:T(8,128)S(1)} %get-tuple-element.43, f32[8,512]{1,0:T(8,128)S(1)} %get-tuple-element.44), kind=kOutput, calls=%fused_computation.30 | convolution fusion | flops 8060665856 | bytes 15761408 | tf_op jit(solution)/shard_map/idvr,ru->idvu/dot_general | solution.py:42
  665.0 14.8 %fusion.11 = f32[80,4,8,512]{3,2,1,0:T(8,128)} fusion(f32[80,4,512,8]{2,3,1,0:T(8,128)S(1)} %convolution_add_fusion, f32[80,4,512,8]{2,3,1,0:T(8,128)S(1)} %convolution_subtract_fusion, f32[8,512]{1,0:T(8,128)S(1)} %get-tuple-element.43, f32[8,512]{1,0:T(8,128)S(1)} %get-tuple-element.44), kind=kOutput, calls=%fused_computation.31 | convolution fusion | flops 8060665856 | bytes 15761408 | tf_op jit(solution)/shard_map/idvr,ru->idvu/dot_general | solution.py:39
  679.9 15.2 %convolution_add_fusion.2 = f32[80,4,8,512]{3,2,1,0:T(8,128)} fusion(f32[80,4,8,512]{3,2,1,0:T(8,128)S(1)} %fusion.9, f32[80,4,512,8]{2,3,1,0:T(8,128)S(1)} %convolution_add_fusion, f32[80,4,512,8]{2,3,1,0:T(8,128)S(1)} %convolution_subtract_fusion, f32[8,512]{1,0:T(8,128)S(1)} %get-tuple-element.43, f32[8,512]{1,0:T(8,128)S(1)} %get-tuple-element.44), kind=kOutput, calls=%fused_computation.26 | convolution fusion | flops 8061976576 | bytes 21004288 | tf_op jit(solution)/shard_map/idvr,ru->idvu/dot_general | solution.py:42
  695.1 7.6 %reshape_reshape.7 = f32[8,10,4,4096]{3,2,1,0:T(4,128)} reshape(f32[80,4,8,512]{3,2,1,0:T(8,128)} %convolution_add_fusion.2) | data formatting | bytes 10485760 | tf_op jit(solution)/shard_map/reshape;reshape | solution.py:167
  702.7 19.4 %convolution_subtract_fusion.2 = f32[80,4,8,512]{3,2,1,0:T(8,128)} fusion(f32[80,4,8,512]{3,2,1,0:T(8,128)} %fusion.11, f32[80,4,512,8]{2,3,1,0:T(8,128)} %copy-done.1, f32[80,4,512,8]{2,3,1,0:T(8,128)} %copy-done, f32[8,512]{1,0:T(8,128)S(1)} %get-tuple-element.43, f32[8,512]{1,0:T(8,128)S(1)} %get-tuple-element.44), kind=kOutput, calls=%fused_computation.27 | convolution fusion | flops 8061976576 | bytes 21004288 | tf_op jit(solution)/shard_map/idvr,ru->idvu/dot_general | solution.py:39
  (78 shorter events, 124.1 us)
Async XLA Ops:
  7.2 25.3 %copy-start.3 = (f32[2,2]{1,0:T(2,128)S(1)}, f32[2,2]{1,0:T(2,128)}, u32[]{:S(2)}) copy-start(f32[2,2]{1,0:T(2,128)} %param.11) | copy-start | bytes 52
  7.2 26.0 %copy-start.4 = (s32[7]{0:T(128)S(1)}, s32[7]{0:T(128)}, u32[]{:S(2)}) copy-start(s32[7]{0:T(128)} %param.10) | copy-start | bytes 88
  7.2 18.2 %all-gather.2.cloned.1.call-start = ((), (), s32[]{:S(2)}) async-start(), calls=%async_computation.4 | async-start | bytes 3145728 | tf_op jit(solution)/shard_map/all_gather | solution.py:78
  29.1 27.0 %collective-permute-start = (f32[2,8,4,4096]{3,2,1,0:T(4,128)S(1)}, f32[2,8,4,4096]{3,2,1,0:T(4,128)S(1)}, u32[]{:S(2)}, u32[]{:S(2)}) collective-permute-start(f32[2,8,4,4096]{3,2,1,0:T(4,128)S(1)} %pad_maximum_fusion.2), channel_id=1, source_target_pairs={{0,64},{64,0},{1,65},{65,1},{2,66},{66,2},{3,67},{67,3},{4,68},{68... | collective-permute-start | bytes 3145736 | tf_op jit(solution)/shard_map/ppermute | solution.py:17
  80.8 118.3 %all-to-all-start.1 = ((f32[80,4,4096]{0,1,2:T(4,128)}), f32[80,4,4096]{0,1,2:T(4,128)}, u32[]{:S(2)}, u32[]{:S(2)}) async-start(f32[80,4,4096]{0,1,2:T(4,128)} %copy.93), calls=%async_computation.1 | async-start | bytes 16777216 | tf_op jit(solution)/shard_map/all_to_all | solution.py:149
  199.1 120.6 %all-to-all-start = ((f32[80,4,4096]{0,1,2:T(4,128)}), f32[80,4,4096]{0,1,2:T(4,128)}, u32[]{:S(2)}, u32[]{:S(2)}) async-start(f32[80,4,4096]{0,1,2:T(4,128)} %copy.89), calls=%async_computation | async-start | bytes 16777216 | tf_op jit(solution)/shard_map/all_to_all | solution.py:148
  328.8 13.2 %slice-start.2 = ((s8[5242880]{0:T(1024)(128)(4,1)}), s8[1048576]{0:T(1024)(128)(4,1)S(1)}, s32[]{:S(2)}) async-start(s8[5242880]{0:T(1024)(128)(4,1)} %bitcast.179), calls=%async_computation.7 | async-start | bytes 2097152
  335.2 6.8 slice-start.3
  342.0 11.0 %slice-start.4 = ((s8[5242880]{0:T(1024)(128)(4,1)}), s8[4194304]{0:T(1024)(128)(4,1)S(1)}, s32[]{:S(2)}) async-start(s8[5242880]{0:T(1024)(128)(4,1)} %bitcast.181), calls=%async_computation.9 | async-start | bytes 8388608
  346.5 6.5 slice-start.5
  369.6 75.2 %all-to-all-start.2 = ((f32[80,128,128]{2,0,1:T(8,128)}), f32[80,128,128]{2,0,1:T(8,128)}, u32[]{:S(2)}, u32[]{:S(2)}) async-start(f32[80,128,128]{2,0,1:T(8,128)} %copy.101), calls=%async_computation.2 | async-start | bytes 10485760 | tf_op jit(solution)/shard_map/all_to_all | solution.py:154
  444.8 169.8 %all-to-all-start.3 = ((f32[80,128,128]{2,0,1:T(8,128)}), f32[80,128,128]{2,0,1:T(8,128)}, u32[]{:S(2)}, u32[]{:S(2)}) async-start(f32[80,128,128]{2,0,1:T(8,128)} %copy.103), calls=%async_computation.3 | async-start | bytes 10485760 | tf_op jit(solution)/shard_map/all_to_all | solution.py:155
  629.3 7.3 copy-start.2
  629.3 15.2 %slice-start = ((s8[5242880]{0:T(1024)(128)(4,1)}), s8[4194304]{0:T(1024)(128)(4,1)S(1)}, s32[]{:S(2)}) async-start(s8[5242880]{0:T(1024)(128)(4,1)} %bitcast.177), calls=%async_computation.5 | async-start | bytes 8388608
  636.7 7.9 %slice-start.1 = ((s8[5242880]{0:T(1024)(128)(4,1)}), s8[1048576]{0:T(1024)(128)(4,1)S(1)}, s32[]{:S(2)}) async-start(s8[5242880]{0:T(1024)(128)(4,1)} %bitcast.177), calls=%async_computation.6 | async-start | bytes 2097152
  644.6 35.3 %copy-start = (f32[80,4,512,8]{2,3,1,0:T(8,128)}, f32[80,4,512,8]{2,3,1,0:T(8,128)S(1)}, u32[]{:S(2)}) copy-start(f32[80,4,512,8]{2,3,1,0:T(8,128)S(1)} %convolution_subtract_fusion) | copy-start | bytes 15728644
  651.2 28.7 %copy-start.1 = (f32[80,4,512,8]{2,3,1,0:T(8,128)}, f32[80,4,512,8]{2,3,1,0:T(8,128)S(1)}, u32[]{:S(2)}) copy-start(f32[80,4,512,8]{2,3,1,0:T(8,128)S(1)} %convolution_add_fusion) | copy-start | bytes 15728644
  729.7 5.0 slice-start.6
  729.7 5.0 slice-start.7
Sparse Core Ops, SparseCore 0:
  9.7 15.7 all-gather.1
where the time goes:
time: 761 us; the launch traced here: 752 us
  waiting for transfers between devices  279 us (37%)
  blocking collectives  132 us (17%)
  matrix products  123 us (16%)
  local copies, waits for them, and re-layouts  113 us (15%)
  starting transfers between devices  53.2 us (7%)
  other arithmetic  36.7 us (5%)
  between operations  14.6 us (2%)
    psum x1, blocking collectives, on_device(): band_power = lax.psum(partial_power, 'tm')  132 us
    all_to_all x1, waiting for transfers between devices, on_device(): lax.all_to_all(items[1], 'tm', split_axis=2, concat_axis=1, tiled=True)  99.7 us
    all_to_all x1, waiting for transfers between devices, on_device(): lax.all_to_all(items[0], 'tm', split_axis=2, concat_axis=1, tiled=True)  88.7 us
    all_to_all x1, waiting for transfers between devices, on_device(): lax.all_to_all(folded[0], 'tm', split_axis=1, concat_axis=2, tiled=True)  55.5 us
    dot_general x3, matrix products, complex_einsum(): jnp.einsum(form, left[1], right[1], precision=HIGHEST)  33.8 us
    dot_general x3, matrix products, complex_einsum(): jnp.einsum(form, left[1], right[0], precision=HIGHEST)  32.1 us
    dot_general x3, matrix products, complex_einsum(): jnp.einsum(form, left[0], right[0], precision=HIGHEST)  31.8 us
    dot_general x3, matrix products, complex_einsum(): jnp.einsum(form, left[0], right[1], precision=HIGHEST)  25.6 us
  transfers between devices with their start and end apart: 6, of which 5 were waited for; matrix products, arithmetic and copies ran while one was open for 9% of the time, Pallas kernels for 0%

commit v1 on v0

v1 whole, which is shorter than its diff:
```python
import math

import jax
import jax.numpy as jnp
import numpy as np
from jax import lax
from jax.experimental import pallas as pl
from jax.experimental.pallas import tpu as pltpu

FOLD = 128
COLS = 4096
BINS = FOLD * COLS
BANDS = 8
CHUNK = 512
STEPS = COLS // CHUNK
LANES = 128
OUT_ROWS = 32
SPACED = True


def rows_of(part):
    tau = np.arange(OUT_ROWS)
    return 4 * tau + part if SPACED else 32 * part + tau


def halves(table):
    high = np.asarray(table, np.float32).astype(jnp.bfloat16)
    low = (np.asarray(table, np.float64) - high.astype(np.float64)).astype(np.float32)
    return high, low.astype(jnp.bfloat16)


def pack_columns(real, imag):
    m = real.shape[0]
    xp = np if isinstance(real, np.ndarray) else jnp
    parts = xp.stack([real.reshape(m, 32, 4), imag.reshape(m, 32, 4)], axis=2)
    return parts.reshape(m, 256)


def stacked_rows(cos, sin, xp=np):
    top = pack_columns(cos, -sin)
    bottom = pack_columns(sin, cos)
    return xp.concatenate([top, bottom], axis=0)


def constant_tables():
    b = np.arange(FOLD)
    even, odd, twiddle = [], [], []
    for part in range(4):
        e = rows_of(part)
        angle = 2 * np.pi * ((e[:, None] * b[None, :]) % FOLD) / FOLD
        cos, sin = np.cos(angle), np.sin(angle)
        for parity, group in ((0, even), (1, odd)):
            blocks = []
            for band in range(parity, BANDS, 2):
                inside = (b >= 16 * band - 8) & (b < 16 * band + 24)
                blocks.append(stacked_rows(cos * inside, sin * inside))
            group.append(np.concatenate(blocks, axis=0))
        a = np.arange(COLS)
        angle = 2 * np.pi * (e[:, None] * a[None, :]) / BINS
        twiddle.append(np.stack([np.cos(angle), np.sin(angle)]))
    even = halves(np.stack(even))
    odd = halves(np.stack(odd))
    bands = np.stack([even[0], even[1], odd[0], odd[1]], axis=1)
    twiddle = np.stack(twiddle).astype(np.float32)
    a1 = np.arange(LANES)
    q2 = np.arange(32)
    angle = 2 * np.pi * (a1[None, :] * q2[:, None]) / COLS
    inner = np.stack([np.cos(angle), np.sin(angle)]).astype(np.float32)
    angle = 2 * np.pi * ((a1[:, None] * a1[None, :]) % LANES) / LANES
    cos, sin = np.cos(angle), np.sin(angle)
    last = np.stack(halves(np.block([[cos, sin], [-sin, cos]])))
    place = np.zeros((512, 512), np.float32)
    u1, u2 = np.meshgrid(np.arange(128), np.arange(4), indexing="ij")
    place[(u2 * 128 + u1).ravel(), (u2 + 4 * u1).ravel()] = 1.0
    return bands, twiddle, inner, last, place.astype(jnp.bfloat16)


def split_two(x):
    high = x.astype(jnp.bfloat16)
    low = (x - high.astype(jnp.float32)).astype(jnp.bfloat16)
    return high, low


def mm(a, b):
    return jnp.dot(a, b, preferred_element_type=jnp.float32)


ROOT = math.sqrt(0.5)


def eight(x):
    def add(p, q):
        return (p[0] + q[0], p[1] + q[1])

    def sub(p, q):
        return (p[0] - q[0], p[1] - q[1])

    def turn(p):
        return (-p[1], p[0])

    def addi(p, q):
        return (p[0] - q[1], p[1] + q[0])

    def subi(p, q):
        return (p[0] + q[1], p[1] - q[0])

    def four(z):
        s02, d02 = add(z[0], z[2]), sub(z[0], z[2])
        s13, d13 = add(z[1], z[3]), sub(z[1], z[3])
        return [add(s02, s13), addi(d02, d13), sub(s02, s13), subi(d02, d13)]

    ev = four([x[0], x[2], x[4], x[6]])
    od = four([x[1], x[3], x[5], x[7]])
    o1 = ((od[1][0] - od[1][1]) * ROOT, (od[1][0] + od[1][1]) * ROOT)
    o3 = ((od[3][0] + od[3][1]) * ROOT, (od[3][1] - od[3][0]) * ROOT)
    return [
        add(ev[0], od[0]),
        add(ev[1], o1),
        addi(ev[2], od[2]),
        sub(ev[3], o3),
        sub(ev[0], od[0]),
        sub(ev[1], o1),
        subi(ev[2], od[2]),
        add(ev[3], o3),
    ]


def four_point(z):
    s0 = (z[0][0] + z[2][0], z[0][1] + z[2][1])
    d0 = (z[0][0] - z[2][0], z[0][1] - z[2][1])
    s1 = (z[1][0] + z[3][0], z[1][1] + z[3][1])
    d1 = (z[1][0] - z[3][0], z[1][1] - z[3][1])
    return [
        (s0[0] + s1[0], s0[1] + s1[1]),
        (d0[0] - d1[1], d0[1] + d1[0]),
        (s0[0] - s1[0], s0[1] - s1[1]),
        (d0[0] + d1[1], d0[1] - d1[0]),
    ]


def times(x, c, s):
    return (x[0] * c - x[1] * s, x[0] * s + x[1] * c)


def swap_halves(x):
    rows, width = x.shape
    return pltpu.roll(x.reshape(rows // 8, 8, width), 4, 1).reshape(rows, width)


def kernel(
    where_ref, bounds_ref, tmpl_ref, own_ref, oth_ref, bands_ref, net_ref, twiddle_ref, ramp_ref,
    inner_ref, last_ref, place_ref, response_ref, out_ref,
    series, net_oth, xe, xo, xn, power, zbuf, bbuf, vbuf,
):
    step = pl.program_id(0)
    start = step * CHUNK

    @pl.when(step == 0)
    def _():
        power[...] = jnp.zeros_like(power)

    sub = lax.broadcasted_iota(jnp.int32, (16, CHUNK), 0)
    lane = lax.broadcasted_iota(jnp.int32, (16, CHUNK), 1)
    top = (sub & 7) < 4
    place_in = ((sub >> 3) * 4 + (sub & 3)) * COLS + lane + start
    for group in range(16):
        rows = slice(16 * group, 16 * group + 16)
        wave = tmpl_ref[rows, :]
        rolled = swap_halves(wave)
        wave_re = jnp.where(top, wave, rolled)
        wave_im = jnp.where(top, rolled, -wave)
        own = own_ref[0, rows, :]
        own = own * wave_re + swap_halves(own) * wave_im
        oth = oth_ref[0, rows, :]
        oth = oth * wave_re + swap_halves(oth) * wave_im
        bound = (group - 1) // 2
        upper = (place_in + 8 * group * COLS) >= bounds_ref[bound + 1]
        even = upper if bound % 2 else jnp.logical_not(upper)
        squares = wave * wave
        low_sum = jnp.where(upper, 0.0, squares)
        fold = lambda v: sum(
            v[r : r + 8, c : c + LANES] for r in (0, 8) for c in range(0, CHUNK, LANES)
        )
        power[2 * group] += fold(low_sum)
        power[2 * group + 1] += fold(squares)
        high = own.astype(jnp.bfloat16).astype(jnp.float32)
        low = own - high
        xe[0, rows, :] = jnp.where(even, high, 0.0).astype(jnp.bfloat16)
        xe[1, rows, :] = jnp.where(even, low, 0.0).astype(jnp.bfloat16)
        xo[0, rows, :] = jnp.where(even, 0.0, high).astype(jnp.bfloat16)
        xo[1, rows, :] = jnp.where(even, 0.0, low).astype(jnp.bfloat16)
        high, low = split_two(oth)
        xn[0, rows, :] = high
        xn[1, rows, :] = low
    cols = pl.ds(pl.multiple_of(start, CHUNK), CHUNK)

    def three(high, low, x):
        return mm(high, x[0]) + mm(low, x[0]) + mm(high, x[1])

    series[0:256, cols] = three(bands_ref[0, 0], bands_ref[0, 1], xe)
    series[256:512, cols] = three(bands_ref[0, 2], bands_ref[0, 3], xo)
    series[512:640, cols] = three(net_ref[0, 0], net_ref[0, 1], xe) + three(net_ref[0, 0], net_ref[0, 1], xo)
    net_oth[:, cols] = three(net_ref[1, 0], net_ref[1, 1], xn)

    @pl.when(step == STEPS - 1)
    def _():
        total = jnp.zeros((1, 1), jnp.float32)
        powers = []
        for band in range(BANDS):
            acc = jnp.zeros((8, LANES), jnp.float32)
            for group in range(16):
                bound = (group - 1) // 2
                if bound == band:
                    acc += power[2 * group]
                if bound + 1 == band:
                    acc += power[2 * group + 1] - power[2 * group]
            value = jnp.sum(jnp.sum(acc, axis=0, keepdims=True), axis=1, keepdims=True)
            powers.append(value)
            total = total + value
        shares = [value / total for value in powers]
        inverse = [(1.0 / (2 * BANDS - 2)) / (total * share) for share in shares]
        net_scale = 1.0 / (total * response_ref[0])

        def block(eb, carry):
            first = pl.multiple_of(eb * 8, 8)
            erows = pl.ds(first, 8)

            def load(item, a2):
                columns = slice(a2 * LANES, (a2 + 1) * LANES)
                if item < 8:
                    base = (item // 2) * 64 + (item % 2) * 256
                    re = series[pl.ds(base + first, 8), columns]
                    im = series[pl.ds(base + 32 + first, 8), columns]
                else:
                    slide = item - 8
                    base = 512 + 64 * slide
                    own = (series[pl.ds(base + first, 8), columns], series[pl.ds(base + 32 + first, 8), columns])
                    base = 64 * slide
                    oth = (net_oth[pl.ds(base + first, 8), columns], net_oth[pl.ds(base + 32 + first, 8), columns])
                    own = times(own, ramp_ref[slide, 0:1, columns], ramp_ref[slide, 1:2, columns])
                    oth = times(oth, ramp_ref[slide, 2:3, columns], ramp_ref[slide, 3:4, columns])
                    re, im = own[0] + oth[0], own[1] + oth[1]
                return times((re, im), twiddle_ref[0, 0, erows, columns], twiddle_ref[0, 1, erows, columns])

            for item in range(10):
                slot = item % 2
                halfway = []
                for r2 in range(4):
                    values = eight([load(item, 4 * s + r2) for s in range(8)])
                    turned = []
                    for v in range(8):
                        if r2 * v == 0:
                            turned.append(values[v])
                        else:
                            angle = 2 * math.pi * r2 * v / 32
                            turned.append(times(values[v], math.cos(angle), math.sin(angle)))
                    halfway.append(turned)
                for v in range(8):
                    done = four_point([halfway[r2][v] for r2 in range(4)])
                    for u2 in range(4):
                        q2 = v + 8 * u2
                        z = times(done[u2], inner_ref[0, q2 : q2 + 1, :], inner_ref[1, q2 : q2 + 1, :])
                        zbuf[slot, q2 * 8 : q2 * 8 + 8, 0:LANES] = z[0]
                        zbuf[slot, q2 * 8 : q2 * 8 + 8, LANES : 2 * LANES] = z[1]
                high, low = split_two(zbuf[slot])
                bbuf[item] = mm(high, last_ref[0]) + mm(low, last_ref[0]) + mm(high, last_ref[1])
            for q2 in range(32):
                rows = slice(q2 * 8, q2 * 8 + 8)
                v, u2 = q2 % 8, q2 // 8
                at = (slice(v * 8, v * 8 + 8), slice(u2 * LANES, (u2 + 1) * LANES))
                re = [bbuf[band, rows, 0:LANES] for band in range(BANDS)]
                im = [bbuf[band, rows, LANES : 2 * LANES] for band in range(BANDS)]
                whole_re, whole_im = sum(re), sum(im)
                chi = jnp.zeros((8, LANES), jnp.float32)
                for band in range(BANDS):
                    gap_re = re[band] - shares[band] * whole_re
                    gap_im = im[band] - shares[band] * whole_im
                    chi = chi + (gap_re * gap_re + gap_im * gap_im) * inverse[band]
                vbuf[0, at[0], at[1]] = chi
                for slide in range(2):
                    re = bbuf[8 + slide, rows, 0:LANES]
                    im = bbuf[8 + slide, rows, LANES : 2 * LANES]
                    vbuf[1 + slide, at[0], at[1]] = (re * re + im * im) * net_scale
            for kind in range(3):
                high, low = split_two(vbuf[kind])
                done = mm(high, place_ref[...]) + mm(low, place_ref[...])
                for v in range(8):
                    out_ref[kind, erows, v * 512 : (v + 1) * 512] = done[v * 8 : v * 8 + 8, :]
            return carry

        lax.fori_loop(0, OUT_ROWS // 8, block, 0)


def filter_rows(part, det, tmpl, strain, bounds, net_tables, ramp, response):
    bands, twiddle, inner, last, place = constant_tables()
    where = jnp.stack([part, det]).astype(jnp.int32)
    edges = jnp.concatenate([jnp.zeros((1,), jnp.int32), bounds, jnp.full((1,), BINS, jnp.int32)])
    one = pl.Buffered(1)
    spec = pltpu.PrefetchScalarGridSpec(
        num_scalar_prefetch=2,
        grid=(STEPS,),
        in_specs=[
            pl.BlockSpec((256, CHUNK), lambda i, w, e: (0, i)),
            pl.BlockSpec((1, 256, CHUNK), lambda i, w, e: (w[1], 0, i)),
            pl.BlockSpec((1, 256, CHUNK), lambda i, w, e: (1 - w[1], 0, i)),
            pl.BlockSpec((1, 4, 256, 256), lambda i, w, e: (w[0], 0, 0, 0), pipeline_mode=one),
            pl.BlockSpec((2, 2, 128, 256), lambda i, w, e: (0, 0, 0, 0), pipeline_mode=one),
            pl.BlockSpec((1, 2, OUT_ROWS, COLS), lambda i, w, e: (w[0], 0, 0, 0), pipeline_mode=one),
            pl.BlockSpec((2, 4, COLS), lambda i, w, e: (0, 0, 0), pipeline_mode=one),
            pl.BlockSpec((2, 32, LANES), lambda i, w, e: (0, 0, 0), pipeline_mode=one),
            pl.BlockSpec((2, 256, 256), lambda i, w, e: (0, 0, 0), pipeline_mode=one),
            pl.BlockSpec((512, 512), lambda i, w, e: (0, 0), pipeline_mode=one),
            pl.BlockSpec(memory_space=pltpu.SMEM),
        ],
        out_specs=pl.BlockSpec((3, OUT_ROWS, COLS), lambda i, w, e: (0, 0, 0), pipeline_mode=one),
        scratch_shapes=[
            pltpu.VMEM((640, COLS), jnp.float32),
            pltpu.VMEM((128, COLS), jnp.float32),
            pltpu.VMEM((2, 256, CHUNK), jnp.bfloat16),
            pltpu.VMEM((2, 256, CHUNK), jnp.bfloat16),
            pltpu.VMEM((2, 256, CHUNK), jnp.bfloat16),
            pltpu.VMEM((32, 8, LANES), jnp.float32),
            pltpu.VMEM((2, 256, 256), jnp.float32),
            pltpu.VMEM((10, 256, 256), jnp.float32),
            pltpu.VMEM((3, 64, 512), jnp.float32),
        ],
    )
    return pl.pallas_call(
        kernel,
        grid_spec=spec,
        out_shape=jax.ShapeDtypeStruct((3, OUT_ROWS, COLS), jnp.float32),
        compiler_params=pltpu.CompilerParams(vmem_limit_bytes=48 * 2**20),
        cost_estimate=pl.CostEstimate(flops=20 * 10**9, bytes_accessed=20 * 10**6, transcendentals=0),
    )(
        where, edges, tmpl, strain, strain, jnp.asarray(bands), net_tables, jnp.asarray(twiddle), ramp,
        jnp.asarray(inner), jnp.asarray(last), jnp.asarray(place), response,
    )


def dynamic_tables(part, det, slides_mine, antenna):
    tau = jnp.arange(OUT_ROWS, dtype=jnp.int32)
    e = 4 * tau + part if SPACED else 32 * part + tau
    b = jnp.arange(FOLD, dtype=jnp.int32)
    a = jnp.arange(COLS, dtype=jnp.int32)

    def unit(index, total):
        angle = (index % total).astype(jnp.float32) * (2.0 * math.pi / total)
        return jnp.cos(angle), jnp.sin(angle)

    tables, ramps = [], []
    for which in (det, 1 - det):
        moving = which == 1
        weight_re, weight_im = antenna[which, 0], antenna[which, 1]
        rows, cols = [], []
        for slide in range(2):
            shift = jnp.where(moving, slides_mine[slide], 0)
            cos, sin = unit((e[:, None] + shift % FOLD) * b[None, :], FOLD)
            re = weight_re * cos - weight_im * sin
            im = weight_re * sin + weight_im * cos
            rows.append(stacked_rows(re, im, jnp))
            cols.append(jnp.stack(unit(a * shift, BINS)))
        table = jnp.concatenate(rows, axis=0)
        high = lax.reduce_precision(table, 8, 7)
        tables.append(jnp.stack([high.astype(jnp.bfloat16), (table - high).astype(jnp.bfloat16)]))
        ramps.append(jnp.stack(cols))
    return jnp.stack(tables), jnp.concatenate(ramps, axis=1)


def on_device(strain, bank, assignment, slides, bounds, antenna):
    tm = lax.axis_index("tm")
    det = lax.axis_index("det")
    grp = lax.axis_index("grp")
    packed = bank.reshape(8, 8, COLS)
    both = lax.all_gather(packed, "grp", axis=0, tiled=True)
    mine = lax.dynamic_slice_in_dim(assignment, grp * 8, 8)
    chosen = jnp.take(both, jnp.repeat(mine, 4), axis=0)
    tmpl = lax.all_to_all(chosen, "tm", split_axis=0, concat_axis=0, tiled=True)
    signal = lax.all_gather(strain.reshape(8, COLS), ("det", "tm"), axis=0, tiled=False)
    part = tm % 4
    mine = lax.dynamic_slice_in_dim(slides, det * 2, 2)
    net_tables, ramp = dynamic_tables(part, det, mine, antenna)
    rows = filter_rows(
        part, det, tmpl.reshape(256, COLS), signal.reshape(2, 256, COLS), bounds, net_tables, ramp,
        jnp.sum(antenna * antenna)[None],
    )
    sent = lax.all_to_all(jnp.swapaxes(rows, 0, 1), "tm", split_axis=0, concat_axis=0, tiled=True)
    sent = sent.reshape(8, 4, 3, COLS)
    return sent[None, :, :, 0], jnp.swapaxes(sent[:, :, 1:], 1, 2)


def solution(mesh):
    P = jax.sharding.PartitionSpec
    return jax.shard_map(
        on_device,
        mesh=mesh,
        in_specs=(P("det", None, "tm", None), P("grp", None, "tm", None), P(), P(), P(), P()),
        out_specs=(P("det", "grp", "tm", None), P("grp", "det", "tm", None)),
        check_vma=False,
    )
```

time: 761 us -> 453 us (0.60); the launches traced: 752 us -> 453 us
  matrix products: 123 us -> 0 us
  blocking collectives: 132 us -> 21.2 us
  local copies, waits for them, and re-layouts: 113 us -> 18.5 us
  waiting for transfers between devices: 279 us -> 349 us
  starting transfers between devices: 53.2 us -> 8.85 us
  Pallas kernels: 0 us -> 26.9 us
  other arithmetic: 36.7 us -> 11.6 us
    all_gather x1 -> x2, waiting for transfers between devices: 12.8 us -> 283 us  [the longest x1 281 us: on_device(): lax.all_gather(strain.reshape(8, COLS), ('det', 'tm'), axis=0, tiled=False)]
    all_to_all x4 -> x1, waiting for transfers between devices: 244 us -> 65.9 us  [on_device(): tmpl = lax.all_to_all(chosen, 'tm', split_axis=0, concat_axis=0, tiled=True)]
    psum x1 -> x0, blocking collectives: 132 us -> none  [on_device(): band_power = lax.psum(partial_power, 'tm')]
    dot_general x12 -> x0, matrix products: 123 us -> none  [the longest x3 33.8 us: complex_einsum(): jnp.einsum(form, left[1], right[1], precision=HIGHEST)]
    all_to_all x6 -> x0, local copies, waits for them, and re-layouts: 46.2 us -> none  [the longest x2 15.4 us: on_device(): lax.all_to_all(items[0], 'tm', split_axis=2, concat_axis=1, tiled=True)]
    all_to_all x4 -> x1, starting transfers between devices: 49.9 us -> 8.77 us  [on_device(): tmpl = lax.all_to_all(chosen, 'tm', split_axis=0, concat_axis=0, tiled=True)]
    reshape x4 -> x3, local copies, waits for them, and re-layouts: 34.5 us -> 2.72 us  [the longest x1 2.55 us: on_device(): packed = bank.reshape(8, 8, COLS)]
    pallas_call x0 -> x1, Pallas kernels: none -> 26.9 us  [filter_rows(): pl.pallas_call(kernel, grid_spec=spec, out_shape=jax.ShapeDtypeStruct((3,...]
  transfers between devices with their start and end apart: 6 -> 3, of which waited for: 5 -> 3; matrix products, arithmetic and copies ran while one was open for 9% -> 5% of each run, Pallas kernels for 0% -> 0%
where the time goes in v1:
time: 453 us
  waiting for transfers between devices  349 us (77%)
  Pallas kernels  26.9 us (6%)
  blocking collectives  21.2 us (5%)
  local copies, waits for them, and re-layouts  18.5 us (4%)
  between operations  16.7 us (4%)
  other arithmetic  11.6 us (3%)
  starting transfers between devices  8.85 us (2%)
    all_gather x1, waiting for transfers between devices, on_device(): lax.all_gather(strain.reshape(8, COLS), ('det', 'tm'), axis=0, tiled=False)  281 us
    all_to_all x1, waiting for transfers between devices, on_device(): tmpl = lax.all_to_all(chosen, 'tm', split_axis=0, concat_axis=0, tiled=True)  65.9 us
    pallas_call x1, Pallas kernels, filter_rows(): pl.pallas_call(kernel, grid_spec=spec, out_shape=jax.ShapeDtypeStruct((3,...  26.9 us
    all_to_all x1, blocking collectives, on_device(): lax.all_to_all(jnp.swapaxes(rows, 0, 1), 'tm', split_axis=0, concat_axis=...  21.2 us
  transfers between devices with their start and end apart: 3, of which 3 were waited for; matrix products, arithmetic and copies ran while one was open for 5% of the time, Pallas kernels for 0%

profile of v1, /device:TPU:0, one launch (start us, length us, event | category | flops | bytes accessed | tf_op | source)
XLA Modules:
  0.0 452.6 jit_solution(3246978589970399227)
XLA Ops:
  7.2 2.6 reshape.993
  9.8 1.6 all_gather_reshape.3
  11.5 0.7 dynamic_slice.20
  12.2 0.6 fusion.47
  15.2 0.7 dynamic_slice.18
  16.1 1.4 constant_dynamic-slice_fusion.3
  17.6 3.4 fusion.22
  22.8 0.7 multiply_reduce_fusion
  23.7 2.4 all-gather.3.cloned.1.call-done
  26.0 4.3 gather_fusion
  30.4 4.7 %broadcast_select_fusion = f32[32,8,4096]{2,1,0:T(8,128)} fusion(f32[32,8,4096]{2,1,0:T(8,128)} %gather_fusion, pred[32]{0:T(512)(128)(4,1)S(1)} %compare_and_fusion), kind=kLoop, calls=%fused_computation.1 | loop fusion | flops 1048576 | bytes 8388640 | tf_op jit(solution)/shard_map/jit(_take)/select_n | solution.py:376
  35.1 8.8 %all-to-all-start = ((f32[32,8,4096]{2,1,0:T(8,128)}), f32[32,8,4096]{2,1,0:T(8,128)}, u32[]{:S(2)}, u32[]{:S(2)}) async-start(f32[32,8,4096]{2,1,0:T(8,128)} %broadcast_select_fusion), calls=%async_computation | async-start | bytes 8388608 | tf_op jit(solution)/shard_map/all_to_all | solution.py:377
  44.0 0.5 fusion.40
  44.5 0.5 fusion.38
  45.0 0.5 fusion.44
  45.6 0.5 fusion.42
  46.3 65.9 %all-to-all-done = f32[32,8,4096]{2,1,0:T(8,128)} async-done(((f32[32,8,4096]{2,1,0:T(8,128)}), f32[32,8,4096]{2,1,0:T(8,128)}, u32[]{:S(2)}, u32[]{:S(2)}) %all-to-all-start) | async-done | bytes 4194336 | tf_op jit(solution)/shard_map/all_to_all | solution.py:377
  112.3 280.6 %all-gather.5.cloned.1.call-done = f32[64,8,4096]{2,1,0:T(8,128)} async-done(((f32[1,8,4096]{2,1,0:T(8,128)}), f32[64,8,4096]{2,1,0:T(8,128)}) %all-gather.5.cloned.1.call-update) | async-done | bytes 8388624 | tf_op jit(solution)/shard_map/all_gather | solution.py:378
  392.9 26.9 %shard_map.122 = f32[3,32,4096]{2,1,0:T(8,128)S(1)} custom-call(s32[2]{0:T(128)S(1)} %pad_add_fusion.where_ref, s32[9]{0:T(128)S(1)} %pad_add_fusion.1.bounds_ref, f32[256,4096]{1,0:T(8,128)} %bitcast.3.tmpl_ref, f32[2,256,4096]{2,1,0:T(8,128)} %bitcast.54, f32[2,256,4096]{2,1,0:T(8,128)} %bitcast.55, bf16[4,4,256,256]{3,2,1,0:T(8,128)(2,1)S(1)} %copy-done, ...), custom_call_target="tpu_custom_call" | custom-call | flops 20000000000 | bytes 20000000 | tf_op jit(solution)/shard_map/pallas_call | solution.py:328
  419.8 1.1 copy.50
  420.9 21.2 %all_to_all.10 = f32[32,3,4096]{2,1,0:T(4,128)S(1)} all-to-all(f32[32,3,4096]{2,1,0:T(4,128)S(1)} %copy.50), channel_id=1, replica_groups=mesh['det'=2,'grp'=2,'tm'=32] {'tm'}, dimensions={0} | all-to-all | bytes 3145728 | tf_op jit(solution)/shard_map/all_to_all | solution.py:386
  442.0 0.6 slice.21
  443.0 1.7 copy.57
  444.7 1.1 copy.58
  (58 shorter events, 2.9 us)
Async XLA Ops:
  7.2 18.9 %all-gather.3.cloned.1.call-start = ((), (), s32[]{:S(2)}) async-start(), calls=%async_computation.2 | async-start | bytes 3145728 | tf_op jit(solution)/shard_map/all_gather | solution.py:374
  9.8 13.0 %copy-start.4 = (f32[2,2]{1,0:T(2,128)S(1)}, f32[2,2]{1,0:T(2,128)}, u32[]{:S(2)}) copy-start(f32[2,2]{1,0:T(2,128)} %param.16) | copy-start | bytes 52
  9.8 383.1 %all-gather.5.cloned.1.call-start = ((), (), s32[]{:S(2)}) async-start(), calls=%async_computation.3 | async-start | bytes 8519680 | tf_op jit(solution)/shard_map/all_gather | solution.py:378
  35.1 8.8 %copy-start.5 = (s32[7]{0:T(128)S(1)}, s32[7]{0:T(128)}, u32[]{:S(2)}) copy-start(s32[7]{0:T(128)} %param.15) | copy-start | bytes 88
  35.1 357.8 %copy-start = (bf16[4,4,256,256]{3,2,1,0:T(8,128)(2,1)S(1)}, bf16[4,4,256,256]{3,2,1,0:T(8,128)(2,1)}, u32[]{:S(2)}) copy-start(bf16[4,4,256,256]{3,2,1,0:T(8,128)(2,1)} %constant.181.clone.bands_ref) | copy-start | bytes 6291460
  35.1 357.8 %copy-start.1 = (bf16[512,512]{1,0:T(8,128)(2,1)S(1)}, bf16[512,512]{1,0:T(8,128)(2,1)}, u32[]{:S(2)}) copy-start(bf16[512,512]{1,0:T(8,128)(2,1)} %constant.185.clone.place_ref) | copy-start | bytes 1572868
  35.1 357.8 %copy-start.2 = (bf16[2,256,256]{2,1,0:T(8,128)(2,1)S(1)}, bf16[2,256,256]{2,1,0:T(8,128)(2,1)}, u32[]{:S(2)}) copy-start(bf16[2,256,256]{2,1,0:T(8,128)(2,1)} %constant.184.clone.last_ref) | copy-start | bytes 786436
  35.1 357.8 %copy-start.3 = (f32[2,32,128]{2,1,0:T(8,128)S(1)}, f32[2,32,128]{2,1,0:T(8,128)}, u32[]{:S(2)}) copy-start(f32[2,32,128]{2,1,0:T(8,128)} %constant.183.clone.inner_ref) | copy-start | bytes 98308
  35.1 77.2 %all-to-all-start = ((f32[32,8,4096]{2,1,0:T(8,128)}), f32[32,8,4096]{2,1,0:T(8,128)}, u32[]{:S(2)}, u32[]{:S(2)}) async-start(f32[32,8,4096]{2,1,0:T(8,128)} %broadcast_select_fusion), calls=%async_computation | async-start | bytes 8388608 | tf_op jit(solution)/shard_map/all_to_all | solution.py:377
Sparse Core Ops, SparseCore 0:
  10.2 15.7 all-gather.2
  28.2 364.5 all-gather.4

commit v2 on v1

--- a/solution.py
+++ b/solution.py
@@ -15,12 +15,11 @@
 STEPS = COLS // CHUNK
 LANES = 128
 OUT_ROWS = 32
-SPACED = True
 
 
 def rows_of(part):
     tau = np.arange(OUT_ROWS)
-    return 4 * tau + part if SPACED else 32 * part + tau
+    return OUT_ROWS * part + tau
 
 
 def halves(table):
@@ -31,15 +30,14 @@
 
 def pack_columns(real, imag):
     m = real.shape[0]
-    xp = np if isinstance(real, np.ndarray) else jnp
-    parts = xp.stack([real.reshape(m, 32, 4), imag.reshape(m, 32, 4)], axis=2)
+    parts = np.stack([real.reshape(m, 32, 4), imag.reshape(m, 32, 4)], axis=2)
     return parts.reshape(m, 256)
 
 
-def stacked_rows(cos, sin, xp=np):
+def stacked_rows(cos, sin):
     top = pack_columns(cos, -sin)
     bottom = pack_columns(sin, cos)
-    return xp.concatenate([top, bottom], axis=0)
+    return np.concatenate([top, bottom], axis=0)
 
 
 def constant_tables():
@@ -148,9 +146,9 @@
 
 
 def kernel(
-    where_ref, bounds_ref, tmpl_ref, own_ref, oth_ref, bands_ref, net_ref, twiddle_ref, ramp_ref,
-    inner_ref, last_ref, place_ref, response_ref, out_ref,
-    series, net_oth, xe, xo, xn, power, zbuf, bbuf, vbuf,
+    where_ref, bounds_ref, tmpl_ref, own_ref, oth_ref, bands_ref, twiddle_ref,
+    inner_ref, last_ref, place_ref, slides_ref, antenna_ref, out_ref,
+    net_ref, ramp_ref, series, net_oth, xe, xo, xn, power, zbuf, bbuf, vbuf,
 ):
     step = pl.program_id(0)
     start = step * CHUNK
@@ -158,6 +156,30 @@
     @pl.when(step == 0)
     def _():
         power[...] = jnp.zeros_like(power)
+        part, det = where_ref[0], where_ref[1]
+        column = (
+            lax.broadcasted_iota(jnp.int32, (32, LANES), 0) * LANES
+            + lax.broadcasted_iota(jnp.int32, (32, LANES), 1)
+        )
+        row = lax.broadcasted_iota(jnp.int32, (OUT_ROWS, 256), 0) + OUT_ROWS * part
+        packed = lax.broadcasted_iota(jnp.int32, (OUT_ROWS, 256), 1)
+        bin_row = (packed >> 3) * 4 + (packed & 3)
+        quarter = ((packed >> 2) & 1) * (FOLD // 4)
+        for side in range(2):
+            which = det if side == 0 else 1 - det
+            weight_re, weight_im = antenna_ref[which, 0], antenna_ref[which, 1]
+            for slide in range(2):
+                shift = which * slides_ref[2 * det + slide]
+                angle = (((row + shift) * bin_row + quarter) & (FOLD - 1)).astype(jnp.float32) * (2.0 * math.pi / FOLD)
+                for half, table in ((0, jnp.cos(angle)), (1, jnp.sin(angle))):
+                    high, low = split_two(table)
+                    at = slice(64 * slide + 32 * half, 64 * slide + 32 * half + 32)
+                    net_ref[side, 0, at, :] = high
+                    net_ref[side, 1, at, :] = low
+                angle = ((column * shift) & (BINS - 1)).astype(jnp.float32) * (2.0 * math.pi / BINS)
+                cos, sin = jnp.cos(angle), jnp.sin(angle)
+                ramp_ref[slide, 2 * side] = weight_re * cos - weight_im * sin
+                ramp_ref[slide, 2 * side + 1] = weight_re * sin + weight_im * cos
 
     sub = lax.broadcasted_iota(jnp.int32, (16, CHUNK), 0)
     lane = lax.broadcasted_iota(jnp.int32, (16, CHUNK), 1)
@@ -219,7 +241,8 @@
             total = total + value
         shares = [value / total for value in powers]
         inverse = [(1.0 / (2 * BANDS - 2)) / (total * share) for share in shares]
-        net_scale = 1.0 / (total * response_ref[0])
+        response = sum(antenna_ref[d, c] * antenna_ref[d, c] for d in range(2) for c in range(2))
+        net_scale = 1.0 / (total * response)
 
         def block(eb, carry):
             first = pl.multiple_of(eb * 8, 8)
@@ -237,8 +260,8 @@
                     own = (series[pl.ds(base + first, 8), columns], series[pl.ds(base + 32 + first, 8), columns])
                     base = 64 * slide
                     oth = (net_oth[pl.ds(base + first, 8), columns], net_oth[pl.ds(base + 32 + first, 8), columns])
-                    own = times(own, ramp_ref[slide, 0:1, columns], ramp_ref[slide, 1:2, columns])
-                    oth = times(oth, ramp_ref[slide, 2:3, columns], ramp_ref[slide, 3:4, columns])
+                    own = times(own, ramp_ref[slide, 0, a2 : a2 + 1, :], ramp_ref[slide, 1, a2 : a2 + 1, :])
+                    oth = times(oth, ramp_ref[slide, 2, a2 : a2 + 1, :], ramp_ref[slide, 3, a2 : a2 + 1, :])
                     re, im = own[0] + oth[0], own[1] + oth[1]
                 return times((re, im), twiddle_ref[0, 0, erows, columns], twiddle_ref[0, 1, erows, columns])
 
@@ -285,13 +308,15 @@
                 high, low = split_two(vbuf[kind])
                 done = mm(high, place_ref[...]) + mm(low, place_ref[...])
                 for v in range(8):
-                    out_ref[kind, erows, v * 512 : (v + 1) * 512] = done[v * 8 : v * 8 + 8, :]
+                    both = done[v * 8 : v * 8 + 8, :]
+                    out_ref[kind, 2 * eb, :, v * 512 : (v + 1) * 512] = both[0:4]
+                    out_ref[kind, 2 * eb + 1, :, v * 512 : (v + 1) * 512] = both[4:8]
             return carry
 
         lax.fori_loop(0, OUT_ROWS // 8, block, 0)
 
 
-def filter_rows(part, det, tmpl, strain, bounds, net_tables, ramp, response):
+def filter_rows(part, det, tmpl, strain, bounds, slides, antenna):
     bands, twiddle, inner, last, place = constant_tables()
     where = jnp.stack([part, det]).astype(jnp.int32)
     edges = jnp.concatenate([jnp.zeros((1,), jnp.int32), bounds, jnp.full((1,), BINS, jnp.int32)])
@@ -304,16 +329,17 @@
             pl.BlockSpec((1, 256, CHUNK), lambda i, w, e: (w[1], 0, i)),
             pl.BlockSpec((1, 256, CHUNK), lambda i, w, e: (1 - w[1], 0, i)),
             pl.BlockSpec((1, 4, 256, 256), lambda i, w, e: (w[0], 0, 0, 0), pipeline_mode=one),
-            pl.BlockSpec((2, 2, 128, 256), lambda i, w, e: (0, 0, 0, 0), pipeline_mode=one),
             pl.BlockSpec((1, 2, OUT_ROWS, COLS), lambda i, w, e: (w[0], 0, 0, 0), pipeline_mode=one),
-            pl.BlockSpec((2, 4, COLS), lambda i, w, e: (0, 0, 0), pipeline_mode=one),
             pl.BlockSpec((2, 32, LANES), lambda i, w, e: (0, 0, 0), pipeline_mode=one),
             pl.BlockSpec((2, 256, 256), lambda i, w, e: (0, 0, 0), pipeline_mode=one),
             pl.BlockSpec((512, 512), lambda i, w, e: (0, 0), pipeline_mode=one),
             pl.BlockSpec(memory_space=pltpu.SMEM),
+            pl.BlockSpec(memory_space=pltpu.SMEM),
         ],
-        out_specs=pl.BlockSpec((3, OUT_ROWS, COLS), lambda i, w, e: (0, 0, 0), pipeline_mode=one),
+        out_specs=pl.BlockSpec((3, 8, 4, COLS), lambda i, w, e: (0, 0, 0, 0), pipeline_mode=one),
         scratch_shapes=[
+            pltpu.VMEM((2, 2, 128, 256), jnp.bfloat16),
+            pltpu.VMEM((2, 4, 32, LANES), jnp.float32),
             pltpu.VMEM((640, COLS), jnp.float32),
             pltpu.VMEM((128, COLS), jnp.float32),
             pltpu.VMEM((2, 256, CHUNK), jnp.bfloat16),
@@ -328,64 +354,299 @@
     return pl.pallas_call(
         kernel,
         grid_spec=spec,
-        out_shape=jax.ShapeDtypeStruct((3, OUT_ROWS, COLS), jnp.float32),
+        out_shape=jax.ShapeDtypeStruct((3, 8, 4, COLS), jnp.float32),
         compiler_params=pltpu.CompilerParams(vmem_limit_bytes=48 * 2**20),
         cost_estimate=pl.CostEstimate(flops=20 * 10**9, bytes_accessed=20 * 10**6, transcendentals=0),
     )(
-        where, edges, tmpl, strain, strain, jnp.asarray(bands), net_tables, jnp.asarray(twiddle), ramp,
-        jnp.asarray(inner), jnp.asarray(last), jnp.asarray(place), response,
+        where, edges, tmpl, strain, strain, jnp.asarray(bands), jnp.asarray(twiddle),
+        jnp.asarray(inner), jnp.asarray(last), jnp.asarray(place), slides, antenna,
     )
 
-
-def dynamic_tables(part, det, slides_mine, antenna):
-    tau = jnp.arange(OUT_ROWS, dtype=jnp.int32)
-    e = 4 * tau + part if SPACED else 32 * part + tau
-    b = jnp.arange(FOLD, dtype=jnp.int32)
-    a = jnp.arange(COLS, dtype=jnp.int32)
-
-    def unit(index, total):
-        angle = (index % total).astype(jnp.float32) * (2.0 * math.pi / total)
-        return jnp.cos(angle), jnp.sin(angle)
-
-    tables, ramps = [], []
-    for which in (det, 1 - det):
-        moving = which == 1
-        weight_re, weight_im = antenna[which, 0], antenna[which, 1]
-        rows, cols = [], []
-        for slide in range(2):
-            shift = jnp.where(moving, slides_mine[slide], 0)
-            cos, sin = unit((e[:, None] + shift % FOLD) * b[None, :], FOLD)
-            re = weight_re * cos - weight_im * sin
-            im = weight_re * sin + weight_im * cos
-            rows.append(stacked_rows(re, im, jnp))
-            cols.append(jnp.stack(unit(a * shift, BINS)))
-        table = jnp.concatenate(rows, axis=0)
-        high = lax.reduce_precision(table, 8, 7)
-        tables.append(jnp.stack([high.astype(jnp.bfloat16), (table - high).astype(jnp.bfloat16)]))
-        ramps.append(jnp.stack(cols))
-    return jnp.stack(tables), jnp.concatenate(ramps, axis=1)
+MESH = pl.DeviceIdType.MESH
+HALF = COLS // 2
+PORTIONS = ((0, 640), (640, 640), (1280, 768))
+ORDERS = (("x", "y", "z"), ("y", "z", "x"), ("z", "x", "y"))
+
+
+def gather_kernel(
+    assign, bank, strain, tmpl, signal, everything, staged,
+    local_sem, swap_send, swap_recv, wide_send, wide_recv, pass_send, pass_recv,
+    far_send, far_recv, near_send, near_recv,
+):
+    det, grp, tm = lax.axis_index("det"), lax.axis_index("grp"), lax.axis_index("tm")
+    here = {"y": tm // 8, "z": det * 2 + (tm // 4) % 2, "x": tm % 4}
+    peer = {"grp": 1 - grp}
+    half = pl.ds(pl.multiple_of(grp * HALF, HALF), HALF)
+    other = pl.ds(pl.multiple_of((1 - grp) * HALF, HALF), HALF)
+
+    def moved(axis, by):
+        there = dict(here)
+        there[axis] = (here[axis] + by + 4) % 4
+        return there
+
+    def tm_of(place):
+        return place["y"] * 8 + (place["z"] % 2) * 4 + place["x"]
+
+    def ident(place):
+        return {"det": place["z"] // 2, "tm": tm_of(place)}
+
+    def shifted(d):
+        dy, dz, dx = d // 8, (d // 4) % 2, d % 4
+        y, z, x = here["y"], here["z"] % 2, here["x"]
+        to = ((y + dy) % 4) * 8 + ((z + dz) % 2) * 4 + (x + dx) % 4
+        back = ((y - dy + 4) % 4) * 8 + ((z - dz + 2) % 2) * 4 + (x - dx + 4) % 4
+        return to, back
+
+    barrier = pltpu.get_barrier_semaphore()
+
+    def greet(d, carry):
+        pl.semaphore_signal(barrier, inc=1, device_id={"tm": shifted(d)[0]}, device_id_type=MESH)
+        return carry
+
+    lax.fori_loop(1, 32, greet, 0)
+    for z in range(2):
+        place = dict(here)
+        place["z"] = (1 - det) * 2 + z
+        pl.semaphore_signal(barrier, inc=1, device_id=ident(place), device_id_type=MESH)
+    pl.semaphore_signal(barrier, inc=1, device_id=peer, device_id_type=MESH)
+    pl.semaphore_wait(barrier, 34)
+
+    def remote(src, dst, send, recv, device):
+        return pltpu.make_async_remote_copy(
+            src_ref=src, dst_ref=dst, send_sem=send, recv_sem=recv, device_id=device, device_id_type=MESH
+        )
+
+    swap = remote(bank.at[:, :, other], everything.at[pl.ds(grp * 8, 8)], swap_send, swap_recv, peer)
+    swap.start()
+    keep = pltpu.make_async_copy(bank.at[:, :, half], everything.at[pl.ds(grp * 8, 8)], local_sem.at[0])
+    keep.start()
+    own = pltpu.make_async_copy(
+        strain, signal.at[det, here["y"], here["z"] % 2, here["x"]], local_sem.at[1]
+    )
+    own.start()
+
+    def columns(portion, core):
+        first, width = PORTIONS[portion]
+        return pl.ds(pl.multiple_of(core * HALF + first, LANES), width)
+
+    def region(portion, stage, place, core):
+        done = ORDERS[portion][:stage]
+        every = lambda axis, value, size: pl.ds(0, size) if axis in done else value
+        return signal.at[
+            every("z", place["z"] // 2, 2), every("y", place["y"], 4), every("z", place["z"] % 2, 2),
+            every("x", place["x"], 4), :, columns(portion, core),
+        ]
+
+    def wide(portion, stage, d):
+        axis = ORDERS[portion][stage]
+        dst = region(portion, stage, here, grp)
+        src = strain.at[:, columns(portion, grp)] if stage == 0 else dst
+        at = (portion, stage, d - 1)
+        return remote(src, dst, wide_send.at[at], wide_recv.at[at], ident(moved(axis, d)))
+
+    def arrived(portion, stage, d):
+        axis = ORDERS[portion][stage]
+        at = (portion, stage, d - 1)
+        got = region(portion, stage, moved(axis, -d), grp)
+        remote(got, got, wide_send.at[at], wide_recv.at[at], peer).wait_recv()
+        remote(got, got, pass_send.at[at], pass_recv.at[at], peer).start()
+
+    for portion in range(3):
+        for d in (1, 3, 2):
+            wide(portion, 0, d).start()
+
+    swap.wait_recv()
+    keep.wait()
+    for slot in range(16):
+        staged[slot] = everything[assign[slot]]
+
+    def far(d):
+        to, back = shifted(d)
+        return remote(
+            staged.at[to % 16], tmpl.at[tm, :, half], far_send.at[d], far_recv.at[d], {"tm": to}
+        ), back
+
+    def send_far(d, carry):
+        far(d)[0].start()
+        return carry
+
+    lax.fori_loop(1, 32, send_far, 0)
+    mine = pltpu.make_async_copy(staged.at[tm % 16], tmpl.at[tm, :, half], local_sem.at[2])
+    mine.start()
+    remote(staged.at[tm % 16], tmpl.at[tm, :, half], near_send.at[0], near_recv.at[0], peer).start()
+
+    own.wait()
+    for stage in range(3):
+        for portion in range(3):
+            for d in (1, 3, 2):
+                arrived(portion, stage, d)
+            if stage < 2:
+                for d in (1, 3, 2):
+                    wide(portion, stage + 1, d).start()
+        if stage == 1:
+
+            def got_far(d, carry):
+                copy, back = far(d)
+                got = tmpl.at[back, :, half]
+                remote(got, got, far_send.at[d], far_recv.at[d], peer).wait_recv()
+                remote(got, got, near_send.at[d], near_recv.at[d], peer).start()
+                return carry
+
+            lax.fori_loop(1, 32, got_far, 0)
+
+    mine.wait()
+    swap.wait_send()
+    for stage in range(3):
+        for portion in range(3):
+            for d in (1, 3, 2):
+                wide(portion, stage, d).wait_send()
+                at = (portion, stage, d - 1)
+                place = moved(ORDERS[portion][stage], -d)
+                got = region(portion, stage, place, grp)
+                remote(got, got, pass_send.at[at], pass_recv.at[at], peer).wait_send()
+                come = region(portion, stage, place, 1 - grp)
+                remote(come, come, pass_send.at[at], pass_recv.at[at], peer).wait_recv()
+
+    def rest(d, carry):
+        copy, back = far(d)
+        piece = tmpl.at[back, :, other]
+        near = remote(piece, piece, near_send.at[d], near_recv.at[d], peer)
+        near.wait_recv()
+        near.wait_send()
+
+        @pl.when(d > 0)
+        def _():
+            copy.wait_send()
+
+        return carry
+
+    lax.fori_loop(0, 32, rest, 0)
+
+
+def gather(assignment, bank, strain):
+    dma = pltpu.SemaphoreType.DMA
+    return pl.pallas_call(
+        gather_kernel,
+        out_shape=(
+            jax.ShapeDtypeStruct((32, 8, COLS), jnp.float32),
+            jax.ShapeDtypeStruct((2, 4, 2, 4, 8, COLS), jnp.float32),
+        ),
+        in_specs=[
+            pl.BlockSpec(memory_space=pltpu.SMEM),
+            pl.BlockSpec(memory_space=pl.ANY),
+            pl.BlockSpec(memory_space=pl.ANY),
+        ],
+        out_specs=[pl.BlockSpec(memory_space=pl.ANY), pl.BlockSpec(memory_space=pl.ANY)],
+        scratch_shapes=[
+            pltpu.VMEM((16, 8, HALF), jnp.float32),
+            pltpu.VMEM((16, 8, HALF), jnp.float32),
+            dma((3,)), dma, dma, dma((3, 3, 3)), dma((3, 3, 3)), dma((3, 3, 3)), dma((3, 3, 3)),
+            dma((32,)), dma((32,)), dma((32,)), dma((32,)),
+        ],
+        compiler_params=pltpu.CompilerParams(collective_id=0, has_side_effects=True),
+    )(assignment, bank, strain)
+
+
+def scatter_kernel(rows, chi, net, send, recv):
+    grp, tm = lax.axis_index("grp"), lax.axis_index("tm")
+    slot = tm % 16
+    to_grp = slot // 8
+    at = slot % 8
+    part = 2 * (tm // 16) + grp
+    from_part = tm // 8
+    from_grp = from_part % 2
+    self_too = (tm // 8) % 2 == grp
+    barrier = pltpu.get_barrier_semaphore()
+
+    def target(i):
+        return 8 * part + (tm + i) % 8
+
+    def source(k):
+        return 8 * grp + k + 16 * (from_part // 2)
+
+    def greet(i, carry):
+        for device, group in ((target(i), to_grp), (source(i), from_grp)):
+            @pl.when(jnp.logical_not((device == tm) & (group == grp)))
+            def _():
+                pl.semaphore_signal(
+                    barrier, inc=1, device_id={"grp": group, "tm": device}, device_id_type=MESH
+                )
+        return carry
+
+    lax.fori_loop(0, 8, greet, 0)
+
+    @pl.when(self_too)
+    def _():
+        pl.semaphore_wait(barrier, 14)
+
+    @pl.when(jnp.logical_not(self_too))
+    def _():
+        pl.semaphore_wait(barrier, 16)
+
+    def parts(i):
+        piece = target(i) % 8
+        return ((rows.at[0, piece], chi.at[at]), (rows.at[pl.ds(1, 2), piece], net.at[at]))
+
+    def copy(i, kind):
+        src, dst = parts(i)[kind]
+        return pltpu.make_async_remote_copy(
+            src_ref=src, dst_ref=dst, send_sem=send.at[kind, i], recv_sem=recv.at[kind, at],
+            device_id={"grp": to_grp, "tm": target(i)}, device_id_type=MESH,
+        )
+
+    def start(i, carry):
+        is_self = (target(i) == tm) & (to_grp == grp)
+        for kind in range(2):
+            @pl.when(is_self)
+            def _():
+                src, dst = parts(i)[kind]
+                pltpu.make_async_copy(src, dst, recv.at[kind, at]).start()
+
+            @pl.when(jnp.logical_not(is_self))
+            def _():
+                copy(i, kind).start()
+        return carry
+
+    lax.fori_loop(0, 8, start, 0)
+
+    def finish(i, carry):
+        is_self = (target(i) == tm) & (to_grp == grp)
+
+        for kind, dst in ((0, chi), (1, net)):
+            pltpu.make_async_copy(dst.at[i], dst.at[i], recv.at[kind, i]).wait()
+
+            @pl.when(jnp.logical_not(is_self))
+            def _():
+                copy(i, kind).wait_send()
+        return carry
+
+    lax.fori_loop(0, 8, finish, 0)
+
+
+def scatter(rows):
+    dma = pltpu.SemaphoreType.DMA
+    return pl.pallas_call(
+        scatter_kernel,
+        out_shape=(
+            jax.ShapeDtypeStruct((8, 4, COLS), jnp.float32),
+            jax.ShapeDtypeStruct((8, 2, 4, COLS), jnp.float32),
+        ),
+        in_specs=[pl.BlockSpec(memory_space=pl.ANY)],
+        out_specs=[pl.BlockSpec(memory_space=pl.ANY), pl.BlockSpec(memory_space=pl.ANY)],
+        scratch_shapes=[dma((2, 8)), dma((2, 8))],
+        compiler_params=pltpu.CompilerParams(collective_id=1, has_side_effects=True),
+    )(rows)
 
 
 def on_device(strain, bank, assignment, slides, bounds, antenna):
     tm = lax.axis_index("tm")
     det = lax.axis_index("det")
     grp = lax.axis_index("grp")
-    packed = bank.reshape(8, 8, COLS)
-    both = lax.all_gather(packed, "grp", axis=0, tiled=True)
-    mine = lax.dynamic_slice_in_dim(assignment, grp * 8, 8)
-    chosen = jnp.take(both, jnp.repeat(mine, 4), axis=0)
-    tmpl = lax.all_to_all(chosen, "tm", split_axis=0, concat_axis=0, tiled=True)
-    signal = lax.all_gather(strain.reshape(8, COLS), ("det", "tm"), axis=0, tiled=False)
-    part = tm % 4
-    mine = lax.dynamic_slice_in_dim(slides, det * 2, 2)
-    net_tables, ramp = dynamic_tables(part, det, mine, antenna)
-    rows = filter_rows(
-        part, det, tmpl.reshape(256, COLS), signal.reshape(2, 256, COLS), bounds, net_tables, ramp,
-        jnp.sum(antenna * antenna)[None],
-    )
-    sent = lax.all_to_all(jnp.swapaxes(rows, 0, 1), "tm", split_axis=0, concat_axis=0, tiled=True)
-    sent = sent.reshape(8, 4, 3, COLS)
-    return sent[None, :, :, 0], jnp.swapaxes(sent[:, :, 1:], 1, 2)
+    tmpl, signal = gather(assignment, bank.reshape(8, 8, COLS), strain.reshape(8, COLS))
+    part = 2 * (tm // 16) + grp
+    rows = filter_rows(part, det, tmpl.reshape(256, COLS), signal.reshape(2, 256, COLS), bounds, slides, antenna)
+    chi, net = scatter(rows)
+    return chi[None], net
 
 
 def solution(mesh):

time: 453 us -> 144 us (0.32)
  the two profiles are of different devices: /device:TPU:0 before, /device:TPU:1 now
where the time goes in v2:
time: 144 us; the launch traced here: 143 us
  Pallas kernels  126 us (88%)
  local copies, waits for them, and re-layouts  15.1 us (10%)
    pallas_call x1, Pallas kernels, gather(): pl.pallas_call(gather_kernel, out_shape=(jax.ShapeDtypeStruct((32, 8, COL...  71.8 us
    pallas_call x1, Pallas kernels, scatter(): pl.pallas_call(scatter_kernel, out_shape=(jax.ShapeDtypeStruct((8, 4, COL...  27.3 us
    pallas_call x1, Pallas kernels, filter_rows(): pl.pallas_call(kernel, grid_spec=spec, out_shape=jax.ShapeDtypeStruct((3,...  27.1 us
    unnamed x16, local copies, waits for them, and re-layouts  11 us

profile of v2, /device:TPU:1, one launch (start us, length us, event | category | flops | bytes accessed | tf_op | source)
XLA Modules:
  0.0 142.9 jit_solution(3046327419975666845)
XLA Ops:
  0.6 0.1 pad_add_fusion.where_ref
  0.7 0.7 pad_add_fusion.1.bounds_ref
  1.5 1.6 %reshape.17.strain = f32[8,4096]{1,0:T(8,128)} reshape(f32[1,2,4,4096]{3,2,1,0:T(4,128)} %param.11) | data formatting | bytes 262144 | tf_op jit(solution)/shard_map/reshape | solution.py:645
  3.1 2.6 %reshape.16.bank = f32[8,8,4096]{2,1,0:T(8,128)} reshape(f32[8,2,4,4096]{3,2,1,0:T(4,128)} %param.12) | data formatting | bytes 2097152 | tf_op jit(solution)/shard_map/reshape | solution.py:645
  5.6 71.8 %shard_map.122 = (f32[32,8,4096]{2,1,0:T(8,128)}, f32[2,4,2,4,8,4096]{5,4,3,2,1,0:T(8,128)}) custom-call(s32[16]{0:T(128)} %assign.1, f32[8,8,4096]{2,1,0:T(8,128)} %reshape.16.bank, f32[8,4096]{1,0:T(8,128)} %reshape.17.strain), custom_call_target="tpu_custom_call" | custom-call | tf_op jit(solution)/shard_map/pallas_call | solution.py:528
  77.4 0.0 copy-start.1
  77.4 0.7 copy-done.1
  78.1 0.0 copy-start.2
  78.1 0.7 copy-done.2
  78.8 0.0 copy-start.3
  78.8 1.6 %copy-done.3 = bf16[4,4,256,256]{3,2,1,0:T(8,128)(2,1)S(1)} copy-done((bf16[4,4,256,256]{3,2,1,0:T(8,128)(2,1)S(1)}, bf16[4,4,256,256]{3,2,1,0:T(8,128)(2,1)}, u32[]{:S(2)}) %copy-start.3) | copy-done | bytes 2097176
  80.4 0.0 copy-start.4
  80.4 1.0 copy-done.4
  81.4 0.0 copy-start.5
  81.4 0.9 copy-done.5
  82.4 0.0 copy-start.6
  82.4 0.8 copy-done.6
  83.1 27.1 %shard_map.123.rows = f32[3,8,4,4096]{3,2,1,0:T(4,128)S(1)} custom-call(s32[2]{0:T(128)S(1)} %pad_add_fusion.where_ref, s32[9]{0:T(128)S(1)} %pad_add_fusion.1.bounds_ref, f32[256,4096]{1,0:T(8,128)} %bitcast.8, f32[2,256,4096]{2,1,0:T(8,128)} %bitcast.6, f32[2,256,4096]{2,1,0:T(8,128)} %bitcast.7, bf16[4,4,256,256]{3,2,1,0:T(8,128)(2,1)S(1)} %copy-done.3, ...), custom_call_target="tpu_custom_call" | custom-call | flops 20000000000 | bytes 20000000 | tf_op jit(solution)/shard_map/pallas_call | solution.py:354
  110.2 0.0 copy-start
  110.2 1.1 copy-done
  111.4 27.3 %shard_map.124 = (f32[8,4,4096]{2,1,0:T(4,128)}, f32[8,2,4,4096]{3,2,1,0:T(4,128)}) custom-call(f32[3,8,4,4096]{3,2,1,0:T(4,128)} %copy-done), custom_call_target="tpu_custom_call" | custom-call | tf_op jit(solution)/shard_map/pallas_call | solution.py:628
  138.7 1.9 %copy.15 = f32[1,8,4,4096]{3,2,1,0:T(4,128)} copy(f32[1,8,4,4096]{3,2,1,0:T(4,128)} %bitcast.5) | data formatting | bytes 1048576
  140.6 2.3 %copy.16 = f32[8,2,4,4096]{3,2,1,0:T(4,128)} copy(f32[8,2,4,4096]{3,2,1,0:T(4,128)} %get-tuple-element.13) | data formatting | bytes 2097152
Async XLA Ops:
  77.4 0.7 copy-start.1
  78.1 0.7 copy-start.2
  78.8 1.6 %copy-start.3 = (bf16[4,4,256,256]{3,2,1,0:T(8,128)(2,1)S(1)}, bf16[4,4,256,256]{3,2,1,0:T(8,128)(2,1)}, u32[]{:S(2)}) copy-start(bf16[4,4,256,256]{3,2,1,0:T(8,128)(2,1)} %constant.45.clone.bands_ref) | copy-start | bytes 6291460
  80.4 1.0 copy-start.4
  81.4 0.9 copy-start.5
  82.4 0.8 copy-start.6
  110.2 1.1 copy-start

commit v3 on v2

--- a/solution.py
+++ b/solution.py
@@ -19,7 +19,7 @@
 
 def rows_of(part):
     tau = np.arange(OUT_ROWS)
-    return OUT_ROWS * part + tau
+    return 64 * (part % 2) + 32 * (tau // 16) + 16 * (part // 2) + tau % 16
 
 
 def halves(table):
@@ -146,22 +146,37 @@
 
 
 def kernel(
-    where_ref, bounds_ref, tmpl_ref, own_ref, oth_ref, bands_ref, twiddle_ref,
-    inner_ref, last_ref, place_ref, slides_ref, antenna_ref, out_ref,
+    where_ref, bounds_ref, tmpl_ref, own_ref, oth_ref, bands_hbm, twiddle_hbm,
+    inner_hbm, last_hbm, place_hbm, slides_ref, antenna_ref, out_ref,
+    bands_ref, twiddle_ref, inner_ref, last_ref, place_ref, table_sem,
     net_ref, ramp_ref, series, net_oth, xe, xo, xn, power, zbuf, bbuf, vbuf,
 ):
     step = pl.program_id(0)
     start = step * CHUNK
 
+    tables = [
+        pltpu.make_async_copy(src, dst, table_sem.at[i])
+        for i, (src, dst) in enumerate((
+            (bands_hbm.at[where_ref[0]], bands_ref.at[0]),
+            (twiddle_hbm.at[where_ref[0]], twiddle_ref.at[0]),
+            (inner_hbm, inner_ref),
+            (last_hbm, last_ref),
+            (place_hbm, place_ref),
+        ))
+    ]
+
     @pl.when(step == 0)
     def _():
+        for copy in tables:
+            copy.start()
         power[...] = jnp.zeros_like(power)
         part, det = where_ref[0], where_ref[1]
         column = (
             lax.broadcasted_iota(jnp.int32, (32, LANES), 0) * LANES
             + lax.broadcasted_iota(jnp.int32, (32, LANES), 1)
         )
-        row = lax.broadcasted_iota(jnp.int32, (OUT_ROWS, 256), 0) + OUT_ROWS * part
+        tau = lax.broadcasted_iota(jnp.int32, (OUT_ROWS, 256), 0)
+        row = 64 * (part & 1) + 32 * (tau >> 4) + 16 * (part >> 1) + (tau & 15)
         packed = lax.broadcasted_iota(jnp.int32, (OUT_ROWS, 256), 1)
         bin_row = (packed >> 3) * 4 + (packed & 3)
         quarter = ((packed >> 2) & 1) * (FOLD // 4)
@@ -215,6 +230,11 @@
         xn[0, rows, :] = high
         xn[1, rows, :] = low
     cols = pl.ds(pl.multiple_of(start, CHUNK), CHUNK)
+
+    @pl.when(step == 0)
+    def _():
+        for copy in tables:
+            copy.wait()
 
     def three(high, low, x):
         return mm(high, x[0]) + mm(low, x[0]) + mm(high, x[1])
@@ -328,16 +348,18 @@
             pl.BlockSpec((256, CHUNK), lambda i, w, e: (0, i)),
             pl.BlockSpec((1, 256, CHUNK), lambda i, w, e: (w[1], 0, i)),
             pl.BlockSpec((1, 256, CHUNK), lambda i, w, e: (1 - w[1], 0, i)),
-            pl.BlockSpec((1, 4, 256, 256), lambda i, w, e: (w[0], 0, 0, 0), pipeline_mode=one),
-            pl.BlockSpec((1, 2, OUT_ROWS, COLS), lambda i, w, e: (w[0], 0, 0, 0), pipeline_mode=one),
-            pl.BlockSpec((2, 32, LANES), lambda i, w, e: (0, 0, 0), pipeline_mode=one),
-            pl.BlockSpec((2, 256, 256), lambda i, w, e: (0, 0, 0), pipeline_mode=one),
-            pl.BlockSpec((512, 512), lambda i, w, e: (0, 0), pipeline_mode=one),
+            *[pl.BlockSpec(memory_space=pltpu.HBM)] * 5,
             pl.BlockSpec(memory_space=pltpu.SMEM),
             pl.BlockSpec(memory_space=pltpu.SMEM),
         ],
         out_specs=pl.BlockSpec((3, 8, 4, COLS), lambda i, w, e: (0, 0, 0, 0), pipeline_mode=one),
         scratch_shapes=[
+            pltpu.VMEM((1, 4, 256, 256), jnp.bfloat16),
+            pltpu.VMEM((1, 2, OUT_ROWS, COLS), jnp.float32),
+            pltpu.VMEM((2, 32, LANES), jnp.float32),
+            pltpu.VMEM((2, 256, 256), jnp.bfloat16),
+            pltpu.VMEM((512, 512), jnp.bfloat16),
+            pltpu.SemaphoreType.DMA((5,)),
             pltpu.VMEM((2, 2, 128, 256), jnp.bfloat16),
             pltpu.VMEM((2, 4, 32, LANES), jnp.float32),
             pltpu.VMEM((640, COLS), jnp.float32),
@@ -369,12 +391,13 @@
 
 
 def gather_kernel(
-    assign, bank, strain, tmpl, signal, everything, staged,
+    assign, bank, strain, tmpl, signal, everything, staged, loaded, packed,
     local_sem, swap_send, swap_recv, wide_send, wide_recv, pass_send, pass_recv,
-    far_send, far_recv, near_send, near_recv,
+    far_send, far_recv, deep_send, deep_recv, near_send, near_recv,
 ):
     det, grp, tm = lax.axis_index("det"), lax.axis_index("grp"), lax.axis_index("tm")
-    here = {"y": tm // 8, "z": det * 2 + (tm // 4) % 2, "x": tm % 4}
+    low_z = (tm // 4) % 2
+    here = {"y": tm // 8, "z": det * 2 + low_z, "x": tm % 4}
     peer = {"grp": 1 - grp}
     half = pl.ds(pl.multiple_of(grp * HALF, HALF), HALF)
     other = pl.ds(pl.multiple_of((1 - grp) * HALF, HALF), HALF)
@@ -384,143 +407,199 @@
         there[axis] = (here[axis] + by + 4) % 4
         return there
 
-    def tm_of(place):
-        return place["y"] * 8 + (place["z"] % 2) * 4 + place["x"]
-
     def ident(place):
-        return {"det": place["z"] // 2, "tm": tm_of(place)}
-
-    def shifted(d):
-        dy, dz, dx = d // 8, (d // 4) % 2, d % 4
-        y, z, x = here["y"], here["z"] % 2, here["x"]
-        to = ((y + dy) % 4) * 8 + ((z + dz) % 2) * 4 + (x + dx) % 4
-        back = ((y - dy + 4) % 4) * 8 + ((z - dz + 2) % 2) * 4 + (x - dx + 4) % 4
-        return to, back
+        return {"det": place["z"] // 2, "tm": place["y"] * 8 + (place["z"] % 2) * 4 + place["x"]}
+
+    def shifted(d, sign=1):
+        there = dict(here)
+        there["y"] = (here["y"] + sign * (d // 4) + 4) % 4
+        there["x"] = (here["x"] + sign * (d % 4) + 4) % 4
+        return there
+
+    keep = pltpu.make_async_copy(bank.at[:, :, :, half], everything.at[pl.ds(grp * 8, 8)], local_sem.at[0])
+    keep.start()
+    own = pltpu.make_async_copy(strain, loaded, local_sem.at[1])
+    own.start()
 
     barrier = pltpu.get_barrier_semaphore()
 
     def greet(d, carry):
-        pl.semaphore_signal(barrier, inc=1, device_id={"tm": shifted(d)[0]}, device_id_type=MESH)
+        pl.semaphore_signal(barrier, inc=1, device_id=ident(shifted(d)), device_id_type=MESH)
         return carry
 
-    lax.fori_loop(1, 32, greet, 0)
-    for z in range(2):
-        place = dict(here)
-        place["z"] = (1 - det) * 2 + z
-        pl.semaphore_signal(barrier, inc=1, device_id=ident(place), device_id_type=MESH)
+    lax.fori_loop(1, 16, greet, 0)
+    for d in (1, 2, 3):
+        pl.semaphore_signal(barrier, inc=1, device_id=ident(moved("z", d)), device_id_type=MESH)
     pl.semaphore_signal(barrier, inc=1, device_id=peer, device_id_type=MESH)
-    pl.semaphore_wait(barrier, 34)
+    pl.semaphore_wait(barrier, 19)
 
     def remote(src, dst, send, recv, device):
         return pltpu.make_async_remote_copy(
             src_ref=src, dst_ref=dst, send_sem=send, recv_sem=recv, device_id=device, device_id_type=MESH
         )
 
-    swap = remote(bank.at[:, :, other], everything.at[pl.ds(grp * 8, 8)], swap_send, swap_recv, peer)
+    swap = remote(bank.at[:, :, :, other], everything.at[pl.ds(grp * 8, 8)], swap_send, swap_recv, peer)
     swap.start()
-    keep = pltpu.make_async_copy(bank.at[:, :, half], everything.at[pl.ds(grp * 8, 8)], local_sem.at[0])
-    keep.start()
-    own = pltpu.make_async_copy(
-        strain, signal.at[det, here["y"], here["z"] % 2, here["x"]], local_sem.at[1]
-    )
-    own.start()
 
     def columns(portion, core):
         first, width = PORTIONS[portion]
         return pl.ds(pl.multiple_of(core * HALF + first, LANES), width)
 
-    def region(portion, stage, place, core):
+    def region(portion, stage, place, core, part=None):
         done = ORDERS[portion][:stage]
-        every = lambda axis, value, size: pl.ds(0, size) if axis in done else value
+        cut = "x" if ORDERS[portion][2] == "y" else "y"
+
+        def every(axis, value, size):
+            if axis not in done:
+                return value
+            if part is not None and axis == cut:
+                return pl.ds(2 * part, 2)
+            return pl.ds(0, size)
+
         return signal.at[
             every("z", place["z"] // 2, 2), every("y", place["y"], 4), every("z", place["z"] % 2, 2),
             every("x", place["x"], 4), :, columns(portion, core),
         ]
 
     def wide(portion, stage, d):
-        axis = ORDERS[portion][stage]
         dst = region(portion, stage, here, grp)
-        src = strain.at[:, columns(portion, grp)] if stage == 0 else dst
+        src = packed.at[:, columns(portion, grp)] if stage == 0 else dst
         at = (portion, stage, d - 1)
-        return remote(src, dst, wide_send.at[at], wide_recv.at[at], ident(moved(axis, d)))
+        return remote(src, dst, wide_send.at[at], wide_recv.at[at], ident(moved(ORDERS[portion][stage], d)))
+
+    def relay(portion, part):
+        axis = ORDERS[portion][2]
+        got = region(portion, 2, moved(axis, -1 if part == 0 else 1), grp, part)
+        at = (portion, 2 + part, 1)
+        return remote(got, got, wide_send.at[at], wide_recv.at[at], ident(moved(axis, 1 if part == 0 else -1)))
+
+    def incoming(portion, stage, d, core):
+        axis = ORDERS[portion][min(stage, 2)]
+        if stage < 2 or d != 2:
+            part = None
+        else:
+            part = stage - 2
+        return region(portion, min(stage, 2), moved(axis, -d), core, part), (portion, stage, d - 1)
 
     def arrived(portion, stage, d):
-        axis = ORDERS[portion][stage]
-        at = (portion, stage, d - 1)
-        got = region(portion, stage, moved(axis, -d), grp)
+        got, at = incoming(portion, stage, d, grp)
         remote(got, got, wide_send.at[at], wide_recv.at[at], peer).wait_recv()
         remote(got, got, pass_send.at[at], pass_recv.at[at], peer).start()
 
+    own.wait()
+    packed[0:4, :] = loaded[0, 0]
+    packed[4:8, :] = loaded[0, 1]
     for portion in range(3):
         for d in (1, 3, 2):
             wide(portion, 0, d).start()
+    mine = pltpu.make_async_copy(packed, signal.at[det, here["y"], low_z, here["x"]], local_sem.at[1])
+    mine.start()
 
     swap.wait_recv()
     keep.wait()
     for slot in range(16):
-        staged[slot] = everything[assign[slot]]
+        wave = everything[assign[slot]]
+        staged[slot, 0:4, :] = wave[0]
+        staged[slot, 4:8, :] = wave[1]
 
     def far(d):
-        to, back = shifted(d)
+        to = shifted(d)
         return remote(
-            staged.at[to % 16], tmpl.at[tm, :, half], far_send.at[d], far_recv.at[d], {"tm": to}
-        ), back
+            staged.at[to["y"] * 4 + to["x"]], tmpl.at[here["y"], low_z, here["x"], :, half],
+            far_send.at[d], far_recv.at[d], ident(to),
+        )
+
+    def piece(place, plane, columns):
+        return tmpl.at[place["y"], plane, place["x"], :, columns]
+
+    def deep(place):
+        got = piece(place, low_z, half)
+        at = place["y"] * 4 + place["x"]
+        to = moved("z", jnp.where(place["y"] < 2, 1, 3))
+        return remote(got, got, deep_send.at[at], deep_recv.at[at], ident(to))
+
+    def near(place, plane, columns):
+        got = piece(place, plane, columns)
+        at = (plane, place["y"] * 4 + place["x"])
+        return remote(got, got, near_send.at[at], near_recv.at[at], peer)
 
     def send_far(d, carry):
-        far(d)[0].start()
+        far(d).start()
         return carry
 
-    lax.fori_loop(1, 32, send_far, 0)
-    mine = pltpu.make_async_copy(staged.at[tm % 16], tmpl.at[tm, :, half], local_sem.at[2])
-    mine.start()
-    remote(staged.at[tm % 16], tmpl.at[tm, :, half], near_send.at[0], near_recv.at[0], peer).start()
-
-    own.wait()
-    for stage in range(3):
-        for portion in range(3):
-            for d in (1, 3, 2):
-                arrived(portion, stage, d)
-            if stage < 2:
-                for d in (1, 3, 2):
-                    wide(portion, stage + 1, d).start()
-        if stage == 1:
-
-            def got_far(d, carry):
-                copy, back = far(d)
-                got = tmpl.at[back, :, half]
-                remote(got, got, far_send.at[d], far_recv.at[d], peer).wait_recv()
-                remote(got, got, near_send.at[d], near_recv.at[d], peer).start()
-                return carry
-
-            lax.fori_loop(1, 32, got_far, 0)
+    lax.fori_loop(1, 16, send_far, 0)
+    slot_here = here["y"] * 4 + here["x"]
+    kept = pltpu.make_async_copy(staged.at[slot_here], piece(here, low_z, half), local_sem.at[2])
+    kept.start()
 
     mine.wait()
+    for portion in range(3):
+        for d in (1, 3, 2):
+            arrived(portion, 0, d)
+        for d in (1, 3, 2):
+            wide(portion, 1, d).start()
+    kept.wait()
+    deep(here).start()
+    near(here, low_z, half).start()
+
+    def got_far(d, carry):
+        place = shifted(d, -1)
+        got = piece(place, low_z, half)
+        remote(got, got, far_send.at[d], far_recv.at[d], peer).wait_recv()
+        deep(place).start()
+        near(place, low_z, half).start()
+        return carry
+
+    lax.fori_loop(1, 16, got_far, 0)
+    for portion in range(3):
+        for d in (1, 3, 2):
+            arrived(portion, 1, d)
+        for d in (1, 3):
+            wide(portion, 2, d).start()
+
+    def place_at(p):
+        return {"y": p // 4, "x": p % 4}
+
+    def got_deep(p, carry):
+        got = piece(place_at(p), 1 - low_z, half)
+        remote(got, got, deep_send.at[p], deep_recv.at[p], peer).wait_recv()
+        near(place_at(p), 1 - low_z, half).start()
+        return carry
+
+    lax.fori_loop(0, 16, got_deep, 0)
+    for portion in range(3):
+        for d, part in ((1, 0), (3, 1)):
+            arrived(portion, 2, d)
+            relay(portion, part).start()
+    for portion in range(3):
+        for part in range(2):
+            arrived(portion, 2 + part, 2)
+
     swap.wait_send()
-    for stage in range(3):
-        for portion in range(3):
-            for d in (1, 3, 2):
+
+    def rest(p, carry):
+        deep(place_at(p)).wait_send()
+        for plane in range(2):
+            near(place_at(p), plane, half).wait_send()
+            near(place_at(p), plane, other).wait_recv()
+
+        @pl.when(p > 0)
+        def _():
+            far(p).wait_send()
+
+        return carry
+
+    lax.fori_loop(0, 16, rest, 0)
+    for portion in range(3):
+        for stage, d in ((0, 1), (0, 2), (0, 3), (1, 1), (1, 2), (1, 3), (2, 1), (2, 3), (2, 2), (3, 2)):
+            if stage < 2 or d != 2:
                 wide(portion, stage, d).wait_send()
-                at = (portion, stage, d - 1)
-                place = moved(ORDERS[portion][stage], -d)
-                got = region(portion, stage, place, grp)
-                remote(got, got, pass_send.at[at], pass_recv.at[at], peer).wait_send()
-                come = region(portion, stage, place, 1 - grp)
-                remote(come, come, pass_send.at[at], pass_recv.at[at], peer).wait_recv()
-
-    def rest(d, carry):
-        copy, back = far(d)
-        piece = tmpl.at[back, :, other]
-        near = remote(piece, piece, near_send.at[d], near_recv.at[d], peer)
-        near.wait_recv()
-        near.wait_send()
-
-        @pl.when(d > 0)
-        def _():
-            copy.wait_send()
-
-        return carry
-
-    lax.fori_loop(0, 32, rest, 0)
+            else:
+                relay(portion, stage - 2).wait_send()
+            got, at = incoming(portion, stage, d, grp)
+            remote(got, got, pass_send.at[at], pass_recv.at[at], peer).wait_send()
+            come, at = incoming(portion, stage, d, 1 - grp)
+            remote(come, come, pass_send.at[at], pass_recv.at[at], peer).wait_recv()
 
 
 def gather(assignment, bank, strain):
@@ -528,64 +607,62 @@
     return pl.pallas_call(
         gather_kernel,
         out_shape=(
-            jax.ShapeDtypeStruct((32, 8, COLS), jnp.float32),
+            jax.ShapeDtypeStruct((4, 2, 4, 8, COLS), jnp.float32),
             jax.ShapeDtypeStruct((2, 4, 2, 4, 8, COLS), jnp.float32),
         ),
         in_specs=[
             pl.BlockSpec(memory_space=pltpu.SMEM),
-            pl.BlockSpec(memory_space=pl.ANY),
-            pl.BlockSpec(memory_space=pl.ANY),
+            pl.BlockSpec(memory_space=pltpu.HBM),
+            pl.BlockSpec(memory_space=pltpu.HBM),
         ],
-        out_specs=[pl.BlockSpec(memory_space=pl.ANY), pl.BlockSpec(memory_space=pl.ANY)],
+        out_specs=[pl.BlockSpec(memory_space=pltpu.HBM), pl.BlockSpec(memory_space=pltpu.HBM)],
         scratch_shapes=[
+            pltpu.VMEM((16, 2, 4, HALF), jnp.float32),
             pltpu.VMEM((16, 8, HALF), jnp.float32),
-            pltpu.VMEM((16, 8, HALF), jnp.float32),
-            dma((3,)), dma, dma, dma((3, 3, 3)), dma((3, 3, 3)), dma((3, 3, 3)), dma((3, 3, 3)),
-            dma((32,)), dma((32,)), dma((32,)), dma((32,)),
+            pltpu.VMEM((1, 2, 4, COLS), jnp.float32),
+            pltpu.VMEM((8, COLS), jnp.float32),
+            dma((3,)), dma, dma, dma((3, 4, 3)), dma((3, 4, 3)), dma((3, 4, 3)), dma((3, 4, 3)),
+            dma((16,)), dma((16,)), dma((16,)), dma((16,)), dma((2, 16)), dma((2, 16)),
         ],
-        compiler_params=pltpu.CompilerParams(collective_id=0, has_side_effects=True),
+        compiler_params=pltpu.CompilerParams(collective_id=0, has_side_effects=True, vmem_limit_bytes=32 * 2**20),
     )(assignment, bank, strain)
 
 
 def scatter_kernel(rows, chi, net, send, recv):
     grp, tm = lax.axis_index("grp"), lax.axis_index("tm")
-    slot = tm % 16
-    to_grp = slot // 8
-    at = slot % 8
-    part = 2 * (tm // 16) + grp
-    from_part = tm // 8
-    from_grp = from_part % 2
-    self_too = (tm // 8) % 2 == grp
+    y, low_z, x = tm // 8, (tm // 4) % 2, tm % 4
+    to_grp = y // 2
+    at = 4 * (y % 2) + x
+    self_too = y // 2 == grp
     barrier = pltpu.get_barrier_semaphore()
 
+    def row_group(i):
+        return (at + i) % 8
+
     def target(i):
-        return 8 * part + (tm + i) % 8
-
-    def source(k):
-        return 8 * grp + k + 16 * (from_part // 2)
+        return (2 * grp + i // 4) * 8 + low_z * 4 + i % 4
 
     def greet(i, carry):
-        for device, group in ((target(i), to_grp), (source(i), from_grp)):
-            @pl.when(jnp.logical_not((device == tm) & (group == grp)))
-            def _():
-                pl.semaphore_signal(
-                    barrier, inc=1, device_id={"grp": group, "tm": device}, device_id_type=MESH
-                )
+        @pl.when(jnp.logical_not((target(i) == tm) & self_too))
+        def _():
+            pl.semaphore_signal(
+                barrier, inc=1, device_id={"grp": to_grp, "tm": target(i)}, device_id_type=MESH
+            )
+
         return carry
 
     lax.fori_loop(0, 8, greet, 0)
 
     @pl.when(self_too)
     def _():
-        pl.semaphore_wait(barrier, 14)
+        pl.semaphore_wait(barrier, 7)
 
     @pl.when(jnp.logical_not(self_too))
     def _():
-        pl.semaphore_wait(barrier, 16)
+        pl.semaphore_wait(barrier, 8)
 
     def parts(i):
-        piece = target(i) % 8
-        return ((rows.at[0, piece], chi.at[at]), (rows.at[pl.ds(1, 2), piece], net.at[at]))
+        return ((rows.at[0, i], chi.at[at]), (rows.at[pl.ds(1, 2), i], net.at[at]))
 
     def copy(i, kind):
         src, dst = parts(i)[kind]
@@ -594,8 +671,9 @@
             device_id={"grp": to_grp, "tm": target(i)}, device_id_type=MESH,
         )
 
-    def start(i, carry):
-        is_self = (target(i) == tm) & (to_grp == grp)
+    def start(step, carry):
+        i = row_group(step)
+        is_self = (target(i) == tm) & self_too
         for kind in range(2):
             @pl.when(is_self)
             def _():
@@ -610,7 +688,7 @@
     lax.fori_loop(0, 8, start, 0)
 
     def finish(i, carry):
-        is_self = (target(i) == tm) & (to_grp == grp)
+        is_self = (target(i) == tm) & self_too
 
         for kind, dst in ((0, chi), (1, net)):
             pltpu.make_async_copy(dst.at[i], dst.at[i], recv.at[kind, i]).wait()
@@ -631,21 +709,45 @@
             jax.ShapeDtypeStruct((8, 4, COLS), jnp.float32),
             jax.ShapeDtypeStruct((8, 2, 4, COLS), jnp.float32),
         ),
-        in_specs=[pl.BlockSpec(memory_space=pl.ANY)],
-        out_specs=[pl.BlockSpec(memory_space=pl.ANY), pl.BlockSpec(memory_space=pl.ANY)],
+        in_specs=[pl.BlockSpec(memory_space=pltpu.HBM)],
+        out_specs=[pl.BlockSpec(memory_space=pltpu.HBM), pl.BlockSpec(memory_space=pltpu.HBM)],
         scratch_shapes=[dma((2, 8)), dma((2, 8))],
         compiler_params=pltpu.CompilerParams(collective_id=1, has_side_effects=True),
     )(rows)
+
+
+def finish_kernel(chi, net, chi_out, net_out, sem):
+    copies = []
+    for k in range(8):
+        copies.append(pltpu.make_async_copy(chi.at[k], chi_out.at[k], sem.at[0, k]))
+        copies.append(pltpu.make_async_copy(net.at[k], net_out.at[k], sem.at[1, k]))
+    for copy in copies:
+        copy.start()
+    for copy in copies:
+        copy.wait()
+
+
+def finish(chi, net):
+    spec = pl.BlockSpec(memory_space=pltpu.HBM)
+    return pl.pallas_call(
+        finish_kernel,
+        out_shape=(
+            jax.ShapeDtypeStruct(chi.shape, jnp.float32), jax.ShapeDtypeStruct(net.shape, jnp.float32)
+        ),
+        in_specs=[spec, spec],
+        out_specs=[spec, spec],
+        scratch_shapes=[pltpu.SemaphoreType.DMA((2, 8))],
+    )(chi, net)
 
 
 def on_device(strain, bank, assignment, slides, bounds, antenna):
     tm = lax.axis_index("tm")
     det = lax.axis_index("det")
     grp = lax.axis_index("grp")
-    tmpl, signal = gather(assignment, bank.reshape(8, 8, COLS), strain.reshape(8, COLS))
-    part = 2 * (tm // 16) + grp
+    tmpl, signal = gather(assignment, bank, strain)
+    part = 2 * ((tm >> 2) & 1) + grp
     rows = filter_rows(part, det, tmpl.reshape(256, COLS), signal.reshape(2, 256, COLS), bounds, slides, antenna)
-    chi, net = scatter(rows)
+    chi, net = finish(*scatter(rows))
     return chi[None], net
 
 

time: 144 us -> 172 us (1.19)
  Pallas kernels: 126 us -> 155 us
    pallas_call x1 -> x2, Pallas kernels: 71.8 us -> 103 us  [the longest x1 54 us: gather(): pl.pallas_call(gather_kernel, out_shape=(jax.ShapeDtypeStruct((4, 2, 4, 8...]
    reshape x2 -> x0, local copies, waits for them, and re-layouts: 4.16 us -> none  [the longest x1 2.55 us: on_device(): bank.reshape(8, 8, COLS)]
    unnamed x16 -> x24, local copies, waits for them, and re-layouts: 11 us -> 14.8 us
    pallas_call x1, Pallas kernels: 27.3 us -> 25.4 us  [scatter(): pl.pallas_call(scatter_kernel, out_shape=(jax.ShapeDtypeStruct((8, 4, COL...]
where the time goes in v3:
time: 172 us
  Pallas kernels  155 us (90%)
  local copies, waits for them, and re-layouts  14.8 us (9%)
    pallas_call x1, Pallas kernels, gather(): pl.pallas_call(gather_kernel, out_shape=(jax.ShapeDtypeStruct((4, 2, 4, 8...  54 us
    pallas_call x1, Pallas kernels, finish(): pl.pallas_call(finish_kernel, out_shape=(jax.ShapeDtypeStruct(chi.shape,...  48.9 us
    pallas_call x1, Pallas kernels, filter_rows(): pl.pallas_call(kernel, grid_spec=spec, out_shape=jax.ShapeDtypeStruct((3,...  27.1 us
    pallas_call x1, Pallas kernels, scatter(): pl.pallas_call(scatter_kernel, out_shape=(jax.ShapeDtypeStruct((8, 4, COL...  25.4 us
    unnamed x24, local copies, waits for them, and re-layouts  14.8 us

profile of v3, /device:TPU:1, one launch (start us, length us, event | category | flops | bytes accessed | tf_op | source)
XLA Modules:
  0.0 171.7 jit_solution(9967374031290724199)
XLA Ops:
  0.6 0.1 pad_add_fusion.where_ref
  0.7 0.7 pad_add_fusion.1.bounds_ref
  1.4 0.0 copy-start.1
  1.4 1.2 copy-done.1
  2.7 0.0 copy-start.2
  2.7 0.9 copy-done.2
  3.6 0.7 copy-done.3
  4.2 54.0 %shard_map.122 = (f32[4,2,4,8,4096]{4,3,2,1,0:T(8,128)S(1)}, f32[2,4,2,4,8,4096]{5,4,3,2,1,0:T(8,128)S(1)}) custom-call(s32[16]{0:T(128)S(1)} %copy-done.3, f32[8,2,4,4096]{3,2,1,0:T(4,128)S(1)} %copy-done.1, f32[1,2,4,4096]{3,2,1,0:T(4,128)S(1)} %copy-done.2), custom_call_target="tpu_custom_call" | custom-call | tf_op jit(solution)/shard_map/pallas_call | solution.py:607
  58.2 0.0 copy-start.4
  58.2 3.2 %copy-done.4 = f32[2,4,2,4,8,4096]{5,4,3,2,1,0:T(8,128)} copy-done((f32[2,4,2,4,8,4096]{5,4,3,2,1,0:T(8,128)}, f32[2,4,2,4,8,4096]{5,4,3,2,1,0:T(8,128)S(1)}, u32[]{:S(2)}) %copy-start.4) | copy-done | bytes 8388632
  61.4 0.0 copy-start.5
  61.4 2.0 %copy-done.5 = f32[4,2,4,8,4096]{4,3,2,1,0:T(8,128)} copy-done((f32[4,2,4,8,4096]{4,3,2,1,0:T(8,128)}, f32[4,2,4,8,4096]{4,3,2,1,0:T(8,128)S(1)}, u32[]{:S(2)}) %copy-start.5) | copy-done | bytes 4194328
  63.4 0.0 copy-start.6
  63.4 0.7 copy-done.6
  64.1 0.7 copy-done.7
  64.7 1.6 copy-done.8
  66.3 1.0 copy-done.9
  67.4 0.9 copy-done.10
  68.3 0.8 copy-done.11
  69.1 27.1 %shard_map.123.rows = f32[3,8,4,4096]{3,2,1,0:T(4,128)S(1)} custom-call(s32[2]{0:T(128)S(1)} %pad_add_fusion.where_ref, s32[9]{0:T(128)S(1)} %pad_add_fusion.1.bounds_ref, f32[256,4096]{1,0:T(8,128)} %bitcast.7, f32[2,256,4096]{2,1,0:T(8,128)} %bitcast.5, f32[2,256,4096]{2,1,0:T(8,128)} %bitcast.6, bf16[4,4,256,256]{3,2,1,0:T(8,128)(2,1)S(1)} %copy-done.8, ...), custom_call_target="tpu_custom_call" | custom-call | flops 20000000000 | bytes 20000000 | tf_op jit(solution)/shard_map/pallas_call | solution.py:376
  96.2 0.0 copy-start
  96.2 1.2 copy-done
  97.4 25.4 %shard_map.124 = (f32[8,4,4096]{2,1,0:T(4,128)}, f32[8,2,4,4096]{3,2,1,0:T(4,128)}) custom-call(f32[3,8,4,4096]{3,2,1,0:T(4,128)} %copy-done), custom_call_target="tpu_custom_call" | custom-call | tf_op jit(solution)/shard_map/pallas_call | solution.py:706
  122.8 48.9 %shard_map.125 = (f32[8,4,4096]{2,1,0:T(4,128)}, f32[8,2,4,4096]{3,2,1,0:T(4,128)}) custom-call(f32[8,4,4096]{2,1,0:T(4,128)} %get-tuple-element.10.chi, f32[8,2,4,4096]{3,2,1,0:T(4,128)} %get-tuple-element.11.net), custom_call_target="tpu_custom_call" | custom-call | tf_op jit(solution)/shard_map/pallas_call | solution.py:732
  (6 shorter events, 0.0 us)
Async XLA Ops:
  1.4 1.2 copy-start.1
  2.7 0.9 copy-start.2
  3.6 0.7 copy-start.3
  58.2 3.2 %copy-start.4 = (f32[2,4,2,4,8,4096]{5,4,3,2,1,0:T(8,128)}, f32[2,4,2,4,8,4096]{5,4,3,2,1,0:T(8,128)S(1)}, u32[]{:S(2)}) copy-start(f32[2,4,2,4,8,4096]{5,4,3,2,1,0:T(8,128)S(1)} %get-tuple-element.9) | copy-start | bytes 25165828
  61.4 2.0 %copy-start.5 = (f32[4,2,4,8,4096]{4,3,2,1,0:T(8,128)}, f32[4,2,4,8,4096]{4,3,2,1,0:T(8,128)S(1)}, u32[]{:S(2)}) copy-start(f32[4,2,4,8,4096]{4,3,2,1,0:T(8,128)S(1)} %get-tuple-element.8) | copy-start | bytes 12582916
  63.4 0.7 copy-start.6
  64.1 0.7 copy-start.7
  64.7 1.6 copy-start.8
  66.3 1.0 copy-start.9
  67.4 0.9 copy-start.10
  68.3 0.8 copy-start.11
  96.2 1.2 copy-start

commit v4 on v3

v4 whole, which is shorter than its diff:
```python
import functools
import math

import jax
import jax.numpy as jnp
import numpy as np
from jax import lax
from jax.experimental import pallas as pl
from jax.experimental.pallas import tpu as pltpu

FOLD = 128
COLS = 4096
BINS = FOLD * COLS
BANDS = 8
CHUNK = 512
STEPS = COLS // CHUNK
LANES = 128
OUT_ROWS = 32


def rows_of(part):
    tau = np.arange(OUT_ROWS)
    return 64 * (part % 2) + 32 * (tau // 16) + 16 * (part // 2) + tau % 16


def halves(table):
    high = np.asarray(table, np.float32).astype(jnp.bfloat16)
    low = (np.asarray(table, np.float64) - high.astype(np.float64)).astype(np.float32)
    return high, low.astype(jnp.bfloat16)


def pack_columns(real, imag):
    m = real.shape[0]
    parts = np.stack([real.reshape(m, 32, 4), imag.reshape(m, 32, 4)], axis=2)
    return parts.reshape(m, 256)


def stacked_rows(cos, sin):
    top = pack_columns(cos, -sin)
    bottom = pack_columns(sin, cos)
    return np.concatenate([top, bottom], axis=0)


def constant_tables():
    b = np.arange(FOLD)
    even, odd, twiddle = [], [], []
    for part in range(4):
        e = rows_of(part)
        angle = 2 * np.pi * ((e[:, None] * b[None, :]) % FOLD) / FOLD
        cos, sin = np.cos(angle), np.sin(angle)
        for parity, group in ((0, even), (1, odd)):
            blocks = []
            for band in range(parity, BANDS, 2):
                inside = (b >= 16 * band - 8) & (b < 16 * band + 24)
                blocks.append(stacked_rows(cos * inside, sin * inside))
            group.append(np.concatenate(blocks, axis=0))
        a = np.arange(COLS)
        angle = 2 * np.pi * (e[:, None] * a[None, :]) / BINS
        twiddle.append(np.stack([np.cos(angle), np.sin(angle)]))
    even = halves(np.stack(even))
    odd = halves(np.stack(odd))
    bands = np.stack([even[0], even[1], odd[0], odd[1]], axis=1)
    twiddle = np.stack(twiddle).astype(np.float32).reshape(4, 2, 4, 8, 32, LANES).swapaxes(3, 4).copy()
    a1 = np.arange(LANES)
    q2 = np.arange(32)
    v, r2 = np.meshgrid(np.arange(8), np.arange(4), indexing="ij")
    angle = (2 * np.pi * v * r2 / 32)[..., None, None] * np.ones((8, LANES))
    turn = np.stack([np.cos(angle), np.sin(angle)]).astype(np.float32)
    angle = 2 * np.pi * (a1[None, :] * q2[:, None]) / COLS
    inner = np.stack([np.cos(angle), np.sin(angle)]).astype(np.float32)
    angle = 2 * np.pi * ((a1[:, None] * a1[None, :]) % LANES) / LANES
    cos, sin = np.cos(angle), np.sin(angle)
    last = np.stack(halves(np.block([[cos, sin], [-sin, cos]])))
    place = np.zeros((512, 512), np.float32)
    u1, u2 = np.meshgrid(np.arange(128), np.arange(4), indexing="ij")
    place[(u2 * 128 + u1).ravel(), (u2 + 4 * u1).ravel()] = 1.0
    return bands, twiddle, turn, inner, last, place.astype(jnp.bfloat16)


def split_two(x):
    high = x.astype(jnp.bfloat16)
    low = (x - high.astype(jnp.float32)).astype(jnp.bfloat16)
    return high, low


def mm(a, b):
    return jnp.dot(a, b, preferred_element_type=jnp.float32)


ROOT = math.sqrt(0.5)


def eight(x):
    def add(p, q):
        return (p[0] + q[0], p[1] + q[1])

    def sub(p, q):
        return (p[0] - q[0], p[1] - q[1])

    def turn(p):
        return (-p[1], p[0])

    def addi(p, q):
        return (p[0] - q[1], p[1] + q[0])

    def subi(p, q):
        return (p[0] + q[1], p[1] - q[0])

    def four(z):
        s02, d02 = add(z[0], z[2]), sub(z[0], z[2])
        s13, d13 = add(z[1], z[3]), sub(z[1], z[3])
        return [add(s02, s13), addi(d02, d13), sub(s02, s13), subi(d02, d13)]

    ev = four([x[0], x[2], x[4], x[6]])
    od = four([x[1], x[3], x[5], x[7]])
    o1 = ((od[1][0] - od[1][1]) * ROOT, (od[1][0] + od[1][1]) * ROOT)
    o3 = ((od[3][0] + od[3][1]) * ROOT, (od[3][1] - od[3][0]) * ROOT)
    return [
        add(ev[0], od[0]),
        add(ev[1], o1),
        addi(ev[2], od[2]),
        sub(ev[3], o3),
        sub(ev[0], od[0]),
        sub(ev[1], o1),
        subi(ev[2], od[2]),
        add(ev[3], o3),
    ]


def four_point(z):
    s0 = (z[0][0] + z[2][0], z[0][1] + z[2][1])
    d0 = (z[0][0] - z[2][0], z[0][1] - z[2][1])
    s1 = (z[1][0] + z[3][0], z[1][1] + z[3][1])
    d1 = (z[1][0] - z[3][0], z[1][1] - z[3][1])
    return [
        (s0[0] + s1[0], s0[1] + s1[1]),
        (d0[0] - d1[1], d0[1] + d1[0]),
        (s0[0] - s1[0], s0[1] - s1[1]),
        (d0[0] + d1[1], d0[1] - d1[0]),
    ]


def times(x, c, s):
    return (x[0] * c - x[1] * s, x[0] * s + x[1] * c)


def prepare(part, det, slides, antenna, net, ramp):
    column = (
        lax.broadcasted_iota(jnp.int32, (32, LANES), 0) * LANES
        + lax.broadcasted_iota(jnp.int32, (32, LANES), 1)
    )
    tau = lax.broadcasted_iota(jnp.int32, (OUT_ROWS, 256), 0)
    row = 64 * (part & 1) + 32 * (tau >> 4) + 16 * (part >> 1) + (tau & 15)
    packed = lax.broadcasted_iota(jnp.int32, (OUT_ROWS, 256), 1)
    bin_row = (packed >> 3) * 4 + (packed & 3)
    quarter = ((packed >> 2) & 1) * (FOLD // 4)
    for side in range(2):
        which = det if side == 0 else 1 - det
        first = which == 0
        weight_re = jnp.where(first, antenna[0, 0], antenna[1, 0])
        weight_im = jnp.where(first, antenna[0, 1], antenna[1, 1])
        for slide in range(2):
            shift = which * jnp.where(det == 0, slides[slide], slides[2 + slide])
            angle = (((row + shift) * bin_row + quarter) & (FOLD - 1)).astype(jnp.float32) * (2.0 * math.pi / FOLD)
            for half, table in ((0, jnp.cos(angle)), (1, jnp.sin(angle))):
                high, low = split_two(table)
                at = slice(64 * slide + 32 * half, 64 * slide + 32 * half + 32)
                net[side, 0, at, :] = high
                net[side, 1, at, :] = low
            angle = ((column * shift) & (BINS - 1)).astype(jnp.float32) * (2.0 * math.pi / BINS)
            cos, sin = jnp.cos(angle), jnp.sin(angle)
            ramp[slide, 2 * side] = weight_re * cos - weight_im * sin
            ramp[slide, 2 * side + 1] = weight_re * sin + weight_im * cos


def first_stage(chunk, det, bounds, tmpl, signal, bands, net, series, xe, xo, xn, power):
    start = pl.multiple_of(chunk * CHUNK, CHUNK)
    cols = pl.ds(start, CHUNK)
    src = lax.broadcasted_iota(jnp.int32, (2, 8, CHUNK), 0)
    sub = lax.broadcasted_iota(jnp.int32, (2, 8, CHUNK), 1)
    lane = lax.broadcasted_iota(jnp.int32, (2, 8, CHUNK), 2)
    top = sub < 4
    place_in = (src * 4 + (sub & 3)) * COLS + lane + start

    def group(i, carry):
        y, low_z, x = i // 4, (i // 2) % 2, pl.ds(2 * (i % 2), 2)
        rows = pl.ds(pl.multiple_of(16 * i, 16), 16)
        wave = tmpl[y, low_z, x, :, cols]
        rolled = pltpu.roll(wave, 4, 1)
        wave_re = jnp.where(top, wave, rolled)
        wave_im = jnp.where(top, rolled, -wave)
        own = signal[det, y, low_z, x, :, cols]
        own = own * wave_re + pltpu.roll(own, 4, 1) * wave_im
        oth = signal[1 - det, y, low_z, x, :, cols]
        oth = oth * wave_re + pltpu.roll(oth, 4, 1) * wave_im
        slot = (i + 1) // 2
        edge = jnp.where(slot == 0, 0, jnp.where(slot == BANDS, BINS, bounds[jnp.clip(slot - 1, 0, BANDS - 2)]))
        upper = (place_in + 8 * i * COLS) >= edge
        even = upper == (slot % 2 == 0)
        squares = wave * wave
        low_sum = jnp.where(upper, 0.0, squares)

        def fold(v):
            v = v[0] + v[1]
            return v[:, 0:128] + v[:, 128:256] + v[:, 256:384] + v[:, 384:512]

        power[i, 0] += fold(low_sum)
        power[i, 1] += fold(squares)
        high = own.astype(jnp.bfloat16).astype(jnp.float32)
        low = own - high

        def keep(value):
            return value.reshape(16, CHUNK).astype(jnp.bfloat16)

        xe[0, rows, :] = keep(jnp.where(even, high, 0.0))
        xe[1, rows, :] = keep(jnp.where(even, low, 0.0))
        xo[0, rows, :] = keep(jnp.where(even, 0.0, high))
        xo[1, rows, :] = keep(jnp.where(even, 0.0, low))
        high, low = split_two(oth.reshape(16, CHUNK))
        xn[0, rows, :] = high
        xn[1, rows, :] = low
        return carry

    lax.fori_loop(0, 16, group, 0)

    def three(high, low, x):
        return mm(high, x[0]) + mm(low, x[0]) + mm(high, x[1])

    def put(first, value):
        rows = value.shape[0] // 8
        for tile in range(CHUNK // LANES):
            piece = value[:, tile * LANES : (tile + 1) * LANES].reshape(rows, 8, LANES)
            series[pl.ds(first, rows), chunk * (CHUNK // LANES) + tile] = piece

    put(0, three(bands[0], bands[1], xe))
    put(32, three(bands[2], bands[3], xo))
    put(64, three(net[0, 0], net[0, 1], xe) + three(net[0, 0], net[0, 1], xo))
    put(80, three(net[1, 0], net[1, 1], xn))


def power_shares(power):
    powers = []
    for band in range(BANDS):
        acc = jnp.zeros((8, LANES), jnp.float32)
        for i in range(16):
            bound = (i - 1) // 2
            if bound == band:
                acc += power[i, 0]
            if bound + 1 == band:
                acc += power[i, 1] - power[i, 0]
        powers.append(jnp.sum(jnp.sum(acc, axis=0, keepdims=True), axis=1, keepdims=True))
    total = sum(powers)
    return total, [value / total for value in powers]


def second_stage(eb, total, shares, response, series, twiddle, turn, inner, last, place, ramp, zbuf, bbuf, vbuf, rows):
    inverse = [(1.0 / (2 * BANDS - 2)) / (total * share) for share in shares]
    net_scale = 1.0 / (total * response)
    cos, sin = twiddle[0, eb], twiddle[1, eb]
    inner_re, inner_im = inner[0][:, None, :], inner[1][:, None, :]

    def transform(item, z):
        z = times(z, cos, sin)
        re, im = z[0].reshape(8, 4, 8, LANES), z[1].reshape(8, 4, 8, LANES)
        values = eight([(re[s], im[s]) for s in range(8)])
        values = [values[0]] + [times(values[v], turn[0, v], turn[1, v]) for v in range(1, 8)]
        re = jnp.stack([value[0] for value in values])
        im = jnp.stack([value[1] for value in values])
        done = four_point([(re[:, r2], im[:, r2]) for r2 in range(4)])
        re = jnp.concatenate([value[0] for value in done], axis=0)
        im = jnp.concatenate([value[1] for value in done], axis=0)
        z = times((re, im), inner_re, inner_im)
        slot = item % 2
        zbuf[slot, :, 0:LANES] = z[0].reshape(256, LANES)
        zbuf[slot, :, LANES : 2 * LANES] = z[1].reshape(256, LANES)
        high, low = split_two(zbuf[slot])
        bbuf[item] = mm(high, last[0]) + mm(low, last[0]) + mm(high, last[1])

    for item in range(BANDS):
        base = (item // 2) * 8 + (item % 2) * 32 + eb
        transform(item, (series[base], series[base + 4]))
    for slide in range(2):
        own = (series[64 + 8 * slide + eb], series[64 + 8 * slide + 4 + eb])
        oth = (series[80 + 8 * slide + eb], series[80 + 8 * slide + 4 + eb])
        line = [ramp[slide, k][:, None, :] for k in range(4)]
        own, oth = times(own, line[0], line[1]), times(oth, line[2], line[3])
        transform(BANDS + slide, (own[0] + oth[0], own[1] + oth[1]))

    for u2 in range(4):
        part = slice(64 * u2, 64 * u2 + 64)
        re = [bbuf[band, part, 0:LANES] for band in range(BANDS)]
        im = [bbuf[band, part, LANES : 2 * LANES] for band in range(BANDS)]
        whole_re, whole_im = sum(re), sum(im)
        chi = None
        for band in range(BANDS):
            gap_re = re[band] - shares[band] * whole_re
            gap_im = im[band] - shares[band] * whole_im
            term = (gap_re * gap_re + gap_im * gap_im) * inverse[band]
            chi = term if chi is None else chi + term
        columns = slice(u2 * LANES, (u2 + 1) * LANES)
        vbuf[0:64, columns] = chi
        for slide in range(2):
            re = bbuf[BANDS + slide, part, 0:LANES]
            im = bbuf[BANDS + slide, part, LANES : 2 * LANES]
            vbuf[64 + 64 * slide : 128 + 64 * slide, columns] = (re * re + im * im) * net_scale
    high, low = split_two(vbuf[...])
    done = mm(high, place[...]) + mm(low, place[...])
    for kind in range(3):
        for v in range(8):
            both = done[kind * 64 + v * 8 : kind * 64 + v * 8 + 8, :]
            rows[kind, 2 * eb, :, v * 512 : (v + 1) * 512] = both[0:4]
            rows[kind, 2 * eb + 1, :, v * 512 : (v + 1) * 512] = both[4:8]


def compute_scratch():
    return [
        pltpu.VMEM((2, 2, 128, 256), jnp.bfloat16),
        pltpu.VMEM((2, 4, 32, LANES), jnp.float32),
        pltpu.VMEM((96, 32, 8, LANES), jnp.float32),
        pltpu.VMEM((2, 256, CHUNK), jnp.bfloat16),
        pltpu.VMEM((2, 256, CHUNK), jnp.bfloat16),
        pltpu.VMEM((2, 256, CHUNK), jnp.bfloat16),
        pltpu.VMEM((16, 2, 8, LANES), jnp.float32),
        pltpu.VMEM((2, 256, 256), jnp.float32),
        pltpu.VMEM((10, 256, 256), jnp.float32),
        pltpu.VMEM((192, 512), jnp.float32),
        pltpu.VMEM((4, 256, 256), jnp.bfloat16),
        pltpu.VMEM((2, 4, 32, 8, LANES), jnp.float32),
        pltpu.VMEM((2, 8, 4, 8, LANES), jnp.float32),
        pltpu.VMEM((2, 32, LANES), jnp.float32),
        pltpu.VMEM((2, 256, 256), jnp.bfloat16),
        pltpu.VMEM((512, 512), jnp.bfloat16),
    ]


MESH = pl.DeviceIdType.MESH
HALF = COLS // 2
PORTIONS = ((0, 640), (640, 640), (1280, 768))
ORDERS = (("x", "y", "z"), ("y", "z", "x"), ("z", "x", "y"))


def kernel(
    assign, bounds, slides, antenna, bank, strain, bands_hbm, twiddle_hbm, turn_hbm, inner_hbm, last_hbm, place_hbm,
    chi, net_out, tmpl, signal, everything, staged, loaded, packed, rows,
    local_sem, swap_send, swap_recv, wide_send, wide_recv, pass_send, pass_recv,
    far_send, far_recv, deep_send, deep_recv, near_send, near_recv, out_send, out_recv, table_sem,
    net, ramp, series, xe, xo, xn, power, zbuf, bbuf, vbuf, bands, twiddle, turn, inner, last, place,
):
    det, grp, tm = lax.axis_index("det"), lax.axis_index("grp"), lax.axis_index("tm")
    low_z = (tm // 4) % 2
    here = {"y": tm // 8, "z": det * 2 + low_z, "x": tm % 4}
    peer = {"grp": 1 - grp}
    half = pl.ds(pl.multiple_of(grp * HALF, HALF), HALF)
    other = pl.ds(pl.multiple_of((1 - grp) * HALF, HALF), HALF)

    def moved(axis, by):
        there = dict(here)
        there[axis] = (here[axis] + by + 4) % 4
        return there

    def ident(place):
        return {"det": place["z"] // 2, "tm": place["y"] * 8 + (place["z"] % 2) * 4 + place["x"]}

    def shifted(d, sign=1):
        there = dict(here)
        there["y"] = (here["y"] + sign * (d // 4) + 4) % 4
        there["x"] = (here["x"] + sign * (d % 4) + 4) % 4
        return there

    keep = pltpu.make_async_copy(bank.at[:, :, :, half], everything.at[pl.ds(grp * 8, 8)], local_sem.at[0])
    keep.start()
    own = pltpu.make_async_copy(strain, loaded, local_sem.at[1])
    own.start()

    part = 2 * low_z + grp
    tables = [
        pltpu.make_async_copy(src, dst, table_sem.at[i])
        for i, (src, dst) in enumerate((
            (bands_hbm.at[part], bands), (twiddle_hbm.at[part], twiddle), (turn_hbm, turn),
            (inner_hbm, inner), (last_hbm, last), (place_hbm, place),
        ))
    ]
    for copy in tables:
        copy.start()

    to_grp = here["y"] // 2
    same_core = to_grp == grp
    slot_at = 4 * (here["y"] % 2) + here["x"]

    def target(i):
        return (2 * grp + i // 4) * 8 + low_z * 4 + i % 4

    barrier = pltpu.get_barrier_semaphore()

    def greet(d, carry):
        pl.semaphore_signal(barrier, inc=1, device_id=ident(shifted(d)), device_id_type=MESH)
        return carry

    lax.fori_loop(1, 16, greet, 0)
    for d in (1, 2, 3):
        pl.semaphore_signal(barrier, inc=1, device_id=ident(moved("z", d)), device_id_type=MESH)
    pl.semaphore_signal(barrier, inc=1, device_id=peer, device_id_type=MESH)

    @pl.when(same_core)
    def _():
        pl.semaphore_wait(barrier, 19)

    @pl.when(jnp.logical_not(same_core))
    def _():
        def greet_other(i, carry):
            pl.semaphore_signal(
                barrier, inc=1, device_id={"grp": 1 - grp, "tm": target(i)}, device_id_type=MESH
            )
            return carry

        lax.fori_loop(0, 8, greet_other, 0)
        pl.semaphore_wait(barrier, 27)

    def remote(src, dst, send, recv, device):
        return pltpu.make_async_remote_copy(
            src_ref=src, dst_ref=dst, send_sem=send, recv_sem=recv, device_id=device, device_id_type=MESH
        )

    swap = remote(bank.at[:, :, :, other], everything.at[pl.ds(grp * 8, 8)], swap_send, swap_recv, peer)
    swap.start()

    def columns(portion, core):
        first, width = PORTIONS[portion]
        return pl.ds(pl.multiple_of(core * HALF + first, LANES), width)

    def region(portion, stage, place, core, part=None):
        done = ORDERS[portion][:stage]
        cut = "x" if ORDERS[portion][2] == "y" else "y"

        def every(axis, value, size):
            if axis not in done:
                return value
            if part is not None and axis == cut:
                return pl.ds(2 * part, 2)
            return pl.ds(0, size)

        return signal.at[
            every("z", place["z"] // 2, 2), every("y", place["y"], 4), every("z", place["z"] % 2, 2),
            every("x", place["x"], 4), :, columns(portion, core),
        ]

    def wide(portion, stage, d):
        dst = region(portion, stage, here, grp)
        src = packed.at[:, columns(portion, grp)] if stage == 0 else dst
        at = (portion, stage, d - 1)
        return remote(src, dst, wide_send.at[at], wide_recv.at[at], ident(moved(ORDERS[portion][stage], d)))

    def relay(portion, part):
        axis = ORDERS[portion][2]
        got = region(portion, 2, moved(axis, -1 if part == 0 else 1), grp, part)
        at = (portion, 2 + part, 1)
        return remote(got, got, wide_send.at[at], wide_recv.at[at], ident(moved(axis, 1 if part == 0 else -1)))

    def incoming(portion, stage, d, core):
        axis = ORDERS[portion][min(stage, 2)]
        if stage < 2 or d != 2:
            part = None
        else:
            part = stage - 2
        return region(portion, min(stage, 2), moved(axis, -d), core, part), (portion, stage, d - 1)

    def arrived(portion, stage, d):
        got, at = incoming(portion, stage, d, grp)
        remote(got, got, wide_send.at[at], wide_recv.at[at], peer).wait_recv()
        remote(got, got, pass_send.at[at], pass_recv.at[at], peer).start()

    own.wait()
    packed[0:4, :] = loaded[0, 0]
    packed[4:8, :] = loaded[0, 1]
    for portion in range(3):
        for d in (1, 3, 2):
            wide(portion, 0, d).start()
    mine = pltpu.make_async_copy(packed, signal.at[det, here["y"], low_z, here["x"]], local_sem.at[1])
    mine.start()

    swap.wait_recv()
    keep.wait()
    for slot in range(16):
        wave = everything[assign[slot]]
        staged[slot, 0:4, :] = wave[0]
        staged[slot, 4:8, :] = wave[1]

    def far(d):
        to = shifted(d)
        return remote(
            staged.at[to["y"] * 4 + to["x"]], tmpl.at[here["y"], low_z, here["x"], :, half],
            far_send.at[d], far_recv.at[d], ident(to),
        )

    def piece(place, plane, columns):
        return tmpl.at[place["y"], plane, place["x"], :, columns]

    def deep(place):
        got = piece(place, low_z, half)
        at = place["y"] * 4 + place["x"]
        to = moved("z", jnp.where(place["y"] < 2, 1, 3))
        return remote(got, got, deep_send.at[at], deep_recv.at[at], ident(to))

    def near(place, plane, columns):
        got = piece(place, plane, columns)
        at = (plane, place["y"] * 4 + place["x"])
        return remote(got, got, near_send.at[at], near_recv.at[at], peer)

    def send_far(d, carry):
        far(d).start()
        return carry

    lax.fori_loop(1, 16, send_far, 0)
    slot_here = here["y"] * 4 + here["x"]
    kept = pltpu.make_async_copy(staged.at[slot_here], piece(here, low_z, half), local_sem.at[2])
    kept.start()

    prepare(part, det, slides, antenna, net, ramp)
    power[...] = jnp.zeros_like(power)
    mine.wait()
    for portion in range(3):
        for d in (1, 3, 2):
            arrived(portion, 0, d)
        for d in (1, 3, 2):
            wide(portion, 1, d).start()
    kept.wait()
    deep(here).start()
    near(here, low_z, half).start()

    def got_far(d, carry):
        place = shifted(d, -1)
        got = piece(place, low_z, half)
        remote(got, got, far_send.at[d], far_recv.at[d], peer).wait_recv()
        deep(place).start()
        near(place, low_z, half).start()
        return carry

    lax.fori_loop(1, 16, got_far, 0)
    for portion in range(3):
        for d in (1, 3, 2):
            arrived(portion, 1, d)
        for d in (1, 3):
            wide(portion, 2, d).start()

    def place_at(p):
        return {"y": p // 4, "x": p % 4}

    def got_deep(p, carry):
        got = piece(place_at(p), 1 - low_z, half)
        remote(got, got, deep_send.at[p], deep_recv.at[p], peer).wait_recv()
        near(place_at(p), 1 - low_z, half).start()
        return carry

    lax.fori_loop(0, 16, got_deep, 0)
    for portion in range(3):
        for d, part in ((1, 0), (3, 1)):
            arrived(portion, 2, d)
            relay(portion, part).start()
    for portion in range(3):
        for part in range(2):
            arrived(portion, 2 + part, 2)

    def arrivals(p, carry):
        for plane in range(2):
            near(place_at(p), plane, other).wait_recv()
        return carry

    lax.fori_loop(0, 16, arrivals, 0)
    events = ((0, 1), (0, 2), (0, 3), (1, 1), (1, 2), (1, 3), (2, 1), (2, 3), (2, 2), (3, 2))
    for portion in range(3):
        for stage, d in events:
            come, at = incoming(portion, stage, d, 1 - grp)
            remote(come, come, pass_send.at[at], pass_recv.at[at], peer).wait_recv()
    for copy in tables:
        copy.wait()

    def chunk(i, carry):
        first_stage(i, det, bounds, tmpl, signal, bands, net, series, xe, xo, xn, power)
        return carry

    lax.fori_loop(0, STEPS, chunk, 0)
    total, shares = power_shares(power)
    response = sum(antenna[d, c] * antenna[d, c] for d in range(2) for c in range(2))

    def parts(i):
        return ((rows.at[0, i], chi.at[slot_at]), (rows.at[pl.ds(1, 2), i], net_out.at[slot_at]))

    def give(i, kind):
        src, dst = parts(i)[kind]
        return pltpu.make_async_remote_copy(
            src_ref=src, dst_ref=dst, send_sem=out_send.at[kind, i], recv_sem=out_recv.at[kind, slot_at],
            device_id={"grp": to_grp, "tm": target(i)}, device_id_type=MESH,
        )

    def block(eb, carry):
        second_stage(
            eb, total, shares, response, series, twiddle, turn, inner, last, place, ramp, zbuf, bbuf, vbuf, rows
        )
        for k in range(2):
            i = 2 * eb + k
            is_self = (target(i) == tm) & same_core
            for kind in range(2):
                @pl.when(is_self)
                def _():
                    src, dst = parts(i)[kind]
                    pltpu.make_async_copy(src, dst, out_recv.at[kind, slot_at]).start()

                @pl.when(jnp.logical_not(is_self))
                def _():
                    give(i, kind).start()
        return carry

    lax.fori_loop(0, 4, block, 0)

    swap.wait_send()

    def rest(p, carry):
        deep(place_at(p)).wait_send()
        for plane in range(2):
            near(place_at(p), plane, half).wait_send()

        @pl.when(p > 0)
        def _():
            far(p).wait_send()

        return carry

    lax.fori_loop(0, 16, rest, 0)
    for portion in range(3):
        for stage, d in events:
            if stage < 2 or d != 2:
                wide(portion, stage, d).wait_send()
            else:
                relay(portion, stage - 2).wait_send()
            got, at = incoming(portion, stage, d, grp)
            remote(got, got, pass_send.at[at], pass_recv.at[at], peer).wait_send()

    def finish(i, carry):
        is_self = (target(i) == tm) & same_core
        for kind, dst in ((0, chi), (1, net_out)):
            pltpu.make_async_copy(dst.at[i], dst.at[i], out_recv.at[kind, i]).wait()

            @pl.when(jnp.logical_not(is_self))
            def _():
                give(i, kind).wait_send()
        return carry

    lax.fori_loop(0, 8, finish, 0)


def on_device(strain, bank, assignment, slides, bounds, antenna):
    dma = pltpu.SemaphoreType.DMA
    smem, hbm = pl.BlockSpec(memory_space=pltpu.SMEM), pl.BlockSpec(memory_space=pltpu.HBM)
    chi, net = pl.pallas_call(
        kernel,
        out_shape=(
            jax.ShapeDtypeStruct((8, 4, COLS), jnp.float32),
            jax.ShapeDtypeStruct((8, 2, 4, COLS), jnp.float32),
        ),
        in_specs=[smem] * 4 + [hbm] * 8,
        out_specs=[hbm, hbm],
        scratch_shapes=[
            pltpu.VMEM((4, 2, 4, 8, COLS), jnp.float32),
            pltpu.VMEM((2, 4, 2, 4, 8, COLS), jnp.float32),
            pltpu.VMEM((16, 2, 4, HALF), jnp.float32),
            pltpu.VMEM((16, 8, HALF), jnp.float32),
            pltpu.VMEM((1, 2, 4, COLS), jnp.float32),
            pltpu.VMEM((8, COLS), jnp.float32),
            pltpu.VMEM((3, 8, 4, COLS), jnp.float32),
            dma((3,)), dma, dma, dma((3, 4, 3)), dma((3, 4, 3)), dma((3, 4, 3)), dma((3, 4, 3)),
            dma((16,)), dma((16,)), dma((16,)), dma((16,)), dma((2, 16)), dma((2, 16)), dma((2, 8)), dma((2, 8)),
            dma((6,)),
        ] + compute_scratch(),
        compiler_params=pltpu.CompilerParams(collective_id=0, has_side_effects=True, vmem_limit_bytes=60 * 2**20),
        cost_estimate=pl.CostEstimate(flops=20 * 10**9, bytes_accessed=20 * 10**6, transcendentals=0),
    )(assignment, bounds, slides, antenna, bank, strain, *[jnp.asarray(table) for table in constant_tables()])
    return chi[None], net


def solution(mesh):
    P = jax.sharding.PartitionSpec
    return jax.shard_map(
        on_device,
        mesh=mesh,
        in_specs=(P("det", None, "tm", None), P("grp", None, "tm", None), P(), P(), P(), P()),
        out_specs=(P("det", "grp", "tm", None), P("grp", "det", "tm", None)),
        check_vma=False,
    )
```

time: 172 us -> 102 us (0.59)
  Pallas kernels: 155 us -> 95.5 us
  local copies, waits for them, and re-layouts: 14.8 us -> 4.17 us
    pallas_call x4 -> x1, Pallas kernels: 155 us -> 95.5 us  [on_device(): pl.pallas_call(kernel, out_shape=(jax.ShapeDtypeStruct((8, 4, COLS), jnp....]
    unnamed x24 -> x2, local copies, waits for them, and re-layouts: 14.8 us -> 4.17 us
where the time goes in v4:
time: 102 us; the launch traced here: 100 us
  Pallas kernels  95.5 us (94%)
  local copies, waits for them, and re-layouts  4.17 us (4%)
    pallas_call x1, Pallas kernels, on_device(): pl.pallas_call(kernel, out_shape=(jax.ShapeDtypeStruct((8, 4, COLS), jnp....  95.5 us
    unnamed x2, local copies, waits for them, and re-layouts  4.17 us

profile of v4, /device:TPU:1, one launch (start us, length us, event | category | flops | bytes accessed | tf_op | source)
XLA Modules:
  0.0 100.3 jit_solution(16803780112628902217)
XLA Ops:
  0.6 95.5 %shard_map.131 = (f32[8,4,4096]{2,1,0:T(4,128)}, f32[8,2,4,4096]{3,2,1,0:T(4,128)}) custom-call(s32[16]{0:T(128)} %assign.1, s32[7]{0:T(128)} %bounds.1, s32[4]{0:T(128)} %slides.1, f32[2,2]{1,0:T(2,128)} %antenna.1, f32[8,2,4,4096]{3,2,1,0:T(4,128)} %bank.1, f32[1,2,4,4096]{3,2,1,0:T(4,128)} %strain.1, bf16[4,4,256,256]{3,2,1,0:T(8,128)(2,1)} %constant.12.clone.bands_hbm, ...), custom_call_target="tpu_custom_call" | custom-call | flops 20000000000 | bytes 20000000 | tf_op jit(solution)/shard_map/pallas_call | solution.py:654
  96.1 1.9 %copy.16 = f32[1,8,4,4096]{3,2,1,0:T(4,128)} copy(f32[1,8,4,4096]{3,2,1,0:T(4,128)} %bitcast.1) | data formatting | bytes 1048576
  98.0 2.3 %copy.17 = f32[8,2,4,4096]{3,2,1,0:T(4,128)} copy(f32[8,2,4,4096]{3,2,1,0:T(4,128)} %get-tuple-element.9) | data formatting | bytes 2097152

commit v5 on v4

--- a/solution.py
+++ b/solution.py
@@ -173,8 +173,12 @@
             ramp[slide, 2 * side + 1] = weight_re * sin + weight_im * cos
 
 
-def first_stage(chunk, det, bounds, tmpl, signal, bands, net, series, xe, xo, xn, power):
-    start = pl.multiple_of(chunk * CHUNK, CHUNK)
+def column_block(step):
+    return 2 * (step // 4) + step % 2 + 4 * ((step // 2) % 2)
+
+
+def products(step, det, bounds, tmpl, signal, held, power):
+    start = pl.multiple_of(column_block(step) * CHUNK, CHUNK)
     cols = pl.ds(start, CHUNK)
     src = lax.broadcasted_iota(jnp.int32, (2, 8, CHUNK), 0)
     sub = lax.broadcasted_iota(jnp.int32, (2, 8, CHUNK), 1)
@@ -182,9 +186,16 @@
     top = sub < 4
     place_in = (src * 4 + (sub & 3)) * COLS + lane + start
 
-    def group(i, carry):
-        y, low_z, x = i // 4, (i // 2) % 2, pl.ds(2 * (i % 2), 2)
-        rows = pl.ds(pl.multiple_of(16 * i, 16), 16)
+    def fold(v):
+        v = v[0] + v[1]
+        return v[:, 0:128] + v[:, 128:256] + v[:, 256:384] + v[:, 384:512]
+
+    def keep(value):
+        return value.reshape(16, CHUNK).astype(jnp.bfloat16)
+
+    for i in range(16):
+        y, low_z, x = i // 4, (i // 2) % 2, slice(2 * (i % 2), 2 * (i % 2) + 2)
+        rows = slice(16 * i, 16 * i + 16)
         wave = tmpl[y, low_z, x, :, cols]
         rolled = pltpu.roll(wave, 4, 1)
         wave_re = jnp.where(top, wave, rolled)
@@ -193,49 +204,47 @@
         own = own * wave_re + pltpu.roll(own, 4, 1) * wave_im
         oth = signal[1 - det, y, low_z, x, :, cols]
         oth = oth * wave_re + pltpu.roll(oth, 4, 1) * wave_im
-        slot = (i + 1) // 2
-        edge = jnp.where(slot == 0, 0, jnp.where(slot == BANDS, BINS, bounds[jnp.clip(slot - 1, 0, BANDS - 2)]))
-        upper = (place_in + 8 * i * COLS) >= edge
-        even = upper == (slot % 2 == 0)
+        bound = (i - 1) // 2
         squares = wave * wave
-        low_sum = jnp.where(upper, 0.0, squares)
-
-        def fold(v):
-            v = v[0] + v[1]
-            return v[:, 0:128] + v[:, 128:256] + v[:, 256:384] + v[:, 384:512]
-
-        power[i, 0] += fold(low_sum)
-        power[i, 1] += fold(squares)
         high = own.astype(jnp.bfloat16).astype(jnp.float32)
         low = own - high
-
-        def keep(value):
-            return value.reshape(16, CHUNK).astype(jnp.bfloat16)
-
-        xe[0, rows, :] = keep(jnp.where(even, high, 0.0))
-        xe[1, rows, :] = keep(jnp.where(even, low, 0.0))
-        xo[0, rows, :] = keep(jnp.where(even, 0.0, high))
-        xo[1, rows, :] = keep(jnp.where(even, 0.0, low))
-        high, low = split_two(oth.reshape(16, CHUNK))
-        xn[0, rows, :] = high
-        xn[1, rows, :] = low
-        return carry
-
-    lax.fori_loop(0, 16, group, 0)
-
-    def three(high, low, x):
-        return mm(high, x[0]) + mm(low, x[0]) + mm(high, x[1])
+        if 0 <= bound < BANDS - 1:
+            upper = place_in >= bounds[bound] - 8 * i * COLS
+            power[i, 0] += fold(jnp.where(upper, 0.0, squares))
+            cut = lambda value: jnp.where(upper, 0.0, value)
+            high_low, low_low = cut(high), cut(low)
+            lower = (keep(high_low), keep(low_low))
+            higher = (keep(high - high_low), keep(low - low_low))
+            even, odd = (higher, lower) if bound % 2 else (lower, higher)
+        else:
+            zero = jnp.zeros((16, CHUNK), jnp.bfloat16)
+            even, odd = (keep(high), keep(low)), (zero, zero)
+            if bound == BANDS - 1:
+                even, odd = odd, even
+                power[i, 0] += fold(squares)
+        power[i, 1] += fold(squares)
+        held[0, rows, :], held[1, rows, :] = even
+        held[2, rows, :], held[3, rows, :] = odd
+        held[4, rows, :], held[5, rows, :] = split_two(oth.reshape(16, CHUNK))
+
+
+def first_stage(step, held, bands, net, series):
+    tiles = CHUNK // LANES
+    block = column_block(step) * tiles
+
+    def three(high, low, k):
+        return mm(high, held[k]) + mm(low, held[k]) + mm(high, held[k + 1])
 
     def put(first, value):
         rows = value.shape[0] // 8
-        for tile in range(CHUNK // LANES):
+        for tile in range(tiles):
             piece = value[:, tile * LANES : (tile + 1) * LANES].reshape(rows, 8, LANES)
-            series[pl.ds(first, rows), chunk * (CHUNK // LANES) + tile] = piece
-
-    put(0, three(bands[0], bands[1], xe))
-    put(32, three(bands[2], bands[3], xo))
-    put(64, three(net[0, 0], net[0, 1], xe) + three(net[0, 0], net[0, 1], xo))
-    put(80, three(net[1, 0], net[1, 1], xn))
+            series[pl.ds(first, rows), block + tile] = piece
+
+    put(0, three(bands[0], bands[1], 0))
+    put(32, three(bands[2], bands[3], 2))
+    put(64, three(net[0, 0], net[0, 1], 0) + three(net[0, 0], net[0, 1], 2))
+    put(80, three(net[1, 0], net[1, 1], 4))
 
 
 def power_shares(power):
@@ -317,9 +326,8 @@
         pltpu.VMEM((2, 2, 128, 256), jnp.bfloat16),
         pltpu.VMEM((2, 4, 32, LANES), jnp.float32),
         pltpu.VMEM((96, 32, 8, LANES), jnp.float32),
-        pltpu.VMEM((2, 256, CHUNK), jnp.bfloat16),
-        pltpu.VMEM((2, 256, CHUNK), jnp.bfloat16),
-        pltpu.VMEM((2, 256, CHUNK), jnp.bfloat16),
+        pltpu.VMEM((6, 256, CHUNK), jnp.bfloat16),
+        pltpu.VMEM((6, 256, CHUNK), jnp.bfloat16),
         pltpu.VMEM((16, 2, 8, LANES), jnp.float32),
         pltpu.VMEM((2, 256, 256), jnp.float32),
         pltpu.VMEM((10, 256, 256), jnp.float32),
@@ -335,8 +343,10 @@
 
 MESH = pl.DeviceIdType.MESH
 HALF = COLS // 2
-PORTIONS = ((0, 640), (640, 640), (1280, 768))
-ORDERS = (("x", "y", "z"), ("y", "z", "x"), ("z", "x", "y"))
+PORTIONS = ((0, 384), (384, 384), (768, 256), (1024, 384), (1408, 256), (1664, 384))
+ORDERS = (("x", "y", "z"), ("y", "z", "x"), ("z", "x", "y")) * 2
+EARLY, LATE = (0, 1, 2), (3, 4, 5)
+FAR = (1, 4, 3, 12, 5, 15, 7, 13, 2, 8, 6, 9, 11, 14, 10)
 
 
 def kernel(
@@ -344,7 +354,7 @@
     chi, net_out, tmpl, signal, everything, staged, loaded, packed, rows,
     local_sem, swap_send, swap_recv, wide_send, wide_recv, pass_send, pass_recv,
     far_send, far_recv, deep_send, deep_recv, near_send, near_recv, out_send, out_recv, table_sem,
-    net, ramp, series, xe, xo, xn, power, zbuf, bbuf, vbuf, bands, twiddle, turn, inner, last, place,
+    net, ramp, series, held_a, held_b, power, zbuf, bbuf, vbuf, bands, twiddle, turn, inner, last, place,
 ):
     det, grp, tm = lax.axis_index("det"), lax.axis_index("grp"), lax.axis_index("tm")
     low_z = (tm // 4) % 2
@@ -401,20 +411,7 @@
         pl.semaphore_signal(barrier, inc=1, device_id=ident(moved("z", d)), device_id_type=MESH)
     pl.semaphore_signal(barrier, inc=1, device_id=peer, device_id_type=MESH)
 
-    @pl.when(same_core)
-    def _():
-        pl.semaphore_wait(barrier, 19)
-
-    @pl.when(jnp.logical_not(same_core))
-    def _():
-        def greet_other(i, carry):
-            pl.semaphore_signal(
-                barrier, inc=1, device_id={"grp": 1 - grp, "tm": target(i)}, device_id_type=MESH
-            )
-            return carry
-
-        lax.fori_loop(0, 8, greet_other, 0)
-        pl.semaphore_wait(barrier, 27)
+    pl.semaphore_wait(barrier, 19)
 
     def remote(src, dst, send, recv, device):
         return pltpu.make_async_remote_copy(
@@ -469,10 +466,35 @@
         remote(got, got, wide_send.at[at], wide_recv.at[at], peer).wait_recv()
         remote(got, got, pass_send.at[at], pass_recv.at[at], peer).start()
 
+    def pass_on(portions):
+        for portion in portions:
+            for d, part in ((1, 0), (3, 1)):
+                arrived(portion, 2, d)
+                relay(portion, part).start()
+
+    def pass_last(portions):
+        for portion in portions:
+            for part in range(2):
+                arrived(portion, 2 + part, 2)
+
+    def pass_first(portions):
+        for portion in portions:
+            for d in (1, 3, 2):
+                arrived(portion, 0, d)
+            for d in (1, 3, 2):
+                wide(portion, 1, d).start()
+
+    def pass_second(portions):
+        for portion in portions:
+            for d in (1, 3, 2):
+                arrived(portion, 1, d)
+            for d in (1, 3):
+                wide(portion, 2, d).start()
+
     own.wait()
     packed[0:4, :] = loaded[0, 0]
     packed[4:8, :] = loaded[0, 1]
-    for portion in range(3):
+    for portion in EARLY + LATE:
         for d in (1, 3, 2):
             wide(portion, 0, d).start()
     mine = pltpu.make_async_copy(packed, signal.at[det, here["y"], low_z, here["x"]], local_sem.at[1])
@@ -498,7 +520,7 @@
     def deep(place):
         got = piece(place, low_z, half)
         at = place["y"] * 4 + place["x"]
-        to = moved("z", jnp.where(place["y"] < 2, 1, 3))
+        to = moved("z", 1 + 2 * (place["x"] % 2))
         return remote(got, got, deep_send.at[at], deep_recv.at[at], ident(to))
 
     def near(place, plane, columns):
@@ -506,59 +528,61 @@
         at = (plane, place["y"] * 4 + place["x"])
         return remote(got, got, near_send.at[at], near_recv.at[at], peer)
 
-    def send_far(d, carry):
+    mine.wait()
+    pass_first(EARLY)
+    for d in FAR:
         far(d).start()
-        return carry
-
-    lax.fori_loop(1, 16, send_far, 0)
     slot_here = here["y"] * 4 + here["x"]
     kept = pltpu.make_async_copy(staged.at[slot_here], piece(here, low_z, half), local_sem.at[2])
     kept.start()
 
     prepare(part, det, slides, antenna, net, ramp)
     power[...] = jnp.zeros_like(power)
-    mine.wait()
-    for portion in range(3):
-        for d in (1, 3, 2):
-            arrived(portion, 0, d)
-        for d in (1, 3, 2):
-            wide(portion, 1, d).start()
     kept.wait()
     deep(here).start()
     near(here, low_z, half).start()
 
-    def got_far(d, carry):
-        place = shifted(d, -1)
-        got = piece(place, low_z, half)
-        remote(got, got, far_send.at[d], far_recv.at[d], peer).wait_recv()
-        deep(place).start()
-        near(place, low_z, half).start()
-        return carry
-
-    lax.fori_loop(1, 16, got_far, 0)
-    for portion in range(3):
-        for d in (1, 3, 2):
-            arrived(portion, 1, d)
-        for d in (1, 3):
-            wide(portion, 2, d).start()
-
     def place_at(p):
         return {"y": p // 4, "x": p % 4}
 
-    def got_deep(p, carry):
-        got = piece(place_at(p), 1 - low_z, half)
-        remote(got, got, deep_send.at[p], deep_recv.at[p], peer).wait_recv()
-        near(place_at(p), 1 - low_z, half).start()
-        return carry
-
-    lax.fori_loop(0, 16, got_deep, 0)
-    for portion in range(3):
-        for d, part in ((1, 0), (3, 1)):
-            arrived(portion, 2, d)
-            relay(portion, part).start()
-    for portion in range(3):
-        for part in range(2):
-            arrived(portion, 2 + part, 2)
+    def got_far(order):
+        for d in order:
+            place = shifted(d, -1)
+            got = piece(place, low_z, half)
+            remote(got, got, far_send.at[d], far_recv.at[d], peer).wait_recv()
+            deep(place).start()
+            near(place, low_z, half).start()
+
+    def got_deep(order):
+        for d in order:
+            place = shifted(d, -1)
+            got = piece(place, 1 - low_z, half)
+            at = place["y"] * 4 + place["x"]
+            remote(got, got, deep_send.at[at], deep_recv.at[at], peer).wait_recv()
+            near(place, 1 - low_z, half).start()
+
+    pass_first(LATE)
+    got_far(FAR[:4])
+    pass_second(EARLY)
+    got_far(FAR[4:8])
+    pass_second(LATE)
+    got_far(FAR[8:12])
+    got_deep((0,) + FAR[:4])
+    got_far(FAR[12:])
+    pass_on(EARLY)
+    got_deep(FAR[4:12])
+    pass_on(LATE)
+    got_deep(FAR[12:])
+    pass_last(EARLY)
+
+    events = ((0, 1), (0, 2), (0, 3), (1, 1), (1, 2), (1, 3), (2, 1), (2, 3), (2, 2), (3, 2))
+
+    def complete(portions):
+        for portion in portions:
+            for stage, d in events:
+                come, at = incoming(portion, stage, d, 1 - grp)
+                remote(come, come, pass_send.at[at], pass_recv.at[at], peer).wait_recv()
+
 
     def arrivals(p, carry):
         for plane in range(2):
@@ -566,19 +590,32 @@
         return carry
 
     lax.fori_loop(0, 16, arrivals, 0)
-    events = ((0, 1), (0, 2), (0, 3), (1, 1), (1, 2), (1, 3), (2, 1), (2, 3), (2, 2), (3, 2))
-    for portion in range(3):
-        for stage, d in events:
-            come, at = incoming(portion, stage, d, 1 - grp)
-            remote(come, come, pass_send.at[at], pass_recv.at[at], peer).wait_recv()
+    complete(EARLY)
     for copy in tables:
         copy.wait()
 
-    def chunk(i, carry):
-        first_stage(i, det, bounds, tmpl, signal, bands, net, series, xe, xo, xn, power)
+    def build(step, held):
+        products(step, det, bounds, tmpl, signal, held, power)
+
+    def pair(p, carry):
+        first_stage(2 * p, held_a, bands, net, series)
+        build(2 * p + 1, held_b)
+
+        @pl.when(p == 1)
+        def _():
+            pass_last(LATE)
+            complete(LATE)
+
+        first_stage(2 * p + 1, held_b, bands, net, series)
+        build(2 * p + 2, held_a)
+
         return carry
 
-    lax.fori_loop(0, STEPS, chunk, 0)
+    build(0, held_a)
+    lax.fori_loop(0, 3, pair, 0)
+    first_stage(6, held_a, bands, net, series)
+    build(7, held_b)
+    first_stage(7, held_b, bands, net, series)
     total, shares = power_shares(power)
     response = sum(antenna[d, c] * antenna[d, c] for d in range(2) for c in range(2))
 
@@ -592,7 +629,8 @@
             device_id={"grp": to_grp, "tm": target(i)}, device_id_type=MESH,
         )
 
-    def block(eb, carry):
+    def block(step, carry):
+        eb = (2 * (here["y"] % 2) + here["x"] // 2) ^ (3 - step)
         second_stage(
             eb, total, shares, response, series, twiddle, turn, inner, last, place, ramp, zbuf, bbuf, vbuf, rows
         )
@@ -626,7 +664,7 @@
         return carry
 
     lax.fori_loop(0, 16, rest, 0)
-    for portion in range(3):
+    for portion in EARLY + LATE:
         for stage, d in events:
             if stage < 2 or d != 2:
                 wide(portion, stage, d).wait_send()
@@ -646,6 +684,26 @@
         return carry
 
     lax.fori_loop(0, 8, finish, 0)
+
+
+def settle_kernel(chi, net, chi_out, net_out):
+    chi_out[...] = chi[...]
+    net_out[...] = net[...]
+
+
+def settle(chi, net):
+    one = pl.BlockSpec((4, 4, COLS), lambda i: (i, 0, 0))
+    two = pl.BlockSpec((4, 2, 4, COLS), lambda i: (i, 0, 0, 0))
+    chi, net = pl.pallas_call(
+        settle_kernel,
+        grid=(2,),
+        out_shape=(jax.ShapeDtypeStruct(chi.shape, chi.dtype), jax.ShapeDtypeStruct(net.shape, net.dtype)),
+        in_specs=[one, two],
+        out_specs=[one, two],
+        compiler_params=pltpu.CompilerParams(vmem_limit_bytes=60 * 2**20),
+        cost_estimate=pl.CostEstimate(flops=0, bytes_accessed=3 * 2**20, transcendentals=0),
+    )(chi, net)
+    return chi[None], net
 
 
 def on_device(strain, bank, assignment, slides, bounds, antenna):
@@ -667,14 +725,14 @@
             pltpu.VMEM((1, 2, 4, COLS), jnp.float32),
             pltpu.VMEM((8, COLS), jnp.float32),
             pltpu.VMEM((3, 8, 4, COLS), jnp.float32),
-            dma((3,)), dma, dma, dma((3, 4, 3)), dma((3, 4, 3)), dma((3, 4, 3)), dma((3, 4, 3)),
+            dma((3,)), dma, dma, dma((6, 4, 3)), dma((6, 4, 3)), dma((6, 4, 3)), dma((6, 4, 3)),
             dma((16,)), dma((16,)), dma((16,)), dma((16,)), dma((2, 16)), dma((2, 16)), dma((2, 8)), dma((2, 8)),
             dma((6,)),
         ] + compute_scratch(),
         compiler_params=pltpu.CompilerParams(collective_id=0, has_side_effects=True, vmem_limit_bytes=60 * 2**20),
         cost_estimate=pl.CostEstimate(flops=20 * 10**9, bytes_accessed=20 * 10**6, transcendentals=0),
     )(assignment, bounds, slides, antenna, bank, strain, *[jnp.asarray(table) for table in constant_tables()])
-    return chi[None], net
+    return settle(chi, net)
 
 
 def solution(mesh):

time: 102 us -> 91 us (0.89); the launches traced: 100 us -> 90.8 us
  Pallas kernels: 95.5 us -> 90.2 us
  local copies, waits for them, and re-layouts: 4.17 us -> 0 us
    pallas_call x1, Pallas kernels: 95.5 us -> 87.8 us  [on_device(): pl.pallas_call(kernel, out_shape=(jax.ShapeDtypeStruct((8, 4, COLS), jnp....]
    unnamed x2 -> x0, local copies, waits for them, and re-layouts: 4.17 us -> none
    pallas_call x0 -> x1, Pallas kernels: none -> 2.33 us  [settle(): pl.pallas_call(settle_kernel, grid=(2,), out_shape=(jax.ShapeDtypeStruct(...]
where the time goes in v5:
time: 91 us; the launch traced here: 90.8 us
  Pallas kernels  90.2 us (99%)
    pallas_call x1, Pallas kernels, on_device(): pl.pallas_call(kernel, out_shape=(jax.ShapeDtypeStruct((8, 4, COLS), jnp....  87.8 us
    pallas_call x1, Pallas kernels, settle(): pl.pallas_call(settle_kernel, grid=(2,), out_shape=(jax.ShapeDtypeStruct(...  2.33 us

profile of v5, /device:TPU:1, one launch (start us, length us, event | category | flops | bytes accessed | tf_op | source)
XLA Modules:
  0.0 90.8 jit_solution(14518581024478602372)
XLA Ops:
  0.6 87.8 %shard_map.131 = (f32[8,4,4096]{2,1,0:T(4,128)}, f32[8,2,4,4096]{3,2,1,0:T(4,128)}) custom-call(s32[16]{0:T(128)} %assign.1, s32[7]{0:T(128)} %bounds.1, s32[4]{0:T(128)} %slides.1, f32[2,2]{1,0:T(2,128)} %antenna.1, f32[8,2,4,4096]{3,2,1,0:T(4,128)} %bank.1, f32[1,2,4,4096]{3,2,1,0:T(4,128)} %strain.1, bf16[4,4,256,256]{3,2,1,0:T(8,128)(2,1)} %constant.12.clone.bands_hbm, ...), custom_call_target="tpu_custom_call" | custom-call | flops 20000000000 | bytes 20000000 | tf_op jit(solution)/shard_map/pallas_call | solution.py:712
  88.5 2.3 %shard_map.132 = (f32[8,4,4096]{2,1,0:T(4,128)}, f32[8,2,4,4096]{3,2,1,0:T(4,128)}) custom-call(f32[8,4,4096]{2,1,0:T(4,128)} %get-tuple-element.6.chi, f32[8,2,4,4096]{3,2,1,0:T(4,128)} %get-tuple-element.7.net), custom_call_target="tpu_custom_call" | custom-call | bytes 3145728 | tf_op jit(solution)/shard_map/pallas_call | solution.py:697

commit v6 on v5

--- a/solution.py
+++ b/solution.py
@@ -59,7 +59,7 @@
         twiddle.append(np.stack([np.cos(angle), np.sin(angle)]))
     even = halves(np.stack(even))
     odd = halves(np.stack(odd))
-    bands = np.stack([even[0], even[1], odd[0], odd[1]], axis=1)
+    bands = np.stack([np.stack([even[1], even[0]], axis=1), np.stack([odd[1], odd[0]], axis=1)], axis=1)
     twiddle = np.stack(twiddle).astype(np.float32).reshape(4, 2, 4, 8, 32, LANES).swapaxes(3, 4).copy()
     a1 = np.arange(LANES)
     q2 = np.arange(32)
@@ -144,7 +144,7 @@
     return (x[0] * c - x[1] * s, x[0] * s + x[1] * c)
 
 
-def prepare(part, det, slides, antenna, net, ramp):
+def prepare(part, det, slides, antenna, bands, net, ramp):
     column = (
         lax.broadcasted_iota(jnp.int32, (32, LANES), 0) * LANES
         + lax.broadcasted_iota(jnp.int32, (32, LANES), 1)
@@ -164,9 +164,14 @@
             angle = (((row + shift) * bin_row + quarter) & (FOLD - 1)).astype(jnp.float32) * (2.0 * math.pi / FOLD)
             for half, table in ((0, jnp.cos(angle)), (1, jnp.sin(angle))):
                 high, low = split_two(table)
-                at = slice(64 * slide + 32 * half, 64 * slide + 32 * half + 32)
-                net[side, 0, at, :] = high
-                net[side, 1, at, :] = low
+                at = 64 * slide + 32 * half
+                if side == 0:
+                    for parity in range(2):
+                        bands[parity, 256 + at : 288 + at, :] = low
+                        bands[parity, 640 + at : 672 + at, :] = high
+                else:
+                    net[at : at + 32, :] = low
+                    net[128 + at : 160 + at, :] = high
             angle = ((column * shift) & (BINS - 1)).astype(jnp.float32) * (2.0 * math.pi / BINS)
             cos, sin = jnp.cos(angle), jnp.sin(angle)
             ramp[slide, 2 * side] = weight_re * cos - weight_im * sin
@@ -174,7 +179,7 @@
 
 
 def column_block(step):
-    return 2 * (step // 4) + step % 2 + 4 * ((step // 2) % 2)
+    return jnp.where(step < 6, step % 3 + 4 * (step // 3), 4 * step - 21)
 
 
 def products(step, det, bounds, tmpl, signal, held, power):
@@ -232,19 +237,23 @@
     tiles = CHUNK // LANES
     block = column_block(step) * tiles
 
-    def three(high, low, k):
-        return mm(high, held[k]) + mm(low, held[k]) + mm(high, held[k + 1])
-
     def put(first, value):
         rows = value.shape[0] // 8
         for tile in range(tiles):
             piece = value[:, tile * LANES : (tile + 1) * LANES].reshape(rows, 8, LANES)
             series[pl.ds(first, rows), block + tile] = piece
 
-    put(0, three(bands[0], bands[1], 0))
-    put(32, three(bands[2], bands[3], 2))
-    put(64, three(net[0, 0], net[0, 1], 0) + three(net[0, 0], net[0, 1], 2))
-    put(80, three(net[1, 0], net[1, 1], 4))
+    net_sum = None
+    for parity in range(2):
+        both = mm(bands[parity], held[2 * parity])
+        fine = mm(bands[parity, 384:768, :], held[2 * parity + 1])
+        value = both[0:384] + both[384:768] + fine
+        put(32 * parity, value[0:256])
+        net_sum = value[256:384] if net_sum is None else net_sum + value[256:384]
+    put(64, net_sum)
+    both = mm(net[...], held[4])
+    fine = mm(net[128:256, :], held[5])
+    put(80, both[0:128] + both[128:256] + fine)
 
 
 def power_shares(power):
@@ -323,7 +332,7 @@
 
 def compute_scratch():
     return [
-        pltpu.VMEM((2, 2, 128, 256), jnp.bfloat16),
+        pltpu.VMEM((256, 256), jnp.bfloat16),
         pltpu.VMEM((2, 4, 32, LANES), jnp.float32),
         pltpu.VMEM((96, 32, 8, LANES), jnp.float32),
         pltpu.VMEM((6, 256, CHUNK), jnp.bfloat16),
@@ -332,7 +341,7 @@
         pltpu.VMEM((2, 256, 256), jnp.float32),
         pltpu.VMEM((10, 256, 256), jnp.float32),
         pltpu.VMEM((192, 512), jnp.float32),
-        pltpu.VMEM((4, 256, 256), jnp.bfloat16),
+        pltpu.VMEM((2, 768, 256), jnp.bfloat16),
         pltpu.VMEM((2, 4, 32, 8, LANES), jnp.float32),
         pltpu.VMEM((2, 8, 4, 8, LANES), jnp.float32),
         pltpu.VMEM((2, 32, LANES), jnp.float32),
@@ -343,7 +352,7 @@
 
 MESH = pl.DeviceIdType.MESH
 HALF = COLS // 2
-PORTIONS = ((0, 384), (384, 384), (768, 256), (1024, 384), (1408, 256), (1664, 384))
+PORTIONS = ((0, 512), (512, 512), (1024, 512), (1536, 128), (1664, 128), (1792, 256))
 ORDERS = (("x", "y", "z"), ("y", "z", "x"), ("z", "x", "y")) * 2
 EARLY, LATE = (0, 1, 2), (3, 4, 5)
 FAR = (1, 4, 3, 12, 5, 15, 7, 13, 2, 8, 6, 9, 11, 14, 10)
@@ -354,28 +363,50 @@
     chi, net_out, tmpl, signal, everything, staged, loaded, packed, rows,
     local_sem, swap_send, swap_recv, wide_send, wide_recv, pass_send, pass_recv,
     far_send, far_recv, deep_send, deep_recv, near_send, near_recv, out_send, out_recv, table_sem,
-    net, ramp, series, held_a, held_b, power, zbuf, bbuf, vbuf, bands, twiddle, turn, inner, last, place,
+    net, ramp, series, held_a, held_b, power, zbuf, bbuf, vbuf, bands, twiddle, turn, inner, last, weave,
 ):
     det, grp, tm = lax.axis_index("det"), lax.axis_index("grp"), lax.axis_index("tm")
-    low_z = (tm // 4) % 2
-    here = {"y": tm // 8, "z": det * 2 + low_z, "x": tm % 4}
+    low_z = lax.rem(lax.div(tm, 4), 2)
+    here = {"y": lax.div(tm, 8), "z": det * 2 + low_z, "x": lax.rem(tm, 4)}
+    onward = {axis: [value] + [lax.rem(value + k, 4) for k in (1, 2, 3)] for axis, value in here.items()}
+    split_z = [(det, low_z)] + [(lax.div(z, 2), lax.rem(z, 2)) for z in onward["z"][1:]]
     peer = {"grp": 1 - grp}
     half = pl.ds(pl.multiple_of(grp * HALF, HALF), HALF)
     other = pl.ds(pl.multiple_of((1 - grp) * HALF, HALF), HALF)
 
+    AXES = ("y", "z", "x")
+
     def moved(axis, by):
-        there = dict(here)
-        there[axis] = (here[axis] + by + 4) % 4
-        return there
+        return tuple(by % 4 if name == axis else 0 for name in AXES)
+
+    def shifted(d, sign=1):
+        return ((sign * (d // 4)) % 4, 0, (sign * (d % 4)) % 4)
+
+    def at_y(place):
+        return onward["y"][place[0]]
+
+    def at_x(place):
+        return onward["x"][place[2]]
+
+    tm_at = {}
 
     def ident(place):
-        return {"det": place["z"] // 2, "tm": place["y"] * 8 + (place["z"] % 2) * 4 + place["x"]}
-
-    def shifted(d, sign=1):
-        there = dict(here)
-        there["y"] = (here["y"] + sign * (d // 4) + 4) % 4
-        there["x"] = (here["x"] + sign * (d % 4) + 4) % 4
-        return there
+        if place not in tm_at:
+            tm_at[place] = at_y(place) * 8 + split_z[place[1]][1] * 4 + at_x(place)
+        return {"det": split_z[place[1]][0], "tm": tm_at[place]}
+
+    slots = {}
+
+    def number(place):
+        if place not in slots:
+            slots[place] = at_y(place) * 4 + at_x(place)
+        return slots[place]
+
+    HERE = (0, 0, 0)
+    PLANE = [shifted(d) for d in range(16)]
+    for place in PLANE + [moved("z", d) for d in (1, 2, 3)]:
+        ident(place)
+        number(place)
 
     keep = pltpu.make_async_copy(bank.at[:, :, :, half], everything.at[pl.ds(grp * 8, 8)], local_sem.at[0])
     keep.start()
@@ -386,27 +417,26 @@
     tables = [
         pltpu.make_async_copy(src, dst, table_sem.at[i])
         for i, (src, dst) in enumerate((
-            (bands_hbm.at[part], bands), (twiddle_hbm.at[part], twiddle), (turn_hbm, turn),
-            (inner_hbm, inner), (last_hbm, last), (place_hbm, place),
+            (bands_hbm.at[part, 0, 0], bands.at[0, pl.ds(0, 256)]), (bands_hbm.at[part, 0, 1], bands.at[0, pl.ds(384, 256)]),
+            (bands_hbm.at[part, 1, 0], bands.at[1, pl.ds(0, 256)]), (bands_hbm.at[part, 1, 1], bands.at[1, pl.ds(384, 256)]),
+            (twiddle_hbm.at[part], twiddle), (turn_hbm, turn),
+            (inner_hbm, inner), (last_hbm, last), (place_hbm, weave),
         ))
     ]
     for copy in tables:
         copy.start()
 
-    to_grp = here["y"] // 2
+    to_grp = lax.div(here["y"], 2)
     same_core = to_grp == grp
-    slot_at = 4 * (here["y"] % 2) + here["x"]
+    slot_at = 4 * lax.rem(here["y"], 2) + here["x"]
 
     def target(i):
         return (2 * grp + i // 4) * 8 + low_z * 4 + i % 4
 
     barrier = pltpu.get_barrier_semaphore()
 
-    def greet(d, carry):
-        pl.semaphore_signal(barrier, inc=1, device_id=ident(shifted(d)), device_id_type=MESH)
-        return carry
-
-    lax.fori_loop(1, 16, greet, 0)
+    for place in PLANE[1:]:
+        pl.semaphore_signal(barrier, inc=1, device_id=ident(place), device_id_type=MESH)
     for d in (1, 2, 3):
         pl.semaphore_signal(barrier, inc=1, device_id=ident(moved("z", d)), device_id_type=MESH)
     pl.semaphore_signal(barrier, inc=1, device_id=peer, device_id_type=MESH)
@@ -437,12 +467,12 @@
             return pl.ds(0, size)
 
         return signal.at[
-            every("z", place["z"] // 2, 2), every("y", place["y"], 4), every("z", place["z"] % 2, 2),
-            every("x", place["x"], 4), :, columns(portion, core),
+            every("z", split_z[place[1]][0], 2), every("y", at_y(place), 4), every("z", split_z[place[1]][1], 2),
+            every("x", at_x(place), 4), :, columns(portion, core),
         ]
 
     def wide(portion, stage, d):
-        dst = region(portion, stage, here, grp)
+        dst = region(portion, stage, HERE, grp)
         src = packed.at[:, columns(portion, grp)] if stage == 0 else dst
         at = (portion, stage, d - 1)
         return remote(src, dst, wide_send.at[at], wide_recv.at[at], ident(moved(ORDERS[portion][stage], d)))
@@ -510,40 +540,38 @@
     def far(d):
         to = shifted(d)
         return remote(
-            staged.at[to["y"] * 4 + to["x"]], tmpl.at[here["y"], low_z, here["x"], :, half],
+            staged.at[number(to)], tmpl.at[here["y"], low_z, here["x"], :, half],
             far_send.at[d], far_recv.at[d], ident(to),
         )
 
     def piece(place, plane, columns):
-        return tmpl.at[place["y"], plane, place["x"], :, columns]
+        return tmpl.at[at_y(place), plane, at_x(place), :, columns]
 
     def deep(place):
         got = piece(place, low_z, half)
-        at = place["y"] * 4 + place["x"]
-        to = moved("z", 1 + 2 * (place["x"] % 2))
+        to = moved("z", 1 + 2 * (place[2] % 2))
+        at = DEEP(place)
         return remote(got, got, deep_send.at[at], deep_recv.at[at], ident(to))
 
+    def DEEP(place):
+        return place[0] * 4 + place[2]
+
     def near(place, plane, columns):
-        got = piece(place, plane, columns)
-        at = (plane, place["y"] * 4 + place["x"])
+        got = piece(place, low_z if plane == 0 else 1 - low_z, columns)
+        at = (plane, DEEP(place))
         return remote(got, got, near_send.at[at], near_recv.at[at], peer)
 
     mine.wait()
     pass_first(EARLY)
     for d in FAR:
         far(d).start()
-    slot_here = here["y"] * 4 + here["x"]
-    kept = pltpu.make_async_copy(staged.at[slot_here], piece(here, low_z, half), local_sem.at[2])
+    kept = pltpu.make_async_copy(staged.at[number(HERE)], piece(HERE, low_z, half), local_sem.at[2])
     kept.start()
-
-    prepare(part, det, slides, antenna, net, ramp)
+    prepare(part, det, slides, antenna, bands, net, ramp)
     power[...] = jnp.zeros_like(power)
     kept.wait()
-    deep(here).start()
-    near(here, low_z, half).start()
-
-    def place_at(p):
-        return {"y": p // 4, "x": p % 4}
+    deep(HERE).start()
+    near(HERE, 0, half).start()
 
     def got_far(order):
         for d in order:
@@ -551,28 +579,23 @@
             got = piece(place, low_z, half)
             remote(got, got, far_send.at[d], far_recv.at[d], peer).wait_recv()
             deep(place).start()
-            near(place, low_z, half).start()
+            near(place, 0, half).start()
 
     def got_deep(order):
         for d in order:
             place = shifted(d, -1)
             got = piece(place, 1 - low_z, half)
-            at = place["y"] * 4 + place["x"]
+            at = DEEP(place)
             remote(got, got, deep_send.at[at], deep_recv.at[at], peer).wait_recv()
-            near(place, 1 - low_z, half).start()
-
+            near(place, 1, half).start()
+
+    pass_second(EARLY)
     pass_first(LATE)
-    got_far(FAR[:4])
-    pass_second(EARLY)
-    got_far(FAR[4:8])
+    got_far(FAR)
+    got_deep((0,) + FAR[:8])
+    pass_on(EARLY)
     pass_second(LATE)
-    got_far(FAR[8:12])
-    got_deep((0,) + FAR[:4])
-    got_far(FAR[12:])
-    pass_on(EARLY)
-    got_deep(FAR[4:12])
-    pass_on(LATE)
-    got_deep(FAR[12:])
+    got_deep(FAR[8:])
     pass_last(EARLY)
 
     events = ((0, 1), (0, 2), (0, 3), (1, 1), (1, 2), (1, 3), (2, 1), (2, 3), (2, 2), (3, 2))
@@ -584,12 +607,9 @@
                 remote(come, come, pass_send.at[at], pass_recv.at[at], peer).wait_recv()
 
 
-    def arrivals(p, carry):
+    for place in PLANE:
         for plane in range(2):
-            near(place_at(p), plane, other).wait_recv()
-        return carry
-
-    lax.fori_loop(0, 16, arrivals, 0)
+            near(place, plane, other).wait_recv()
     complete(EARLY)
     for copy in tables:
         copy.wait()
@@ -601,17 +621,17 @@
         first_stage(2 * p, held_a, bands, net, series)
         build(2 * p + 1, held_b)
 
-        @pl.when(p == 1)
+        @pl.when(p == 2)
         def _():
             pass_last(LATE)
             complete(LATE)
 
         first_stage(2 * p + 1, held_b, bands, net, series)
         build(2 * p + 2, held_a)
-
         return carry
 
     build(0, held_a)
+    pass_on(LATE)
     lax.fori_loop(0, 3, pair, 0)
     first_stage(6, held_a, bands, net, series)
     build(7, held_b)
@@ -630,9 +650,9 @@
         )
 
     def block(step, carry):
-        eb = (2 * (here["y"] % 2) + here["x"] // 2) ^ (3 - step)
+        eb = (2 * lax.rem(here["y"], 2) + lax.div(here["x"], 2)) ^ (3 - step)
         second_stage(
-            eb, total, shares, response, series, twiddle, turn, inner, last, place, ramp, zbuf, bbuf, vbuf, rows
+            eb, total, shares, response, series, twiddle, turn, inner, last, weave, ramp, zbuf, bbuf, vbuf, rows
         )
         for k in range(2):
             i = 2 * eb + k
@@ -652,18 +672,12 @@
 
     swap.wait_send()
 
-    def rest(p, carry):
-        deep(place_at(p)).wait_send()
+    for d, place in enumerate(PLANE):
+        deep(place).wait_send()
         for plane in range(2):
-            near(place_at(p), plane, half).wait_send()
-
-        @pl.when(p > 0)
-        def _():
-            far(p).wait_send()
-
-        return carry
-
-    lax.fori_loop(0, 16, rest, 0)
+            near(place, plane, half).wait_send()
+        if d > 0:
+            far(d).wait_send()
     for portion in EARLY + LATE:
         for stage, d in events:
             if stage < 2 or d != 2:
@@ -727,7 +741,7 @@
             pltpu.VMEM((3, 8, 4, COLS), jnp.float32),
             dma((3,)), dma, dma, dma((6, 4, 3)), dma((6, 4, 3)), dma((6, 4, 3)), dma((6, 4, 3)),
             dma((16,)), dma((16,)), dma((16,)), dma((16,)), dma((2, 16)), dma((2, 16)), dma((2, 8)), dma((2, 8)),
-            dma((6,)),
+            dma((9,)),
         ] + compute_scratch(),
         compiler_params=pltpu.CompilerParams(collective_id=0, has_side_effects=True, vmem_limit_bytes=60 * 2**20),
         cost_estimate=pl.CostEstimate(flops=20 * 10**9, bytes_accessed=20 * 10**6, transcendentals=0),

time: 91 us -> 85.4 us (0.938)
  Pallas kernels: 90.2 us -> 84.6 us
    pallas_call x1, Pallas kernels: 87.8 us -> 82.3 us  [on_device(): pl.pallas_call(kernel, out_shape=(jax.ShapeDtypeStruct((8, 4, COLS), jnp....]
where the time goes in v6:
time: 85.4 us; the launch traced here: 85.3 us
  Pallas kernels  84.6 us (99%)
    pallas_call x1, Pallas kernels, on_device(): pl.pallas_call(kernel, out_shape=(jax.ShapeDtypeStruct((8, 4, COLS), jnp....  82.3 us
    pallas_call x1, Pallas kernels, settle(): pl.pallas_call(settle_kernel, grid=(2,), out_shape=(jax.ShapeDtypeStruct(...  2.33 us

profile of v6, /device:TPU:1, one launch (start us, length us, event | category | flops | bytes accessed | tf_op | source)
XLA Modules:
  0.0 85.3 jit_solution(10883204323523641636)
XLA Ops:
  0.6 82.3 %shard_map.131 = (f32[8,4,4096]{2,1,0:T(4,128)}, f32[8,2,4,4096]{3,2,1,0:T(4,128)}) custom-call(s32[16]{0:T(128)} %assign.1, s32[7]{0:T(128)} %bounds.1, s32[4]{0:T(128)} %slides.1, f32[2,2]{1,0:T(2,128)} %antenna.1, f32[8,2,4,4096]{3,2,1,0:T(4,128)} %bank.1, f32[1,2,4,4096]{3,2,1,0:T(4,128)} %strain.1, ...), custom_call_target="tpu_custom_call" | custom-call | flops 20000000000 | bytes 20000000 | tf_op jit(solution)/shard_map/pallas_call | solution.py:726
  83.0 2.3 %shard_map.132 = (f32[8,4,4096]{2,1,0:T(4,128)}, f32[8,2,4,4096]{3,2,1,0:T(4,128)}) custom-call(f32[8,4,4096]{2,1,0:T(4,128)} %get-tuple-element.6.chi, f32[8,2,4,4096]{3,2,1,0:T(4,128)} %get-tuple-element.7.net), custom_call_target="tpu_custom_call" | custom-call | bytes 3145728 | tf_op jit(solution)/shard_map/pallas_call | solution.py:711

commit v7 on v6

--- a/solution.py
+++ b/solution.py
@@ -271,20 +271,31 @@
     return total, [value / total for value in powers]
 
 
-def second_stage(eb, total, shares, response, series, twiddle, turn, inner, last, place, ramp, zbuf, bbuf, vbuf, rows):
+def second_stage(eb, total, shares, response, series, twiddle, turn, inner, last, place, ramp, zbuf, bbuf, vbuf, rows, first):
     inverse = [(1.0 / (2 * BANDS - 2)) / (total * share) for share in shares]
     net_scale = 1.0 / (total * response)
     cos, sin = twiddle[0, eb], twiddle[1, eb]
     inner_re, inner_im = inner[0][:, None, :], inner[1][:, None, :]
 
+    def settle_rows(kinds):
+        high, low = split_two(vbuf[64 * kinds[0] : 64 * kinds[-1] + 64, :])
+        done = mm(high, place[...]) + mm(low, place[...])
+        for at, kind in enumerate(kinds):
+            for v in range(8):
+                both = done[at * 64 + v * 8 : at * 64 + v * 8 + 8, :]
+                rows[kind, 2 * eb, :, v * 512 : (v + 1) * 512] = both[0:4]
+                rows[kind, 2 * eb + 1, :, v * 512 : (v + 1) * 512] = both[4:8]
+
     def transform(item, z):
         z = times(z, cos, sin)
         re, im = z[0].reshape(8, 4, 8, LANES), z[1].reshape(8, 4, 8, LANES)
         values = eight([(re[s], im[s]) for s in range(8)])
-        values = [values[0]] + [times(values[v], turn[0, v], turn[1, v]) for v in range(1, 8)]
-        re = jnp.stack([value[0] for value in values])
-        im = jnp.stack([value[1] for value in values])
-        done = four_point([(re[:, r2], im[:, r2]) for r2 in range(4)])
+        turned = [(values[0][0][1:], values[0][1][1:])]
+        turned += [times((values[v][0][1:], values[v][1][1:]), turn[0, v, 1:], turn[1, v, 1:]) for v in range(1, 8)]
+        first = tuple(jnp.stack([value[c][0] for value in values]) for c in range(2))
+        re = jnp.stack([value[0] for value in turned])
+        im = jnp.stack([value[1] for value in turned])
+        done = four_point([first] + [(re[:, r2], im[:, r2]) for r2 in range(3)])
         re = jnp.concatenate([value[0] for value in done], axis=0)
         im = jnp.concatenate([value[1] for value in done], axis=0)
         z = times((re, im), inner_re, inner_im)
@@ -297,13 +308,6 @@
     for item in range(BANDS):
         base = (item // 2) * 8 + (item % 2) * 32 + eb
         transform(item, (series[base], series[base + 4]))
-    for slide in range(2):
-        own = (series[64 + 8 * slide + eb], series[64 + 8 * slide + 4 + eb])
-        oth = (series[80 + 8 * slide + eb], series[80 + 8 * slide + 4 + eb])
-        line = [ramp[slide, k][:, None, :] for k in range(4)]
-        own, oth = times(own, line[0], line[1]), times(oth, line[2], line[3])
-        transform(BANDS + slide, (own[0] + oth[0], own[1] + oth[1]))
-
     for u2 in range(4):
         part = slice(64 * u2, 64 * u2 + 64)
         re = [bbuf[band, part, 0:LANES] for band in range(BANDS)]
@@ -317,17 +321,23 @@
             chi = term if chi is None else chi + term
         columns = slice(u2 * LANES, (u2 + 1) * LANES)
         vbuf[0:64, columns] = chi
+    settle_rows(range(1))
+    first()
+    for slide in range(2):
+        own = (series[64 + 8 * slide + eb], series[64 + 8 * slide + 4 + eb])
+        oth = (series[80 + 8 * slide + eb], series[80 + 8 * slide + 4 + eb])
+        line = [ramp[slide, k][:, None, :] for k in range(4)]
+        own, oth = times(own, line[0], line[1]), times(oth, line[2], line[3])
+        transform(BANDS + slide, (own[0] + oth[0], own[1] + oth[1]))
+
+    for u2 in range(4):
+        part = slice(64 * u2, 64 * u2 + 64)
+        columns = slice(u2 * LANES, (u2 + 1) * LANES)
         for slide in range(2):
             re = bbuf[BANDS + slide, part, 0:LANES]
             im = bbuf[BANDS + slide, part, LANES : 2 * LANES]
             vbuf[64 + 64 * slide : 128 + 64 * slide, columns] = (re * re + im * im) * net_scale
-    high, low = split_two(vbuf[...])
-    done = mm(high, place[...]) + mm(low, place[...])
-    for kind in range(3):
-        for v in range(8):
-            both = done[kind * 64 + v * 8 : kind * 64 + v * 8 + 8, :]
-            rows[kind, 2 * eb, :, v * 512 : (v + 1) * 512] = both[0:4]
-            rows[kind, 2 * eb + 1, :, v * 512 : (v + 1) * 512] = both[4:8]
+    settle_rows(range(1, 3))
 
 
 def compute_scratch():
@@ -355,7 +365,7 @@
 PORTIONS = ((0, 512), (512, 512), (1024, 512), (1536, 128), (1664, 128), (1792, 256))
 ORDERS = (("x", "y", "z"), ("y", "z", "x"), ("z", "x", "y")) * 2
 EARLY, LATE = (0, 1, 2), (3, 4, 5)
-FAR = (1, 4, 3, 12, 5, 15, 7, 13, 2, 8, 6, 9, 11, 14, 10)
+FAR = (1, 4, 3, 12, 2, 8, 5, 15, 7, 13, 6, 9, 11, 14, 10)
 
 
 def kernel(
@@ -589,30 +599,34 @@
             remote(got, got, deep_send.at[at], deep_recv.at[at], peer).wait_recv()
             near(place, 1, half).start()
 
+    events = ((0, 1), (0, 2), (0, 3), (1, 1), (1, 2), (1, 3), (2, 1), (2, 3), (2, 2), (3, 2))
+
+    def complete(portions, events):
+        for portion in portions:
+            for stage, d in events:
+                come, at = incoming(portion, stage, d, 1 - grp)
+                remote(come, come, pass_send.at[at], pass_recv.at[at], peer).wait_recv()
+
+
+    def complete_near(plane):
+        for place in PLANE:
+            near(place, plane, other).wait_recv()
+
     pass_second(EARLY)
     pass_first(LATE)
     got_far(FAR)
+    for copy in tables:
+        copy.wait()
+    complete(EARLY, events[:6])
+    complete_near(0)
     got_deep((0,) + FAR[:8])
     pass_on(EARLY)
     pass_second(LATE)
     got_deep(FAR[8:])
     pass_last(EARLY)
 
-    events = ((0, 1), (0, 2), (0, 3), (1, 1), (1, 2), (1, 3), (2, 1), (2, 3), (2, 2), (3, 2))
-
-    def complete(portions):
-        for portion in portions:
-            for stage, d in events:
-                come, at = incoming(portion, stage, d, 1 - grp)
-                remote(come, come, pass_send.at[at], pass_recv.at[at], peer).wait_recv()
-
-
-    for place in PLANE:
-        for plane in range(2):
-            near(place, plane, other).wait_recv()
-    complete(EARLY)
-    for copy in tables:
-        copy.wait()
+    complete_near(1)
+    complete(EARLY, events[6:])
 
     def build(step, held):
         products(step, det, bounds, tmpl, signal, held, power)
@@ -624,7 +638,7 @@
         @pl.when(p == 2)
         def _():
             pass_last(LATE)
-            complete(LATE)
+            complete(LATE, events[6:])
 
         first_stage(2 * p + 1, held_b, bands, net, series)
         build(2 * p + 2, held_a)
@@ -632,6 +646,7 @@
 
     build(0, held_a)
     pass_on(LATE)
+    complete(LATE, events[:6])
     lax.fori_loop(0, 3, pair, 0)
     first_stage(6, held_a, bands, net, series)
     build(7, held_b)
@@ -651,13 +666,11 @@
 
     def block(step, carry):
         eb = (2 * lax.rem(here["y"], 2) + lax.div(here["x"], 2)) ^ (3 - step)
-        second_stage(
-            eb, total, shares, response, series, twiddle, turn, inner, last, weave, ramp, zbuf, bbuf, vbuf, rows
-        )
-        for k in range(2):
-            i = 2 * eb + k
-            is_self = (target(i) == tm) & same_core
-            for kind in range(2):
+        def send(kind):
+            for k in range(2):
+                i = 2 * eb + k
+                is_self = (target(i) == tm) & same_core
+
                 @pl.when(is_self)
                 def _():
                     src, dst = parts(i)[kind]
@@ -666,6 +679,12 @@
                 @pl.when(jnp.logical_not(is_self))
                 def _():
                     give(i, kind).start()
+
+        second_stage(
+            eb, total, shares, response, series, twiddle, turn, inner, last, weave, ramp, zbuf, bbuf, vbuf, rows,
+            lambda: send(0),
+        )
+        send(1)
         return carry
 
     lax.fori_loop(0, 4, block, 0)
@@ -700,20 +719,34 @@
     lax.fori_loop(0, 8, finish, 0)
 
 
-def settle_kernel(chi, net, chi_out, net_out):
-    chi_out[...] = chi[...]
-    net_out[...] = net[...]
+def settle_kernel(chi, net, chi_out, net_out, chi_held, net_held, sem):
+    moves = []
+    for k in range(4):
+        part = pl.ds(2 * k, 2)
+        for i, (src, held, dst) in enumerate(((net, net_held, net_out), (chi, chi_held, chi_out))):
+            moves.append((
+                pltpu.make_async_copy(src.at[part], held.at[part], sem.at[0, i, k]),
+                pltpu.make_async_copy(held.at[part], dst.at[part], sem.at[1, i, k]),
+            ))
+    for come, _ in moves:
+        come.start()
+    for come, go in moves:
+        come.wait()
+        go.start()
+    for _, go in moves:
+        go.wait()
 
 
 def settle(chi, net):
-    one = pl.BlockSpec((4, 4, COLS), lambda i: (i, 0, 0))
-    two = pl.BlockSpec((4, 2, 4, COLS), lambda i: (i, 0, 0, 0))
+    hbm = pl.BlockSpec(memory_space=pltpu.HBM)
     chi, net = pl.pallas_call(
         settle_kernel,
-        grid=(2,),
         out_shape=(jax.ShapeDtypeStruct(chi.shape, chi.dtype), jax.ShapeDtypeStruct(net.shape, net.dtype)),
-        in_specs=[one, two],
-        out_specs=[one, two],
+        in_specs=[hbm, hbm],
+        out_specs=[hbm, hbm],
+        scratch_shapes=[
+            pltpu.VMEM(chi.shape, chi.dtype), pltpu.VMEM(net.shape, net.dtype), pltpu.SemaphoreType.DMA((2, 2, 4)),
+        ],
         compiler_params=pltpu.CompilerParams(vmem_limit_bytes=60 * 2**20),
         cost_estimate=pl.CostEstimate(flops=0, bytes_accessed=3 * 2**20, transcendentals=0),
     )(chi, net)

time: 85.4 us -> 84.8 us (level)
  no operation moved by 1% of the time
where the time goes in v7:
time: 84.8 us; the launch traced here: 84.7 us
  Pallas kernels  84 us (99%)
    pallas_call x1, Pallas kernels, on_device(): pl.pallas_call(kernel, out_shape=(jax.ShapeDtypeStruct((8, 4, COLS), jnp....  81.8 us
    pallas_call x1, Pallas kernels, settle(): pl.pallas_call(settle_kernel, out_shape=(jax.ShapeDtypeStruct(chi.shape,...  2.23 us

profile of v7, /device:TPU:1, one launch (start us, length us, event | category | flops | bytes accessed | tf_op | source)
XLA Modules:
  0.0 84.7 jit_solution(13393635155573782429)
XLA Ops:
  0.6 81.8 %shard_map.131 = (f32[8,4,4096]{2,1,0:T(4,128)}, f32[8,2,4,4096]{3,2,1,0:T(4,128)}) custom-call(s32[16]{0:T(128)} %assign.1, s32[7]{0:T(128)} %bounds.1, s32[4]{0:T(128)} %slides.1, f32[2,2]{1,0:T(2,128)} %antenna.1, f32[8,2,4,4096]{3,2,1,0:T(4,128)} %bank.1, f32[1,2,4,4096]{3,2,1,0:T(4,128)} %strain.1, ...), custom_call_target="tpu_custom_call" | custom-call | flops 20000000000 | bytes 20000000 | tf_op jit(solution)/shard_map/pallas_call | solution.py:759
  82.4 2.2 %shard_map.132 = (f32[8,4,4096]{2,1,0:T(4,128)}, f32[8,2,4,4096]{3,2,1,0:T(4,128)}) custom-call(f32[8,4,4096]{2,1,0:T(4,128)} %get-tuple-element.6.chi, f32[8,2,4,4096]{3,2,1,0:T(4,128)} %get-tuple-element.7.net), custom_call_target="tpu_custom_call" | custom-call | bytes 3145728 | tf_op jit(solution)/shard_map/pallas_call | solution.py:742

commit v8 on v7

--- a/solution.py
+++ b/solution.py
@@ -445,9 +445,10 @@
 
     barrier = pltpu.get_barrier_semaphore()
 
-    for place in PLANE[1:]:
+    hops = lambda place: min(place[0], 4 - place[0]) + min(place[2], 4 - place[2])
+    for place in sorted(PLANE[1:], key=hops, reverse=True):
         pl.semaphore_signal(barrier, inc=1, device_id=ident(place), device_id_type=MESH)
-    for d in (1, 2, 3):
+    for d in (2, 1, 3):
         pl.semaphore_signal(barrier, inc=1, device_id=ident(moved("z", d)), device_id_type=MESH)
     pl.semaphore_signal(barrier, inc=1, device_id=peer, device_id_type=MESH)
 

time: 84.8 us -> 84.8 us (level)
  no operation moved by 1% of the time
where the time goes in v8:
time: 84.8 us; the launch traced here: 84.6 us
  Pallas kernels  84 us (99%)
    pallas_call x1, Pallas kernels, on_device(): pl.pallas_call(kernel, out_shape=(jax.ShapeDtypeStruct((8, 4, COLS), jnp....  81.7 us
    pallas_call x1, Pallas kernels, settle(): pl.pallas_call(settle_kernel, out_shape=(jax.ShapeDtypeStruct(chi.shape,...  2.23 us

profile of v8, /device:TPU:1, one launch (start us, length us, event | category | flops | bytes accessed | tf_op | source)
XLA Modules:
  0.0 84.6 jit_solution(3085361211725200809)
XLA Ops:
  0.6 81.7 %shard_map.131 = (f32[8,4,4096]{2,1,0:T(4,128)}, f32[8,2,4,4096]{3,2,1,0:T(4,128)}) custom-call(s32[16]{0:T(128)} %assign.1, s32[7]{0:T(128)} %bounds.1, s32[4]{0:T(128)} %slides.1, f32[2,2]{1,0:T(2,128)} %antenna.1, f32[8,2,4,4096]{3,2,1,0:T(4,128)} %bank.1, f32[1,2,4,4096]{3,2,1,0:T(4,128)} %strain.1, ...), custom_call_target="tpu_custom_call" | custom-call | flops 20000000000 | bytes 20000000 | tf_op jit(solution)/shard_map/pallas_call | solution.py:760
  82.4 2.2 %shard_map.132 = (f32[8,4,4096]{2,1,0:T(4,128)}, f32[8,2,4,4096]{3,2,1,0:T(4,128)}) custom-call(f32[8,4,4096]{2,1,0:T(4,128)} %get-tuple-element.6.chi, f32[8,2,4,4096]{3,2,1,0:T(4,128)} %get-tuple-element.7.net), custom_call_target="tpu_custom_call" | custom-call | bytes 3145728 | tf_op jit(solution)/shard_map/pallas_call | solution.py:743
